TPU v7x, 32 devices: a whole 2x2x4 slice. The times are simulated.
32 devices in a mesh: fsdp: 4 (over x, core), seq: 8 (over z, y).
Axes of the slice: x: 2, y: 2, z: 4, core: 2. Of those that a mesh axis runs over, the one named last changes fastest.
Arguments:
- hidden: bfloat16 [4, 1024, 2880], P('fsdp', 'seq'), may hold values from -6 to 6
- out_grad: bfloat16 [4, 1024, 2880], P('fsdp', 'seq'), may hold values from -6 to 6
- routes: int32 [4, 1024, 4], P('fsdp', 'seq'), may hold values from 0 to 7, all different within a row; in each aligned block of 128 rows (0 to 127, 128 to 255, ..., all dimensions but the last counted through in order) at most 72 rows name the same one
- norm1_gain: float32 [2880], replicated, may hold values from 0.5 to 1.5
- qkv_weight: bfloat16 [2880, 5120], P(None, ('fsdp', 'seq')), may hold values from -0.109375 to 0.109375
- qkv_bias: float32 [5120], replicated, may hold values from -0.625 to 0.625
- sink_logits: float32 [64], replicated, may hold values from -6 to 6
- out_weight: bfloat16 [4096, 2880], P(('fsdp', 'seq')), may hold values from -0.1875 to 0.1875
- out_bias: float32 [2880], replicated, may hold values from -0.625 to 0.625
- norm2_gain: float32 [2880], replicated, may hold values from 0.5 to 1.5
- router_weight: bfloat16 [2880, 8], replicated, may hold values from -0.0546875 to 0.0546875
- router_bias: float32 [8], replicated, may hold values from -0.625 to 0.625
- gate_up_weight: bfloat16 [8, 2880, 5760], P('seq', 'fsdp'), may hold values from -0.109375 to 0.109375
- gate_up_bias: bfloat16 [8, 5760], P('seq', 'fsdp'), may hold values from -0.625 to 0.625
- down_weight: bfloat16 [8, 2880, 2880], P('seq', 'fsdp'), may hold values from -0.109375 to 0.109375
- down_bias: bfloat16 [8, 2880], P('seq', 'fsdp'), may hold values from -0.625 to 0.625
Outputs:
- out_hidden: bfloat16 [4, 1024, 2880], P('fsdp', 'seq')
- grad_hidden: bfloat16 [4, 1024, 2880], P('fsdp', 'seq')
- grad_norm1_gain: float32 [2880], replicated
- grad_qkv_weight: float32 [2880, 5120], P(None, ('fsdp', 'seq'))
- grad_qkv_bias: float32 [5120], replicated
- grad_sink_logits: float32 [64], replicated
- grad_out_weight: float32 [4096, 2880], P(('fsdp', 'seq'))
- grad_out_bias: float32 [2880], replicated
- grad_norm2_gain: float32 [2880], replicated
- grad_router_weight: float32 [2880, 8], replicated
- grad_router_bias: float32 [8], replicated
- grad_gate_up_weight: float32 [8, 2880, 5760], P('seq', 'fsdp')
- grad_gate_up_bias: float32 [8, 5760], P('seq', 'fsdp')
- grad_down_weight: float32 [8, 2880, 2880], P('seq', 'fsdp')
- grad_down_bias: float32 [8, 2880], P('seq', 'fsdp')
Inputs may be any that keep to these rules, and one draw needn't show every extreme that they name: `routes`: the 4 experts of a token differ. Within the 128 positions of one device, no expert is named more than 72 times, a bound that some block reaches.
All inputs are finite; a program needn't handle non-finite values.
Results may differ from a plain program's by a relative error of at most 0.018.
Values may be sent and summed in bfloat16 or wider, within the bound.
No kernel may reach another device: no remote copies, remote signals or barrier semaphores. Data moves between devices by JAX's collectives and lax.ppermute only.
A program may use at most 576 MiB of HBM per device.

v0:
```python
import jax
import jax.numpy as jnp
from jax import lax
from jax.sharding import PartitionSpec as P

KV_HEADS = 8
HD = 64
TOPK = 4


ROPE_BASE = 150000.0
SWIGLU_SLOPE = 1.702
CLAMP_LIMIT = 7.0
NORM_EPSILON = 1e-05
PRECISE = lax.Precision.HIGHEST
CONTRACT_ROWS = (((0,), (0,)), ((), ()))


def rms_scale(values, norm_gain):
    factor = lax.rsqrt(jnp.mean(values * values, axis=-1, keepdims=True) + NORM_EPSILON)
    return (values * factor * norm_gain, factor)


def rms_back(values, factor, norm_gain, upstream):
    scaled = upstream * norm_gain
    value_grad = factor * scaled - values * factor * factor * factor * jnp.mean(
        scaled * values, axis=-1, keepdims=True
    )
    gain_grad = jnp.sum(upstream * values * factor, axis=0)
    return (value_grad, gain_grad)


def rope_tables(positions, head_width):
    half_width = head_width // 2
    frequency = ROPE_BASE ** (-(jnp.arange(half_width, dtype=jnp.float32) * 2.0) / head_width)
    angles = positions.astype(jnp.float32)[:, None] * frequency[None, :]
    return (jnp.cos(angles), jnp.sin(angles))


def rotate(values, cosine_table, sine_table):
    half_width = values.shape[-1] // 2
    front_part = values[..., :half_width]
    back_part = values[..., half_width:]
    cosine_rows = cosine_table[:, None, :]
    sine_rows = sine_table[:, None, :]
    return jnp.concatenate(
        [
            front_part * cosine_rows - back_part * sine_rows,
            back_part * cosine_rows + front_part * sine_rows,
        ],
        axis=-1,
    )


def unrotate(values, cosine_table, sine_table):
    half_width = values.shape[-1] // 2
    front_part = values[..., :half_width]
    back_part = values[..., half_width:]
    cosine_rows = cosine_table[:, None, :]
    sine_rows = sine_table[:, None, :]
    return jnp.concatenate(
        [
            front_part * cosine_rows + back_part * sine_rows,
            back_part * cosine_rows - front_part * sine_rows,
        ],
        axis=-1,
    )


def clamped_glu(joined, expert_width):
    gate_part = jnp.minimum(joined[:, :expert_width], CLAMP_LIMIT)
    linear_part = jnp.clip(joined[:, expert_width:], -CLAMP_LIMIT, CLAMP_LIMIT)
    return (linear_part + 1.0) * gate_part * jax.nn.sigmoid(SWIGLU_SLOPE * gate_part)


def glu_back(joined, expert_width, upstream):
    raw_gate = joined[:, :expert_width]
    raw_linear = joined[:, expert_width:]
    gate_part = jnp.minimum(raw_gate, CLAMP_LIMIT)
    linear_part = jnp.clip(raw_linear, -CLAMP_LIMIT, CLAMP_LIMIT)
    sigmoid_part = jax.nn.sigmoid(SWIGLU_SLOPE * gate_part)
    gate_open = (raw_gate < CLAMP_LIMIT).astype(jnp.float32)
    linear_open = (jnp.abs(raw_linear) < CLAMP_LIMIT).astype(jnp.float32)
    slope_part = sigmoid_part + gate_part * SWIGLU_SLOPE * sigmoid_part * (1.0 - sigmoid_part)
    gate_grad = upstream * (linear_part + 1.0) * slope_part * gate_open
    linear_grad = upstream * gate_part * sigmoid_part * linear_open
    return jnp.concatenate([gate_grad, linear_grad], axis=1)


def attend_forward(queries, key_values, sink_part, row_block):
    length = queries.shape[0]
    head_total = sink_part.shape[0]
    head_width = key_values.shape[1] // 2
    score_scale = head_width ** (-0.5)
    query_heads = queries.reshape(length, head_total, head_width)
    out_blocks = []
    total_blocks = []
    for block_index in range(length // row_block):
        begin_row = block_index * row_block
        end_row = begin_row + row_block
        block_keys = key_values[:end_row, :head_width]
        block_values = key_values[:end_row, head_width:]
        scores = (
            jnp.einsum(
                "qhd,kd->hqk",
                query_heads[begin_row:end_row],
                block_keys,
                preferred_element_type=jnp.float32,
            )
            * score_scale
        )
        row_ids = begin_row + jnp.arange(row_block, dtype=jnp.int32)
        allowed = (row_ids[:, None] >= jnp.arange(end_row, dtype=jnp.int32)[None, :])[None]
        scores = jnp.where(allowed, scores, -1e30)
        row_peak = jnp.maximum(jnp.max(scores, axis=-1), sink_part[:, None])
        weights = jnp.where(allowed, jnp.exp(scores - row_peak[..., None]), 0.0)
        row_total = jnp.sum(weights, axis=-1) + jnp.exp(sink_part[:, None] - row_peak)
        weights_low = (weights / row_total[..., None]).astype(jnp.bfloat16)
        mixed = jnp.einsum(
            "hqk,kd->qhd", weights_low, block_values, preferred_element_type=jnp.float32
        )
        out_blocks.append(mixed.astype(jnp.bfloat16).reshape(row_block, head_total * head_width))
        total_blocks.append(row_peak + jnp.log(row_total))
    return (jnp.concatenate(out_blocks, axis=0), jnp.concatenate(total_blocks, axis=1))


def attend_backward(queries, key_values, sink_part, attended, log_totals, upstream, row_block):
    length = queries.shape[0]
    head_total = sink_part.shape[0]
    head_width = key_values.shape[1] // 2
    score_scale = head_width ** (-0.5)
    query_heads = queries.reshape(length, head_total, head_width)
    out_heads = attended.reshape(length, head_total, head_width)
    grad_heads = upstream.reshape(length, head_total, head_width)
    row_dots = jnp.sum(grad_heads.astype(jnp.float32) * out_heads.astype(jnp.float32), axis=2)
    key_grad = jnp.zeros((length, head_width), jnp.float32)
    value_grad = jnp.zeros((length, head_width), jnp.float32)
    query_parts = []
    for block_index in range(length // row_block):
        begin_row = block_index * row_block
        end_row = begin_row + row_block
        block_queries = query_heads[begin_row:end_row]
        block_grads = grad_heads[begin_row:end_row]
        block_keys = key_values[:end_row, :head_width]
        block_values = key_values[:end_row, head_width:]
        scores = (
            jnp.einsum("qhd,kd->hqk", block_queries, block_keys, preferred_element_type=jnp.float32)
            * score_scale
        )
        row_ids = begin_row + jnp.arange(row_block, dtype=jnp.int32)
        allowed = (row_ids[:, None] >= jnp.arange(end_row, dtype=jnp.int32)[None, :])[None]
        scores = jnp.where(allowed, scores, -1e30)
        weights = jnp.where(allowed, jnp.exp(scores - log_totals[:, begin_row:end_row, None]), 0.0)
        grad_weights = jnp.einsum(
            "qhd,kd->hqk", block_grads, block_values, preferred_element_type=jnp.float32
        )
        block_dots = row_dots[begin_row:end_row].T[:, :, None]
        grad_scores = (weights * (grad_weights - block_dots)).astype(jnp.bfloat16)
        query_parts.append(
            jnp.einsum("hqk,kd->qhd", grad_scores, block_keys, preferred_element_type=jnp.float32)
            * score_scale
        )
        key_grad = key_grad.at[:end_row].add(
            jnp.einsum(
                "hqk,qhd->kd", grad_scores, block_queries, preferred_element_type=jnp.float32
            )
            * score_scale
        )
        value_grad = value_grad.at[:end_row].add(
            jnp.einsum(
                "hqk,qhd->kd",
                weights.astype(jnp.bfloat16),
                block_grads,
                preferred_element_type=jnp.float32,
            )
        )
    sink_grad = -jnp.sum(jnp.exp(sink_part[:, None] - log_totals) * row_dots.T, axis=1)
    query_grad = jnp.concatenate(query_parts, axis=0).reshape(length, head_total * head_width)
    return (query_grad, jnp.concatenate([key_grad, value_grad], axis=1), sink_grad)


def move_rows(blocks):
    return lax.all_to_all(blocks, "seq", split_axis=0, concat_axis=0, tiled=True)


def body(
    hidden,
    out_grad,
    routes,
    norm1_gain,
    qkv_weight,
    qkv_bias,
    sink_logits,
    out_weight,
    out_bias,
    norm2_gain,
    router_weight,
    router_bias,
    gate_up_weight,
    gate_up_bias,
    down_weight,
    down_bias,
):
    tokens = hidden.shape[1]
    model_width = hidden.shape[2]
    groups = lax.axis_size("seq")
    position = lax.axis_index("seq")
    fsdp_count = lax.axis_size("fsdp")
    head_count = sink_logits.shape[0]
    group_heads = head_count // groups
    head_width = HD
    value_heads = KV_HEADS
    expert_width = down_weight.shape[1] * fsdp_count
    capacity = tokens * TOPK * 9 // (8 * groups)
    slot_count = groups * capacity
    length = tokens * groups
    row_block = min(512, length)
    query_width = head_count * head_width
    pair_width = value_heads * head_width
    inputs = hidden[0].astype(jnp.float32)
    first_normed, first_factor = rms_scale(inputs, norm1_gain)
    first_low = first_normed.astype(jnp.bfloat16)
    qkv_full, out_full = (
        lax.all_gather(qkv_weight, ("fsdp", "seq"), axis=1, tiled=True),
        lax.all_gather(out_weight, ("fsdp", "seq"), axis=0, tiled=True),
    )
    projected = jnp.dot(first_low, qkv_full, preferred_element_type=jnp.float32) + qkv_bias
    positions = position * tokens + jnp.arange(tokens, dtype=jnp.int32)
    cosine_table, sine_table = rope_tables(positions, head_width)
    queries = rotate(
        projected[:, :query_width].reshape(tokens, head_count, head_width), cosine_table, sine_table
    ).astype(jnp.bfloat16)
    key_rows = rotate(
        projected[:, query_width : query_width + pair_width].reshape(
            tokens, value_heads, head_width
        ),
        cosine_table,
        sine_table,
    ).astype(jnp.bfloat16)
    value_rows = (
        projected[:, query_width + pair_width :]
        .reshape(tokens, value_heads, head_width)
        .astype(jnp.bfloat16)
    )
    send_queries = queries.reshape(tokens, groups, group_heads * head_width)
    send_pairs = jnp.repeat(
        jnp.concatenate([key_rows, value_rows], axis=2), groups // value_heads, axis=1
    )
    group_queries, group_pairs = (
        lax.all_to_all(send_queries, "seq", split_axis=1, concat_axis=0, tiled=True),
        lax.all_to_all(send_pairs, "seq", split_axis=1, concat_axis=0, tiled=True),
    )
    group_queries = group_queries.reshape(length, group_heads * head_width)
    group_pairs = group_pairs.reshape(length, 2 * head_width)
    sink_part = lax.dynamic_slice_in_dim(sink_logits, position * group_heads, group_heads)
    attended, log_totals = attend_forward(group_queries, group_pairs, sink_part, row_block)
    gathered_heads = lax.all_to_all(attended, "seq", split_axis=0, concat_axis=1, tiled=True)
    branch = jnp.dot(gathered_heads, out_full, preferred_element_type=jnp.float32) + out_bias
    middle = inputs + branch
    second_normed, second_factor = rms_scale(middle, norm2_gain)
    second_low = second_normed.astype(jnp.bfloat16)
    logits = jnp.dot(second_low, router_weight, preferred_element_type=jnp.float32) + router_bias
    chosen = routes[0]
    mixing = jax.nn.softmax(jnp.take_along_axis(logits, chosen, axis=1), axis=-1)
    expert_ids = jnp.arange(groups, dtype=jnp.int32)
    one_hot = (chosen.reshape(-1)[:, None] == expert_ids[None, :]).astype(jnp.int32)
    earlier = jnp.cumsum(one_hot, axis=0) - one_hot
    slot_ids = jnp.sum(earlier * one_hot, axis=1).reshape(tokens, TOPK)
    places = chosen * capacity + slot_ids
    matches = jnp.arange(slot_count, dtype=jnp.int32)[:, None, None] == places[None, :, :]
    dispatch = jnp.sum(matches, axis=2).astype(jnp.bfloat16)
    outgoing = jnp.dot(dispatch, second_low, preferred_element_type=jnp.float32).astype(
        jnp.bfloat16
    )
    expert_inputs = move_rows(outgoing.reshape(groups, capacity, model_width)).reshape(
        groups * capacity, model_width
    )
    joined_weight, joined_bias, down_full, down_shift = (
        lax.all_gather(gate_up_weight, "fsdp", axis=1, tiled=True),
        lax.all_gather(gate_up_bias, "fsdp", axis=1, tiled=True),
        lax.all_gather(down_weight, "fsdp", axis=1, tiled=True),
        lax.all_gather(down_bias, "fsdp", axis=1, tiled=True),
    )
    joined = jnp.dot(
        expert_inputs, joined_weight[0], preferred_element_type=jnp.float32
    ) + joined_bias[0].astype(jnp.float32)
    activated = clamped_glu(joined, expert_width).astype(jnp.bfloat16)
    expert_out = (
        jnp.dot(activated, down_full[0], preferred_element_type=jnp.float32)
        + down_shift[0].astype(jnp.float32)
    ).astype(jnp.bfloat16)
    returned = move_rows(expert_out.reshape(groups, capacity, model_width)).reshape(
        slot_count, model_width
    )
    picked_rows = jnp.take(returned, places, axis=0).astype(jnp.float32)
    combined = jnp.sum(mixing[..., None] * picked_rows, axis=1)
    outputs = middle + combined
    upstream = out_grad[0].astype(jnp.float32)
    mixing_grad = jnp.sum(upstream[:, None, :] * picked_rows, axis=-1)
    picked_grad = mixing * (mixing_grad - jnp.sum(mixing * mixing_grad, axis=-1, keepdims=True))
    choose_table = (chosen[..., None] == expert_ids).astype(jnp.float32)
    logits_grad = jnp.sum(choose_table * picked_grad[..., None], axis=1)
    weighted = jnp.sum(matches.astype(jnp.float32) * mixing[None], axis=2)
    rows_grad = jnp.dot(weighted, upstream, precision=PRECISE).astype(jnp.bfloat16)
    expert_grad_in = move_rows(rows_grad.reshape(groups, capacity, model_width)).reshape(
        groups * capacity, model_width
    )
    joined_weight, joined_bias, down_full, down_shift = (
        lax.all_gather(gate_up_weight, "fsdp", axis=1, tiled=True),
        lax.all_gather(gate_up_bias, "fsdp", axis=1, tiled=True),
        lax.all_gather(down_weight, "fsdp", axis=1, tiled=True),
        lax.all_gather(down_bias, "fsdp", axis=1, tiled=True),
    )
    activated_grad = jnp.dot(expert_grad_in, down_full[0].T, preferred_element_type=jnp.float32)
    joined_grad = glu_back(joined, expert_width, activated_grad).astype(jnp.bfloat16)
    input_rows_grad = jnp.dot(
        joined_grad, joined_weight[0].T, preferred_element_type=jnp.float32
    ).astype(jnp.bfloat16)
    returned_grad = move_rows(input_rows_grad.reshape(groups, capacity, model_width)).reshape(
        slot_count, model_width
    )
    second_grad = jnp.dot(dispatch.T, returned_grad, preferred_element_type=jnp.float32)
    second_grad = second_grad + jnp.dot(
        logits_grad, router_weight.astype(jnp.float32).T, precision=PRECISE
    )
    router_weight_grad = jnp.dot(second_low.astype(jnp.float32).T, logits_grad, precision=PRECISE)
    router_bias_grad = jnp.sum(logits_grad, axis=0)
    middle_part, gain2_grad = rms_back(middle, second_factor, norm2_gain, second_grad)
    middle_grad = upstream + middle_part
    branch_low = middle_grad.astype(jnp.bfloat16)
    qkv_full, out_full = (
        lax.all_gather(qkv_weight, ("fsdp", "seq"), axis=1, tiled=True),
        lax.all_gather(out_weight, ("fsdp", "seq"), axis=0, tiled=True),
    )
    out_term = lax.dot_general(
        gathered_heads, branch_low, CONTRACT_ROWS, preferred_element_type=jnp.float32
    )
    out_bias_grad = jnp.sum(branch_low.astype(jnp.float32), axis=0)
    heads_grad = jnp.dot(branch_low, out_full.T, preferred_element_type=jnp.float32).astype(
        jnp.bfloat16
    )
    group_grad = lax.all_to_all(heads_grad, "seq", split_axis=1, concat_axis=0, tiled=True)
    query_grad, pair_grad, sink_grad = attend_backward(
        group_queries, group_pairs, sink_part, attended, log_totals, group_grad, row_block
    )
    query_grad = lax.optimization_barrier(query_grad.astype(jnp.bfloat16)).astype(jnp.float32)
    back_queries, back_pairs = (
        lax.all_to_all(query_grad, "seq", split_axis=0, concat_axis=1, tiled=True),
        lax.all_to_all(pair_grad, "seq", split_axis=0, concat_axis=1, tiled=True),
    )
    pair_sums = jnp.sum(
        back_pairs.reshape(tokens, value_heads, groups // value_heads, 2 * head_width), axis=2
    )
    pair_sums = lax.optimization_barrier(pair_sums.astype(jnp.bfloat16)).astype(jnp.float32)
    query_plain = unrotate(
        back_queries.reshape(tokens, head_count, head_width), cosine_table, sine_table
    )
    key_plain = unrotate(pair_sums[..., :head_width], cosine_table, sine_table)
    value_plain = pair_sums[..., head_width:]
    projected_grad = jnp.concatenate(
        [
            query_plain.reshape(tokens, query_width),
            key_plain.reshape(tokens, pair_width),
            value_plain.reshape(tokens, pair_width),
        ],
        axis=1,
    ).astype(jnp.bfloat16)
    qkv_term = lax.dot_general(
        first_low, projected_grad, CONTRACT_ROWS, preferred_element_type=jnp.float32
    )
    qkv_bias_grad = jnp.sum(projected_grad.astype(jnp.float32), axis=0)
    first_grad = jnp.dot(projected_grad, qkv_full.T, preferred_element_type=jnp.float32)
    input_part, gain1_grad = rms_back(inputs, first_factor, norm1_gain, first_grad)
    input_grad = middle_grad + input_part
    sink_full = lax.dynamic_update_slice_in_dim(
        jnp.zeros((head_count,), jnp.float32), sink_grad, position * group_heads, 0
    )
    down_term = lax.dot_general(
        activated, expert_grad_in, CONTRACT_ROWS, preferred_element_type=jnp.float32
    )
    down_bias_term = jnp.sum(expert_grad_in.astype(jnp.float32), axis=0)
    joined_term = lax.dot_general(
        expert_inputs, joined_grad, CONTRACT_ROWS, preferred_element_type=jnp.float32
    )
    joined_bias_term = jnp.sum(joined_grad.astype(jnp.float32), axis=0)
    joined_shard, joined_bias_shard, down_shard, down_bias_shard = (
        lax.psum_scatter(joined_term[None], "fsdp", scatter_dimension=1, tiled=True),
        lax.psum_scatter(joined_bias_term[None], "fsdp", scatter_dimension=1, tiled=True),
        lax.psum_scatter(down_term[None], "fsdp", scatter_dimension=1, tiled=True),
        lax.psum_scatter(down_bias_term[None], "fsdp", scatter_dimension=1, tiled=True),
    )
    qkv_shard, out_shard = (
        lax.psum_scatter(qkv_term, ("fsdp", "seq"), scatter_dimension=1, tiled=True),
        lax.psum_scatter(out_term, ("fsdp", "seq"), scatter_dimension=0, tiled=True),
    )
    summed = lax.psum(
        (
            gain1_grad,
            qkv_bias_grad,
            sink_full,
            out_bias_grad,
            gain2_grad,
            router_weight_grad,
            router_bias_grad,
        ),
        ("fsdp", "seq"),
    )
    return (
        outputs.astype(jnp.bfloat16)[None],
        input_grad.astype(jnp.bfloat16)[None],
        summed[0],
        qkv_shard,
        summed[1],
        summed[2],
        out_shard,
        summed[3],
        summed[4],
        summed[5],
        summed[6],
        joined_shard,
        joined_bias_shard,
        down_shard,
        down_bias_shard,
    )


def solution(mesh):
    placed = (
        P("fsdp", "seq", None),
        P("fsdp", "seq", None),
        P("fsdp", "seq", None),
        P(),
        P(None, ("fsdp", "seq")),
        P(),
        P(),
        P(("fsdp", "seq"), None),
        P(),
        P(),
        P(),
        P(),
        P("seq", "fsdp", None),
        P("seq", "fsdp"),
        P("seq", "fsdp", None),
        P("seq", "fsdp"),
    )
    return jax.shard_map(
        body,
        mesh=mesh,
        in_specs=placed,
        out_specs=(
            P("fsdp", "seq", None),
            P("fsdp", "seq", None),
            P(),
            P(None, ("fsdp", "seq")),
            P(),
            P(),
            P(("fsdp", "seq"), None),
            P(),
            P(),
            P(),
            P(),
            P("seq", "fsdp", None),
            P("seq", "fsdp"),
            P("seq", "fsdp", None),
            P("seq", "fsdp"),
        ),
        check_vma=False,
    )
```

profile of v0, /device:TPU:24, one launch (start us, length us, event | category | flops | bytes accessed | tf_op | source)
XLA Modules:
  0.0 2957.0 jit_solution(12781793387065410510)
XLA Ops:
  11.0 177.6 %all-gather.5.cloned.1.call-done = bf16[2880,5120]{0,1:T(8,128)(2,1)} async-done(((bf16[2880,160]{0,1:T(8,128)(2,1)}), bf16[2880,5120]{0,1:T(8,128)(2,1)}) %all-gather.5.cloned.1.call-update) | async-done | bytes 29491216 | tf_op jit(solution)/shard_map/all_gather | solution.py:224
  188.6 15.0 convolution_add_fusion
  233.4 26.1 all-to-all-done.1
  309.3 25.8 all-to-all-done.2
  335.8 45.1 %all-gather.7.cloned.1.call-done = bf16[4096,2880]{0,1:T(8,128)(2,1)} async-done(((bf16[128,2880]{0,1:T(8,128)(2,1)}), bf16[4096,2880]{0,1:T(8,128)(2,1)}) %all-gather.7.cloned.1.call-update) | async-done | bytes 23592976 | tf_op jit(solution)/shard_map/all_gather | solution.py:225
  412.6 67.3 %all-to-all-done.3 = bf16[8,72,2880]{2,1,0:T(8,128)(2,1)} async-done(((bf16[8,72,2880]{2,1,0:T(8,128)(2,1)}), bf16[8,72,2880]{2,1,0:T(8,128)(2,1)}, u32[]{:S(2)}, u32[]{:S(2)}) %all-to-all-start.3) | async-done | bytes 3317792 | tf_op jit(solution)/shard_map/all_to_all | solution.py:183
  499.9 84.7 %all-gather.9.cloned.1.call-done = bf16[1,2880,5760]{2,1,0:T(8,128)(2,1)} async-done(((bf16[1,720,5760]{2,1,0:T(8,128)(2,1)}), bf16[1,2880,5760]{2,1,0:T(8,128)(2,1)}) %all-gather.9.cloned.1.call-update) | async-done | bytes 33177616 | tf_op jit(solution)/shard_map/all_gather | solution.py:279
  584.5 28.9 fusion.12
  613.4 82.0 %all-gather.11.cloned.1.call-done = bf16[1,2880,2880]{2,1,0:T(8,128)(2,1)} async-done(((bf16[1,720,2880]{2,1,0:T(8,128)(2,1)}), bf16[1,2880,2880]{2,1,0:T(8,128)(2,1)}) %all-gather.11.cloned.1.call-update) | async-done | bytes 16588816 | tf_op jit(solution)/shard_map/all_gather | solution.py:281
  695.4 24.7 select_convert_fusion.1
  720.1 17.0 add_convert_fusion
  762.9 55.0 %all-to-all-done.4 = bf16[8,72,2880]{2,1,0:T(8,128)(2,1)S(1)} async-done(((bf16[8,72,2880]{2,1,0:T(8,128)(2,1)}), bf16[8,72,2880]{2,1,0:T(8,128)(2,1)S(1)}, u32[]{:S(2)}, u32[]{:S(2)}) %all-to-all-start.4) | async-done | bytes 3317792 | tf_op jit(solution)/shard_map/all_to_all | solution.py:183
  841.0 19.8 convolution_bitcast_fusion.1
  862.8 27.8 fusion.27
  899.2 72.2 %all-to-all-done.6 = bf16[8,72,2880]{2,1,0:T(8,128)(2,1)S(1)} async-done(((bf16[8,72,2880]{2,1,0:T(8,128)(2,1)}), bf16[8,72,2880]{2,1,0:T(8,128)(2,1)S(1)}, u32[]{:S(2)}, u32[]{:S(2)}) %all-to-all-start.6) | async-done | bytes 3317792 | tf_op jit(solution)/shard_map/all_to_all | solution.py:183
  978.6 20.7 fusion.90
  1014.7 28.4 all_to_all.118
  1114.3 43.7 %all-to-all-done.8 = f32[8,128,512]{2,1,0:T(8,128)} async-done(((f32[8,128,512]{2,1,0:T(8,128)}), f32[8,128,512]{2,1,0:T(8,128)}, u32[]{:S(2)}, u32[]{:S(2)}) %all-to-all-start.8) | async-done | bytes 2097184 | tf_op jit(solution)/shard_map/all_to_all | solution.py:348
  1163.2 24.3 fusion.69
  1187.5 39.4 %convolution_bitcast_fusion = f32[1,2880,5760]{2,1,0:T(8,128)} fusion(bf16[576,2880]{1,0:T(8,128)(2,1)} %bitcast.30, bf16[576,2880]{1,0:T(8,128)(2,1)} %get-tuple-element.104, bf16[576,2880]{1,0:T(8,128)(2,1)} %get-tuple-element.103), kind=kOutput, calls=%fused_computation.2 | convolution fusion | flops 19123568640 | bytes 76308480 | tf_op jit(solution)/shard_map/dot_general | solution.py:382
  1226.9 745.1 %reduce_scatter.65 = f32[1,720,5760]{2,1,0:T(8,128)} reduce-scatter(f32[1,2880,5760]{2,1,0:T(8,128)} %convolution_bitcast_fusion), channel_id=1, replica_groups=mesh['fsdp'=4,'seq'=8] {'fsdp'}, use_global_device_ids=true, dimensions={1}, to_apply=%region_35.36 | reduce-scatter | bytes 82944000 | tf_op jit(solution)/shard_map/reduce_scatter | solution.py:387
  1977.3 18.2 fusion.47
  1995.6 50.8 %all-reduce.5 = (f32[2880]{0:T(1024)}, f32[5120]{0:T(1024)}, f32[64]{0:T(128)}, f32[2880]{0:T(1024)}, f32[2880]{0:T(1024)}, /*index=5*/f32[8]{0:T(128)}) all-reduce(f32[2880]{0:T(1024)S(1)} %get-tuple-element.83, f32[5120]{0:T(1024)S(1)} %convert_reduce_fusion.2, ...), channel_id=1, replica_groups=mesh['fsdp'=4,'seq'=8] {'fsdp','seq'}, use_global_device_ids=true, to_apply=%region_21.22 | all-reduce | flops 13832 | bytes 110656 | tf_op jit(solution)/shard_map/psum | solution.py:396
  2049.1 899.3 %reduce-scatter.15.cloned.1.call-done = f32[2880,160]{0,1:T(8,128)} async-done(((f32[2880,5120]{0,1:T(8,128)}), f32[2880,160]{0,1:T(8,128)}) %reduce-scatter.15.cloned.1.call-update) | async-done | bytes 1843216 | tf_op jit(solution)/shard_map/reduce_scatter | solution.py:393
  (317 shorter events, 301.5 us)
Async XLA Ops:
  7.2 397.9 %copy-start = (bf16[2880,8]{0,1:T(8,128)(2,1)S(1)}, bf16[2880,8]{0,1:T(8,128)(2,1)}, u32[]{:S(2)}) copy-start(bf16[2880,8]{0,1:T(8,128)(2,1)} %param.38) | copy-start | bytes 138244
  7.2 181.4 %all-gather.5.cloned.1.call-start = ((), (), s32[]{:S(2)}) async-start(), calls=%async_computation.16 | async-start | bytes 31088640 | tf_op jit(solution)/shard_map/all_gather | solution.py:224
  7.9 373.0 %all-gather.7.cloned.1.call-start = ((), (), s32[]{:S(2)}) async-start(), calls=%async_computation.17 | async-start | bytes 24330240 | tf_op jit(solution)/shard_map/all_gather | solution.py:225
  8.7 179.9 %copy-start.35 = (f32[2880]{0:T(1024)S(1)}, f32[2880]{0:T(1024)}, u32[]{:S(2)}) copy-start(f32[2880]{0:T(1024)} %param.31) | copy-start | bytes 34564
  8.7 179.9 %copy-start.50 = (f32[5120]{0:T(1024)S(1)}, f32[5120]{0:T(1024)}, u32[]{:S(2)}) copy-start(f32[5120]{0:T(1024)} %param.33) | copy-start | bytes 61444
  8.7 575.8 %all-gather.9.cloned.1.call-start = ((), (), s32[]{:S(2)}) async-start(), calls=%async_computation.18 | async-start | bytes 41472000 | tf_op jit(solution)/shard_map/all_gather | solution.py:279
  11.0 208.2 %copy-start.37 = (f32[128,32]{0,1:T(8,128)}, f32[128,32]{0,1:T(8,128)S(1)}, u32[]{:S(2)}) copy-start(f32[128,32]{0,1:T(8,128)S(1)} %get-tuple-element.123) | copy-start | bytes 49156
  209.5 15.0 all-to-all-start
  224.5 35.0 %all-to-all-start.1 = ((bf16[128,8,512]{0,2,1:T(8,128)(2,1)}), bf16[128,8,512]{0,2,1:T(8,128)(2,1)S(1)}, u32[]{:S(2)}, u32[]{:S(2)}) async-start(bf16[128,8,512]{0,2,1:T(8,128)(2,1)} %bitcast.9), calls=%async_computation.1 | async-start | bytes 2097152 | tf_op jit(solution)/shard_map/all_to_all | solution.py:250
  230.8 464.6 %all-gather.11.cloned.1.call-start = ((), (), s32[]{:S(2)}) async-start(), calls=%async_computation.19 | async-start | bytes 21196800 | tf_op jit(solution)/shard_map/all_gather | solution.py:281
  300.2 35.0 %all-to-all-start.2 = ((bf16[8,128,512]{2,1,0:T(8,128)(2,1)}), bf16[8,128,512]{2,1,0:T(8,128)(2,1)S(1)}, u32[]{:S(2)}, u32[]{:S(2)}) async-start(bf16[8,128,512]{2,1,0:T(8,128)(2,1)} %bitcast.21), calls=%async_computation.2 | async-start | bytes 2097152 | tf_op jit(solution)/shard_map/all_to_all | solution.py:257
  397.1 82.9 %all-to-all-start.3 = ((bf16[8,72,2880]{2,1,0:T(8,128)(2,1)}), bf16[8,72,2880]{2,1,0:T(8,128)(2,1)}, u32[]{:S(2)}, u32[]{:S(2)}) async-start(bf16[8,72,2880]{2,1,0:T(8,128)(2,1)} %bitcast.29), calls=%async_computation.3 | async-start | bytes 6782976 | tf_op jit(solution)/shard_map/all_to_all | solution.py:183
  480.0 215.5 %all-to-all-start.5 = ((bf16[8,72,2880]{2,1,0:T(8,128)(2,1)}), bf16[8,72,2880]{2,1,0:T(8,128)(2,1)S(1)}, u32[]{:S(2)}, u32[]{:S(2)}) async-start(bf16[8,72,2880]{2,1,0:T(8,128)(2,1)} %bitcast.40), calls=%async_computation.5 | async-start | bytes 6782976 | tf_op jit(solution)/shard_map/all_to_all | solution.py:183
  737.1 80.8 %all-to-all-start.4 = ((bf16[8,72,2880]{2,1,0:T(8,128)(2,1)}), bf16[8,72,2880]{2,1,0:T(8,128)(2,1)S(1)}, u32[]{:S(2)}, u32[]{:S(2)}) async-start(bf16[8,72,2880]{2,1,0:T(8,128)(2,1)} %bitcast.276), calls=%async_computation.4 | async-start | bytes 6782976 | tf_op jit(solution)/shard_map/all_to_all | solution.py:183
  743.1 1228.9 %reduce-scatter.21.cloned.1.call-start = ((), (), s32[]{:S(2)}) async-start(), calls=%async_computation.24 | async-start | bytes 1843200
  754.0 1219.7 %reduce-scatter.19.cloned.1.call-start = ((), (), s32[]{:S(2)}) async-start(), calls=%async_computation.23 | async-start | bytes 3686400
  762.8 1286.3 %all-reduce.9.cloned.1.call-start = ((), (), s32[]{:S(2)}) async-start(), calls=%async_computation.22 | async-start | bytes 188416 | tf_op jit(solution)/shard_map/psum | solution.py:396
  840.8 1208.3 %reduce-scatter.23.cloned.1.call-start = ((), (), s32[]{:S(2)}) async-start(), calls=%async_computation.25 | async-start | bytes 42393600
  890.6 80.8 %all-to-all-start.6 = ((bf16[8,72,2880]{2,1,0:T(8,128)(2,1)}), bf16[8,72,2880]{2,1,0:T(8,128)(2,1)S(1)}, u32[]{:S(2)}, u32[]{:S(2)}) async-start(bf16[8,72,2880]{2,1,0:T(8,128)(2,1)} %bitcast.277), calls=%async_computation.6 | async-start | bytes 6782976 | tf_op jit(solution)/shard_map/all_to_all | solution.py:183
  895.8 1153.3 %reduce-scatter.17.cloned.1.call-start = ((), (), s32[]{:S(2)}) async-start(), calls=%async_computation.21 | async-start | bytes 48660480 | tf_op jit(solution)/shard_map/reduce_scatter | solution.py:394
  1090.7 16.7 all-to-all-start.9
  1107.3 50.6 %all-to-all-start.8 = ((f32[8,128,512]{2,1,0:T(8,128)}), f32[8,128,512]{2,1,0:T(8,128)}, u32[]{:S(2)}, u32[]{:S(2)}) async-start(f32[8,128,512]{2,1,0:T(8,128)} %convert.67), calls=%async_computation.8 | async-start | bytes 4194304 | tf_op jit(solution)/shard_map/all_to_all | solution.py:348
  1113.5 1834.9 %reduce-scatter.15.cloned.1.call-start = ((), (), s32[]{:S(2)}) async-start(), calls=%async_computation.20 | async-start | bytes 62177280 | tf_op jit(solution)/shard_map/reduce_scatter | solution.py:393
  1226.9 748.8 %copy-start.52 = (f32[8]{0:T(128)S(1)}, f32[8]{0:T(128)}, u32[]{:S(2)}) copy-start(f32[8]{0:T(128)} %copy-done.51) | copy-start | bytes 100
  (61 other events, 1184.4 us)
Sparse Core Ops, SparseCore 0:
  11.0 177.5 all-gather.4
  190.0 190.8 all-gather.6
  382.6 201.9 all-gather.8
  586.0 109.4 all-gather.10
  754.1 27.5 reduce-scatter.20
  784.3 36.7 reduce-scatter.18
  840.9 143.3 all-reduce.8
  987.5 242.1 reduce-scatter.22
  1237.8 444.5 reduce-scatter.16
  1685.1 1263.2 reduce-scatter.14
where the time goes:
time: 2970 us; the launch traced here: 2960 us
  waiting for transfers between devices  1590 us (54%)
  blocking collectives  836 us (28%)
  matrix products  338 us (11%)
  local copies, waits for them, and re-layouts  66 us (2%)
  other arithmetic  57.1 us (2%)
  starting transfers between devices  57 us (2%)
    reduce_scatter x1, waiting for transfers between devices, body(): lax.psum_scatter(qkv_term, ('fsdp', 'seq'), scatter_dimension=1, tiled=True)  899 us
    reduce_scatter x1, blocking collectives, body(): lax.psum_scatter(joined_term[None], 'fsdp', scatter_dimension=1, tiled=True)  745 us
    all_to_all x4, waiting for transfers between devices, move_rows(): lax.all_to_all(blocks, 'seq', split_axis=0, concat_axis=0, tiled=True)  194 us
    all_gather x1, waiting for transfers between devices, body(): lax.all_gather(qkv_weight, ('fsdp', 'seq'), axis=1, tiled=True)  178 us
    all_gather x1, waiting for transfers between devices, body(): lax.all_gather(gate_up_weight, 'fsdp', axis=1, tiled=True)  84.7 us
    all_gather x1, waiting for transfers between devices, body(): lax.all_gather(down_weight, 'fsdp', axis=1, tiled=True)  82 us
  transfers between devices with their start and end apart: 19, of which 12 were waited for; matrix products, arithmetic and copies ran while one was open for 14% of the time, Pallas kernels for 0%

commit v1 on v0

v1 whole, which is shorter than its diff:
```python
import functools
import math

import jax
import jax.numpy as jnp
import numpy as np
from jax import lax
from jax.experimental.layout import Layout, with_layout_constraint
from jax.experimental import pallas as pl
from jax.experimental.pallas import tpu as pltpu
from jax.sharding import PartitionSpec as P

KV_HEADS = 8
HD = 64
TOPK = 4

ROPE_BASE = 150000.0
SWIGLU_SLOPE = 1.702
CLAMP_LIMIT = 7.0
NORM_EPSILON = 1e-05
PRECISE = lax.Precision.HIGHEST
BOTH = ("fsdp", "seq")
LOW = jnp.bfloat16
WIDE = jnp.float32
NN = (((1,), (0,)), ((), ()))
NT = (((1,), (1,)), ((), ()))
TN = (((0,), (0,)), ((), ()))


def mul(left, right, dims=NN):
    return lax.dot_general(left, right, dims, preferred_element_type=WIDE)


def straight(values):
    return with_layout_constraint(values, Layout(major_to_minor=tuple(range(values.ndim))))


def blank(shape, dtype):
    return pl.pallas_call(
        lambda out: None,
        out_specs=pl.BlockSpec(memory_space=pl.ANY),
        out_shape=jax.ShapeDtypeStruct(shape, dtype),
        name="blank",
    )()


def ring_order(count):
    return list(range(0, count, 2)) + list(range(1, count, 2))[::-1]


def ring_pairs(count):
    order = ring_order(count)
    ahead = [(order[i], order[(i + 1) % count]) for i in range(count)]
    return ahead, [(b, a) for a, b in ahead]


def ring_ids():
    count = lax.axis_size("seq")
    order = ring_order(count)
    rank = {p: i for i, p in enumerate(order)}
    table = [[order[(rank[p] + j) % count] for j in range(count)] for p in range(count)]
    return jnp.asarray(np.array(table, np.int32))[lax.axis_index("seq")]


def send(values, axis, pairs):
    if values.ndim == 2 and values.shape[0] % 16 == 0:
        blocks = straight(values.reshape(values.shape[0] // 16, 16, values.shape[1]))
        return straight(lax.ppermute(blocks, axis, pairs)).reshape(values.shape)
    return straight(lax.ppermute(straight(values), axis, pairs))


def swap(values, axis, bit):
    return send(values, axis, [(i, i ^ bit) for i in range(lax.axis_size(axis))])


class Freight:
    def __init__(self):
        self.hurried, self.flying, self.pending = [], [], []
        self.now = 0

    def load(self, values, sizes, land, when, lags, start=0):
        for size, delay, lag in zip(sizes, when, lags):
            piece = values[start : start + size]
            start += size
            self.after(delay, piece, functools.partial(self.hurry, land=land, lag=lag))

    def hurry(self, values, land, lag=1):
        self.hurried.append((values, land, lag))

    def need(self, values, use):
        self.pending.append((values, use))

    def __call__(self, *values):
        self.now += 1
        due = self.pending + [(array, use) for array, use, when in self.flying if when <= self.now]
        self.flying = [flight for flight in self.flying if flight[2] > self.now]
        self.pending = []
        if due:
            out = lax.optimization_barrier((*values, *(array for array, _ in due)))
            values = out[: len(values)]
            for array, (_, use) in zip(out[len(values) :], due):
                use(array)
        going, self.hurried = self.hurried, []
        for fresh, use, lag in going:
            self.flying.append((swap(fresh, "fsdp", 2), use, self.now + lag))
        return values

    def after(self, events, values, use):
        if events == 0:
            return use(values)
        self.need(values, lambda held: self.after(events - 1, held, use))

    def chain(self, values, steps, use):
        if not steps:
            return use(values)
        self.need(values, lambda held: self.chain(steps[0](held), steps[1:], use))

    def blocks(self, terms, use):
        def near_there(near):
            away = straight((terms[2].astype(WIDE) + near[0].astype(WIDE)).astype(LOW))
            own = terms[0].astype(WIDE) + near[1].astype(WIDE)
            self.hurry(away, lambda far: use(own + far.astype(WIDE)), 2)

        self.need(swap(straight(jnp.stack([terms[3], terms[1]])), "fsdp", 1), near_there)

    def settle(self):
        while self.pending:
            due, self.pending = self.pending, []
            for array, use in due:
                use(array)

    def finish(self):
        self.settle()
        while self.flying or self.hurried:
            self.flying += [(swap(fresh, "fsdp", 2), use, 0) for fresh, use, _ in self.hurried]
            due, self.flying, self.hurried = self.flying, [], []
            for array, use, _ in due:
                use(array)
            self.settle()


def alone(*values):
    return values


def ring_gather_steps(rows, ids, beside=alone, after=None):
    count = lax.axis_size("seq")
    ahead, behind = ring_pairs(count)
    tokens = rows.shape[0]
    half = tokens // 2

    def put(full, part, index, offset=0):
        return straight(lax.dynamic_update_slice(full, part, (index * tokens + offset, 0)))

    rows = straight(rows)
    if after is not None:
        rows, _ = lax.optimization_barrier((rows, after))
    full = put(blank((count * tokens, rows.shape[1]), rows.dtype), rows, ids[0])
    up = down = rows
    for hop in range(1, (count + 1) // 2):
        up, down = beside(up, down)
        up, down = send(up, "seq", ahead), send(down, "seq", behind)
        landed = yield up, down
        if landed is not None:
            up, down = landed
            yield None
        full = put(put(full, up, ids[count - hop]), down, ids[hop])
    if count % 2 == 0:
        up, down = beside(straight(up[:half]), straight(down[half:]))
        up, down = send(up, "seq", ahead), send(down, "seq", behind)
        yield up, down
        full = put(put(full, up, ids[count // 2]), down, ids[count // 2], half)
    yield full, (up, down)


def ring_gather(rows, ids, beside=alone):
    for out in ring_gather_steps(rows, ids, beside):
        pass
    return out


def ring_reduce(term, ids, beside=alone):
    count = lax.axis_size("seq")
    ahead, behind = ring_pairs(count)
    middle = count // 2
    if count == 1:
        return term(ids[0])
    up = down = None
    if count % 2 == 0:
        whole = straight(term(ids[middle]).astype(LOW))
        half = whole.shape[0] // 2
        up, down = beside(straight(whole[:half]), straight(whole[half:]))
        up = send(up, "seq", ahead).astype(WIDE)
        down = send(down, "seq", behind).astype(WIDE)
        up = jnp.pad(up, ((0, half), (0, 0)))
        down = jnp.pad(down, ((half, 0), (0, 0)))
    for hop in range((count - 1) // 2, 0, -1):
        send_up = term(ids[hop])
        send_down = term(ids[count - hop])
        if up is not None:
            send_up, send_down = send_up + up, send_down + down
        send_up, send_down = beside(straight(send_up.astype(LOW)), straight(send_down.astype(LOW)))
        up = send(send_up, "seq", ahead).astype(WIDE)
        down = send(send_down, "seq", behind).astype(WIDE)
    return straight(term(ids[0]) + up + down)


def xor_steps(axis):
    def step(held, bit):
        return jnp.concatenate([held, swap(held, axis, bit)])

    bits = [1 << i for i in range((lax.axis_size(axis) - 1).bit_length())]
    return [functools.partial(step, bit=bit) for bit in bits]


def straighten(parts, axis):
    count = parts.shape[0]
    me = lax.axis_index(axis)
    bit = 1
    while bit < count:
        other = jnp.stack([parts[j ^ bit] for j in range(count)])
        parts = jnp.where((me & bit) != 0, other, parts)
        bit *= 2
    return parts


def sum_steps(axes):
    def step(values, axis, bit):
        return values + swap(values, axis, bit)

    return [
        functools.partial(step, axis=axis, bit=1 << i)
        for axis in axes
        for i in range((lax.axis_size(axis) - 1).bit_length())
    ]


def spread(total, parts):
    ends = [round(total * sum(parts[: i + 1]) / sum(parts) / 16) * 16 for i in range(len(parts))]
    ends[-1] = total
    return [end - start for start, end in zip([0] + ends, ends)]


def add_pieces(kept, pieces):
    total, sums = kept
    start = 0
    for piece in pieces:
        size = min(piece.shape[0], total.shape[0] - start)
        rows = total[start : start + size] + piece[:size].astype(WIDE)
        total = straight(lax.dynamic_update_slice(total, rows, (start, 0)))
        start += size
    return total, sums[0] + pieces[-1][-1].astype(WIDE)


UNIT_PARTS = [
    3, 1, 2, 1, 0, 1, 3, 2, 1, 0, 0, 1, 2, 0, 0, 3, 3, 3, 1, 2, 0, 0, 1, 1, 0, 1, 2, 1, 0, 3, 0, 3,
    0, 2, 0, 2, 0, 2, 0, 1, 1, 2, 0, 1, 1, 3, 1, 3, 3, 3, 0, 1, 2, 1, 0, 1, 1, 0, 1, 0, 2, 2, 0, 2,
    2, 0, 3, 0, 3, 3, 0, 0, 2, 1, 3, 3, 1, 2, 0, 1, 3, 0, 1, 0, 2, 2, 2, 1, 3, 3, 3, 2, 2, 3, 1, 0,
    0, 3, 3, 3, 0, 1, 2, 2, 3, 2, 2, 2, 1, 0, 0, 1, 1, 3, 3, 2, 1, 1, 1, 1, 2, 0, 3, 2, 0, 3, 0, 0,
    3, 2, 2, 2, 3, 3, 3, 3, 1, 1, 1, 0, 0, 3, 2, 2, 2, 3, 2, 3, 3, 2, 2, 3, 2, 2, 0, 1, 1, 1, 0, 3,
]
BLOCK_PARTS = [
    0, 3, 1, 2, 2, 3, 0, 1, 1, 2, 3, 0, 3, 0, 1, 2, 3, 0, 1, 2, 1, 0, 2, 3, 1, 2, 3, 0, 2, 3, 1, 0,
]


def group_places(groups):
    return [1, 4, 6, 3, 2, 0, 5, 7] if groups == 8 else list(range(groups))


@functools.lru_cache(None)
def unit_plan(fsdp, groups, query_width, pair_width):
    columns = query_width + 2 * pair_width
    per_device = columns // (fsdp * groups)
    group_query, group_pair = query_width // groups, pair_width // groups
    unit = math.gcd(math.gcd(per_device, group_query), group_pair)
    rounds = per_device // unit
    total = fsdp * groups
    wanted = []
    for index in range(columns // unit):
        column = index * unit
        if column < query_width:
            group, place = divmod(column, group_query)
        elif column < query_width + pair_width:
            group, place = divmod(column - query_width, group_pair)
            place += group_query
        else:
            group, place = divmod(column - query_width - pair_width, group_pair)
            place += group_query + group_pair
        wanted.append((index // rounds, index % rounds, group, place // unit))
    filled = {}
    edges = []
    near = UNIT_PARTS if groups == 8 and len(wanted) == len(UNIT_PARTS) else None
    spots = group_places(groups)
    for index, (source, slot, group, place) in enumerate(wanted):
        own = near[index] if near else source // groups
        for turn in (0, 1, 2, 3):
            part = own ^ turn
            if filled.get((part, group), 0) < rounds:
                filled[(part, group)] = filled.get((part, group), 0) + 1
                edges.append((source, slot, part * groups + spots[group], place))
                break
    steps = []
    for _ in range(rounds):
        taken = {}

        def find(source, seen):
            for edge in edges:
                if edge[0] != source or edge[2] in seen:
                    continue
                seen.add(edge[2])
                if edge[2] not in taken or find(taken[edge[2]][0], seen):
                    taken[edge[2]] = edge
                    return True
            return False

        for source in range(total):
            find(source, set())
        steps.append(sorted(taken.values()))
        for edge in taken.values():
            edges.remove(edge)
    send = np.zeros((rounds, total), np.int32)
    place_at = np.zeros((rounds, total), np.int32)
    pairs = []
    for i, step in enumerate(steps):
        pairs.append([(edge[0], edge[2]) for edge in step])
        for source, slot, target, place in step:
            send[i, source] = slot
            place_at[i, target] = place
    count = fsdp * rounds
    order = np.zeros((total, count), np.int32)
    back = np.zeros((total, count), np.int32)
    for device in range(total):
        part, group = divmod(device, groups)
        for j in range(fsdp):
            for i in range(rounds):
                place = place_at[i, (part ^ j) * groups + group]
                order[device, place] = j * rounds + i
                back[device, j * rounds + i] = place
    home = np.argsort(send, axis=0).astype(np.int32)
    return unit, rounds, pairs, send, order, back, home


def out_pairs(fsdp, groups):
    total = fsdp * groups
    parts = BLOCK_PARTS if (fsdp, groups) == (4, 8) else [b % fsdp for b in range(total)]
    spots = group_places(groups)
    moves = [(b, parts[b] * groups + spots[b // fsdp]) for b in range(total)]
    found = np.zeros((total, fsdp), np.int32)
    for b, target in moves:
        part, spot = divmod(target, groups)
        for turn in range(fsdp):
            found[(part ^ turn) * groups + spot, b % fsdp] = turn
    return moves, found


def turn(front, back, cosine, sine):
    return front * cosine - back * sine, back * cosine + front * sine


def forward_kernel(
    at_ref, sink_ref, front_ref, back_ref, key_front, key_back, value_front, value_back,
    query_bias, pair_bias, cos_ref, sin_ref,
    turned_ref, pairs_ref, out_ref, total_ref, keys,
    *, block, scale,
):
    head = pl.program_id(0)
    length = front_ref.shape[1]
    half = HD // 2
    cosine, sine = cos_ref[...], sin_ref[...]

    @pl.when(head == 0)
    def _():
        front, back = turn(
            key_front[...] + pair_bias[:half], key_back[...] + pair_bias[half:HD], cosine, sine
        )
        key = jnp.concatenate([front, back], axis=0)
        pairs_ref[:HD, :] = key.astype(LOW)
        pairs_ref[HD : HD + half, :] = (value_front[...] + pair_bias[HD : HD + half]).astype(LOW)
        pairs_ref[HD + half :, :] = (value_back[...] + pair_bias[HD + half :]).astype(LOW)
        keys[...] = key.T.astype(LOW)

    front, back = turn(
        front_ref[...] + query_bias[:half], back_ref[...] + query_bias[half:], cosine, sine
    )
    turned_ref[:half, :] = (front.astype(LOW).astype(WIDE) * scale).astype(LOW)
    turned_ref[half:, :] = (back.astype(LOW).astype(WIDE) * scale).astype(LOW)
    sink = sink_ref[head]
    count = length // block
    below = lax.broadcasted_iota(jnp.int32, (block, block), 0) > lax.broadcasted_iota(
        jnp.int32, (block, block), 1
    )
    for index in range(count):
        columns = pl.ds(index * block, block)
        query = turned_ref[:, columns]

        def scores(rows):
            return mul(keys[rows, :], query)

        def step(start, carry, masked):
            peak, total, mixed = carry
            rows = pl.ds(start, block)
            tile = scores(rows)
            if masked:
                tile = jnp.where(below, -1e30, tile)
            top = jnp.maximum(peak, jnp.max(tile, axis=0, keepdims=True))
            weights = jnp.exp(tile - top)
            shrink = jnp.exp(peak - top)
            total = total * shrink + jnp.sum(weights, axis=0, keepdims=True)
            mixed = mixed * shrink + mul(pairs_ref[HD:, rows], weights.astype(LOW))
            return top, total, mixed

        carry = (
            jnp.full((1, block), sink, WIDE),
            jnp.ones((1, block), WIDE),
            jnp.zeros((HD, block), WIDE),
        )
        if count <= 4:
            for earlier in range(index):
                carry = step(earlier * block, carry, False)
        elif index:
            carry = lax.fori_loop(
                0, index, lambda i, c: step(pl.multiple_of(i * block, block), c, False), carry
            )
        peak, total, mixed = step(index * block, carry, True)
        out_ref[:, columns] = (mixed / total).astype(LOW)
        total_ref[0, :, columns] = peak + jnp.log(total)


def attend(at, projected, bias, sinks, cosine, sine, heads):
    length = projected.shape[1]
    rows = heads * HD
    half = HD // 2
    block = min(256, length)
    last = rows // (2 * HD)

    def piece(place):
        return pl.BlockSpec((half, length), lambda h, at: (at[place], 0))

    return pl.pallas_call(
        functools.partial(forward_kernel, block=block, scale=HD**-0.5),
        grid_spec=pltpu.PrefetchScalarGridSpec(
            num_scalar_prefetch=1,
            grid=(heads,),
            in_specs=[
                pl.BlockSpec(memory_space=pltpu.SMEM),
                pl.BlockSpec((half, length), lambda h, at: (at[2 * h], 0)),
                pl.BlockSpec((half, length), lambda h, at: (at[2 * h + 1], 0)),
                piece(2 * heads),
                piece(2 * heads + 1),
                piece(2 * heads + 2),
                piece(2 * heads + 3),
                pl.BlockSpec((HD, 1), lambda h, at: (h, 0)),
                pl.BlockSpec((2 * HD, 1), lambda h, at: (last, 0)),
                pl.BlockSpec((half, length), lambda h, at: (0, 0)),
                pl.BlockSpec((half, length), lambda h, at: (0, 0)),
            ],
            out_specs=[
                pl.BlockSpec((HD, length), lambda h, at: (h, 0)),
                pl.BlockSpec((2 * HD, length), lambda h, at: (0, 0)),
                pl.BlockSpec((HD, length), lambda h, at: (at[2 * heads + 4 + h], 0)),
                pl.BlockSpec((1, 1, length), lambda h, at: (h, 0, 0)),
            ],
            scratch_shapes=[pltpu.VMEM((length, HD), LOW)],
        ),
        out_shape=[
            jax.ShapeDtypeStruct((rows, length), LOW),
            jax.ShapeDtypeStruct((2 * HD, length), LOW),
            jax.ShapeDtypeStruct((rows, length), LOW),
            jax.ShapeDtypeStruct((heads, 1, length), WIDE),
        ],
        compiler_params=pltpu.CompilerParams(
            dimension_semantics=("arbitrary",), vmem_limit_bytes=40 * 2**20
        ),
        cost_estimate=pl.CostEstimate(
            flops=0, bytes_accessed=0, transcendentals=0
        ),
        name="attend",
    )(at, sinks, *[projected] * 6, bias, bias, cosine, sine)


def backward_kernel(
    at_ref, sink_ref, turned_ref, pairs_ref, out_ref, grad_ref, total_ref, cos_ref, sin_ref,
    query_ref, pair_ref, sink_grad_ref, keys, values, key_sum, value_sum, query_rows, grad_rows,
    *, block, scale,
):
    head = pl.program_id(0)
    length = turned_ref.shape[1]
    half = HD // 2
    count = length // block

    @pl.when(head == 0)
    def _():
        keys[...] = pairs_ref[:HD, :].astype(WIDE).T.astype(LOW)
        values[...] = pairs_ref[HD:, :].astype(WIDE).T.astype(LOW)
        key_sum[...] = jnp.zeros_like(key_sum)
        value_sum[...] = jnp.zeros_like(value_sum)

    query_rows[...] = turned_ref[...].astype(WIDE).T.astype(LOW)
    grad_rows[...] = grad_ref[...].astype(WIDE).T.astype(LOW)
    below = lax.broadcasted_iota(jnp.int32, (block, block), 0) > lax.broadcasted_iota(
        jnp.int32, (block, block), 1
    )
    deltas = jnp.sum(grad_ref[...].astype(WIDE) * out_ref[...].astype(WIDE), axis=0, keepdims=True)
    totals = total_ref[0]
    sink_term = -jnp.sum(jnp.exp(sink_ref[head] - totals) * deltas, axis=1, keepdims=True)
    sink_grad_ref[0] = jnp.broadcast_to(sink_term, (1, 128))
    for index in range(count):
        columns = pl.ds(index * block, block)
        query = turned_ref[:, columns]
        grad = grad_ref[:, columns]
        total = totals[:, index * block : (index + 1) * block]
        delta = deltas[:, index * block : (index + 1) * block]

        def step(start, query_sum, masked):
            rows = pl.ds(start, block)
            weights = jnp.exp(mul(keys[rows, :], query) - total)
            if masked:
                weights = jnp.where(below, 0.0, weights)
            inner = (weights * (mul(values[rows, :], grad) - delta)).astype(LOW)
            key_sum[rows, :] += mul(inner, query_rows[columns, :])
            value_sum[rows, :] += mul(weights.astype(LOW), grad_rows[columns, :])
            return query_sum + mul(pairs_ref[:HD, rows], inner)

        query_sum = jnp.zeros((HD, block), WIDE)
        if count <= 4:
            for earlier in range(index):
                query_sum = step(earlier * block, query_sum, False)
        elif index:
            query_sum = lax.fori_loop(
                0, index, lambda i, c: step(pl.multiple_of(i * block, block), c, False), query_sum
            )
        query_sum = step(index * block, query_sum, True)
        rounded = (query_sum * scale).astype(LOW).astype(WIDE)
        cosine, sine = cos_ref[:, columns], sin_ref[:, columns]
        front, back = turn(rounded[:half], rounded[half:], cosine, -sine)
        query_ref[:half, columns] = front.astype(LOW)
        query_ref[half:, columns] = back.astype(LOW)

    @pl.when(head == pl.num_programs(0) - 1)
    def _():
        rounded = key_sum[...].T.astype(LOW).astype(WIDE)
        front, back = turn(rounded[:half], rounded[half:], cos_ref[...], -sin_ref[...])
        pair_ref[:half, :] = front.astype(LOW)
        pair_ref[half:HD, :] = back.astype(LOW)
        pair_ref[HD:, :] = value_sum[...].T.astype(LOW)


def attend_back(at, sinks, turned, pairs, attended, upstream, totals, cosine, sine):
    heads, _, length = totals.shape
    rows = heads * HD
    block = min(256, length)
    by_head = pl.BlockSpec((HD, length), lambda h, at: (h, 0))
    moved = pl.BlockSpec((HD, length), lambda h, at: (at[2 * heads + 4 + h], 0))
    table = pl.BlockSpec((HD // 2, length), lambda h, at: (0, 0))
    whole = pl.BlockSpec((2 * HD, length), lambda h, at: (0, 0))
    return pl.pallas_call(
        functools.partial(backward_kernel, block=block, scale=HD**-0.5),
        grid_spec=pltpu.PrefetchScalarGridSpec(
            num_scalar_prefetch=1,
            grid=(heads,),
            in_specs=[
                pl.BlockSpec(memory_space=pltpu.SMEM),
                by_head,
                whole,
                moved,
                moved,
                pl.BlockSpec((1, 1, length), lambda h, at: (h, 0, 0)),
                table,
                table,
            ],
            out_specs=[by_head, whole, pl.BlockSpec((1, 1, 128), lambda h, at: (h, 0, 0))],
            scratch_shapes=[
                pltpu.VMEM((length, HD), LOW),
                pltpu.VMEM((length, HD), LOW),
                pltpu.VMEM((length, HD), WIDE),
                pltpu.VMEM((length, HD), WIDE),
                pltpu.VMEM((length, HD), LOW),
                pltpu.VMEM((length, HD), LOW),
            ],
        ),
        out_shape=[
            jax.ShapeDtypeStruct((rows, length), LOW),
            jax.ShapeDtypeStruct((2 * HD, length), LOW),
            jax.ShapeDtypeStruct((heads, 1, 128), WIDE),
        ],
        compiler_params=pltpu.CompilerParams(
            dimension_semantics=("arbitrary",), vmem_limit_bytes=40 * 2**20
        ),
        cost_estimate=pl.CostEstimate(
            flops=0, bytes_accessed=0, transcendentals=0
        ),
        name="attend_back",
    )(at, sinks, turned, pairs, attended, upstream, totals, cosine, sine)


EXTRA = 16


def term_kernel(at_ref, left_ref, right_ref, *refs, others):
    size = left_ref.shape[0]
    total = mul(left_ref[...], right_ref[...])
    sums = jnp.sum(right_ref[...].astype(WIDE), axis=0, keepdims=True)
    sums = jnp.broadcast_to(sums, (EXTRA, sums.shape[1]))
    for other in refs[:others]:
        total = total + other[:size, :].astype(WIDE)
        sums = sums + other[size:, :].astype(WIDE)
    if len(refs) > others + 1:
        refs[-2][...], refs[-1][...] = total, sums
    else:
        refs[-1][:size, :] = total.astype(LOW)
        refs[-1][size:, :] = sums.astype(LOW)


def weight_term(left, right, index, size, *others, final=False):
    depth, width = right.shape
    block = min(640, width)
    at = jnp.full((1,), index, jnp.int32)

    def tile(rows):
        return pl.BlockSpec((rows, block), lambda n, at: (0, n))

    low = jax.ShapeDtypeStruct((size + EXTRA, width), LOW)
    split = [jax.ShapeDtypeStruct((rows, width), WIDE) for rows in (size, EXTRA)]
    return pl.pallas_call(
        functools.partial(term_kernel, others=len(others)),
        grid_spec=pltpu.PrefetchScalarGridSpec(
            num_scalar_prefetch=1,
            grid=(pl.cdiv(width, block),),
            in_specs=[
                pl.BlockSpec((size, depth), lambda n, at: (at[0], 0)),
                pl.BlockSpec((depth, block), lambda n, at: (0, n)),
                *[tile(size + EXTRA)] * len(others),
            ],
            out_specs=[tile(size), tile(EXTRA)] if final else tile(size + EXTRA),
        ),
        out_shape=split if final else low,
        compiler_params=pltpu.CompilerParams(
            dimension_semantics=("arbitrary",), vmem_limit_bytes=32 * 2**20
        ),
        cost_estimate=pl.CostEstimate(
            flops=2 * size * depth * width,
            bytes_accessed=2 * (depth * (size + width) + (2 + len(others)) * size * width),
            transcendentals=0,
        ),
        name="weight_term",
    )(at, left, right, *others)


def rms_scale(values, norm_gain):
    factor = lax.rsqrt(jnp.mean(values * values, axis=-1, keepdims=True) + NORM_EPSILON)
    return (values * factor * norm_gain, factor)


def rms_back(values, factor, norm_gain, upstream):
    scaled = upstream * norm_gain
    value_grad = factor * scaled - values * factor * factor * factor * jnp.mean(
        scaled * values, axis=-1, keepdims=True
    )
    gain_grad = jnp.sum(upstream * values * factor, axis=0)
    return (value_grad, gain_grad)


def clamped_glu(joined, expert_width):
    gate_part = jnp.minimum(joined[:, :expert_width], CLAMP_LIMIT)
    linear_part = jnp.clip(joined[:, expert_width:], -CLAMP_LIMIT, CLAMP_LIMIT)
    return (linear_part + 1.0) * gate_part * jax.nn.sigmoid(SWIGLU_SLOPE * gate_part)


def glu_back(joined, expert_width, upstream):
    raw_gate = joined[:, :expert_width]
    raw_linear = joined[:, expert_width:]
    gate_part = jnp.minimum(raw_gate, CLAMP_LIMIT)
    linear_part = jnp.clip(raw_linear, -CLAMP_LIMIT, CLAMP_LIMIT)
    sigmoid_part = jax.nn.sigmoid(SWIGLU_SLOPE * gate_part)
    gate_open = (raw_gate < CLAMP_LIMIT).astype(jnp.float32)
    linear_open = (jnp.abs(raw_linear) < CLAMP_LIMIT).astype(jnp.float32)
    slope_part = sigmoid_part + gate_part * SWIGLU_SLOPE * sigmoid_part * (1.0 - sigmoid_part)
    gate_grad = upstream * (linear_part + 1.0) * slope_part * gate_open
    linear_grad = upstream * gate_part * sigmoid_part * linear_open
    return jnp.concatenate([gate_grad, linear_grad], axis=1)


def mixing_of(rows, routes, router_weight, router_bias):
    logits = mul(rows, router_weight) + router_bias
    experts = jnp.arange(router_bias.shape[0], dtype=jnp.int32)
    chosen = jnp.any(routes[:, :, None] == experts, axis=1)
    logits = jnp.where(chosen, logits, -jnp.inf)
    weights = jnp.exp(logits - jnp.max(logits, axis=1, keepdims=True))
    return weights / jnp.sum(weights, axis=1, keepdims=True)


def rows_of(values, index, size):
    return lax.dynamic_slice_in_dim(values, index * size, size, axis=0)


def columns_of(values, index, size):
    return lax.dynamic_slice_in_dim(values, index * size, size, axis=1)


def body(
    hidden,
    out_grad,
    routes,
    norm1_gain,
    qkv_weight,
    qkv_bias,
    sink_logits,
    out_weight,
    out_bias,
    norm2_gain,
    router_weight,
    router_bias,
    gate_up_weight,
    gate_up_bias,
    down_weight,
    down_bias,
):
    tokens = hidden.shape[1]
    groups = lax.axis_size("seq")
    position = lax.axis_index("seq")
    spots = np.argsort(np.array(group_places(lax.axis_size("seq")))).astype(np.int32)
    group = jnp.asarray(spots)[position]
    fsdp = lax.axis_size("fsdp")
    part = lax.axis_index("fsdp")
    device = part * groups + position
    head_count = sink_logits.shape[0]
    group_heads = head_count // groups
    expert_width = down_weight.shape[1] * fsdp
    capacity = tokens * TOPK * 9 // (8 * groups)
    slot_count = groups * capacity
    length = tokens * groups
    query_width = head_count * HD
    pair_width = KV_HEADS * HD
    group_query = group_heads * HD
    ids = ring_ids()

    planned = groups == KV_HEADS and fsdp == 4 and qkv_weight.shape[1] % (HD // 2) == 0
    qkv_rows = straight(qkv_weight.T)
    held = {}
    freight = Freight()
    out_moves, out_found = out_pairs(fsdp, groups)

    def keep(name):
        return lambda values: held.__setitem__(name, values)

    def gather_parts(name):
        def land(far):
            mine = held[name]

            def near(other):
                held[name] = jnp.stack([mine, other[0], far, other[1]])

            freight.need(swap(jnp.stack([mine, far]), "fsdp", 1), near)

        return land

    def arrived(name, lag=1):
        def use(block):
            held[name] = block
            freight.hurry(block, gather_parts(name), lag)

        return use

    if planned:
        unit, rounds, pairs, send_slots, order, back, home = unit_plan(
            fsdp, groups, query_width, pair_width
        )
        slots = jnp.asarray(send_slots)[:, device]
        bias_at = (group, group, group)
        head_units = jnp.asarray(order)[device]
        units = qkv_rows.reshape(rounds, unit, -1)
        blocks = [
            send(lax.dynamic_index_in_dim(units, slots[i], 0, keepdims=False), BOTH, pairs[i])
            for i in range(rounds)
        ]
        freight.after(1, straight(jnp.stack(blocks)), arrived("qkv"))
    else:
        pair_index = group * KV_HEADS // groups
        bias_at = (group, pair_index, pair_index)
        head_units = jnp.arange(2 * group_heads + 4, dtype=jnp.int32)
    bias_group = jnp.concatenate(
        [
            rows_of(qkv_bias[:query_width], bias_at[0], group_query),
            rows_of(qkv_bias[query_width : query_width + pair_width], bias_at[1], HD),
            rows_of(qkv_bias[query_width + pair_width :], bias_at[2], HD),
        ]
    )
    block_heads = out_weight.shape[0] // HD
    by_block = out_weight.shape[0] % HD == 0
    head_ids = jnp.arange(group_heads, dtype=jnp.int32)
    if by_block:
        turns = jnp.asarray(np.repeat(out_found, block_heads, axis=1))[device]
        head_ids = turns * block_heads + head_ids % block_heads
    places_at = jnp.concatenate([head_units, head_ids])

    def open_out(weight):
        freight.need(send(weight, BOTH, out_moves), arrived("out", 2))

    def open_expert(name):
        def use(shard):
            held[name] = lax.all_gather(shard, "fsdp", axis=0, tiled=True)

        return use

    freight.need(out_weight, open_out)
    freight.after(4, gate_up_weight[0], open_expert("gate_up"))
    freight.after(4, down_weight[0], open_expert("down"))

    inputs = hidden[0].astype(WIDE)
    first_normed, first_factor = rms_scale(inputs, norm1_gain)
    first_full, first_last = ring_gather(first_normed.astype(LOW), ids, freight)
    frequency = ROPE_BASE ** (-(jnp.arange(HD // 2, dtype=WIDE) * 2.0) / HD)
    angles = jnp.arange(length, dtype=jnp.int32).astype(WIDE)[None, :] * frequency[:, None]
    cosine, sine = jnp.cos(angles), jnp.sin(angles)
    sink_part = rows_of(sink_logits, group, group_heads)
    gather = ring_gather_steps(out_grad[0], ids, freight, first_last)
    next(gather)
    if planned:
        qkv_group = straight(held["qkv"]).reshape(fsdp * rounds * unit, -1)
    else:
        qkv_full = lax.all_gather(qkv_rows, BOTH, axis=0, tiled=True)
        qkv_group = jnp.concatenate(
            [
                rows_of(qkv_full[:query_width], group, group_query),
                rows_of(qkv_full[query_width : query_width + pair_width], pair_index, HD),
                rows_of(qkv_full[query_width + pair_width :], pair_index, HD),
            ]
        )
    freight.need(mul(qkv_group, first_full, NT), keep("projected"))
    hop = next(gather)
    out_group = straight(held["out"])
    if not by_block:
        out_group = straight(straighten(out_group, "fsdp"))
    out_group = out_group.reshape(fsdp * out_weight.shape[0], -1)
    held["projected"], out_group = lax.optimization_barrier((held["projected"], out_group))
    turned, pair_rows, attended, log_totals = attend(
        places_at, held["projected"], bias_group[:, None], sink_part, cosine, sine, group_heads
    )

    freight.need(hop, gather.send)
    freight.chain(routes, xor_steps("seq"), keep("routes"))
    biases = jnp.concatenate([gate_up_bias, down_bias], axis=1)
    freight.chain(biases, xor_steps("fsdp"), keep("biases"))
    branch = ring_reduce(
        lambda index: mul(columns_of(attended, index, tokens), out_group, TN), ids, freight
    )
    middle = inputs + (branch + out_bias)
    second_normed, second_factor = rms_scale(middle, norm2_gain)
    second_low = second_normed.astype(LOW)

    second_full, last = ring_gather(second_low, ids, freight)
    freight.need(last[0], lambda values: None)
    next(gather)
    freight.settle()
    joined_weight, down_full = held["gate_up"], held["down"]
    all_routes = straighten(held["routes"], "seq").reshape(length, TOPK)
    biases = straighten(held["biases"], "fsdp")
    joined_bias = biases[:, : gate_up_bias.shape[1]].reshape(-1).astype(WIDE)
    down_shift = biases[:, gate_up_bias.shape[1] :].reshape(-1).astype(WIDE)
    mine = jnp.any(all_routes == position, axis=1)
    counted = mine.astype(jnp.int32)
    earlier = jnp.cumsum(counted) - counted
    places = jnp.where(mine, earlier, -1)
    slots_here = jnp.arange(slot_count, dtype=jnp.int32)
    into = slots_here[:, None] == places[None, :]
    back_to = places[:, None] == slots_here[None, :]
    into_low, back_low = into.astype(LOW), back_to.astype(LOW)
    mixing_all = mixing_of(second_full, all_routes, router_weight, router_bias)
    expert_ids = jnp.arange(groups, dtype=jnp.int32)
    mixing_mine = jnp.sum(jnp.where(expert_ids == position, mixing_all, 0.0), axis=1)
    mixing_rows = jnp.sum(jnp.where(into, mixing_mine[None, :], 0.0), axis=1)[:, None]
    expert_rows = mul(into_low, second_full).astype(LOW)
    joined = mul(expert_rows, joined_weight) + joined_bias
    activated = lax.optimization_barrier(clamped_glu(joined, expert_width).astype(LOW))
    expert_columns = expert_rows.T
    activated_rows = activated.T
    upstream_full = None
    for upstream_full in gather:
        pass
    upstream_full = upstream_full[0]
    freight.finish()
    freight = Freight()
    landed = {"down": [], "joined": []}
    down_rows = expert_width // fsdp
    joined_rows = hidden.shape[2] // fsdp

    def down_term(j, *others, final=False):
        return weight_term(activated_rows, rows_grad, part ^ j, down_rows, *others, final=final)

    def joined_term(j, *others, final=False):
        grad = held["joined_grad"]
        return weight_term(expert_columns, grad, part ^ j, joined_rows, *others, final=final)

    upstream_rows = mul(into_low, upstream_full)
    rows_grad = (upstream_rows * mixing_rows).astype(LOW)
    near = swap(down_term(3), "fsdp", 1)
    down_away = down_term(2, near)
    down_close = swap(down_term(1), "fsdp", 1)
    freight.load(down_away, [down_away.shape[0]], landed["down"].append, [1], [4])
    expert_out = (mul(activated, down_full) + down_shift).astype(LOW).astype(WIDE)
    weighted = (expert_out * mixing_rows).astype(LOW)
    mixing_grad_rows = jnp.sum(upstream_rows * expert_out, axis=1)

    def back_first(upstream):
        activated_grad = mul(upstream, down_full, NT)
        joined_grad = glu_back(joined, expert_width, activated_grad).astype(LOW)
        freight.need(joined_grad, back_second)

    def back_second(joined_grad):
        held["joined_grad"] = joined_grad
        near = swap(joined_term(3), "fsdp", 1)
        freight.need(joined_term(1), keep("joined_one"))
        freight.need(near, back_third)

    def back_third(near):
        held["joined_close"] = swap(held["joined_one"], "fsdp", 1)
        freight.need(held["joined_grad"], keep("joined_grad"))
        freight.need(joined_term(2, near), back_fourth)

    def back_fourth(away):
        sizes = spread(away.shape[0], [1, 1, 1])
        freight.load(away, sizes, landed["joined"].append, [1, 4, 7], [3, 3, 3])
        rows = mul(held["joined_grad"], joined_weight, NT).astype(LOW)
        held["input_rows_grad"] = rows

    freight.need(rows_grad, back_first)
    combined = ring_reduce(lambda index: mul(rows_of(back_low, index, tokens), weighted), ids, freight)
    outputs = middle + combined
    mixing_grad = jnp.sum(jnp.where(back_to, mixing_grad_rows[None, :], 0.0), axis=1)
    mixing_grad = lax.all_to_all(
        mixing_grad.reshape(groups, tokens), "seq", split_axis=0, concat_axis=0, tiled=True
    ).T
    if "input_rows_grad" not in held:
        freight.settle()
    joined_grad, input_rows_grad = held["joined_grad"], held["input_rows_grad"]
    def down_last(close):
        freight.need(down_term(0, close, final=True), keep("down_keep"))

    def joined_last(close):
        freight.need(joined_term(0, close, final=True), keep("joined_keep"))

    freight.after(2, down_close, down_last)
    freight.after(5, held["joined_close"], joined_last)
    second_grad = ring_reduce(
        lambda index: mul(rows_of(back_low, index, tokens), input_rows_grad), ids, freight
    )
    mixing = mixing_of(second_low, routes[0], router_weight, router_bias)
    logits_grad = mixing * (
        mixing_grad - jnp.sum(mixing * mixing_grad, axis=-1, keepdims=True)
    )
    second_grad = second_grad + jnp.dot(
        logits_grad, router_weight.astype(WIDE).T, precision=PRECISE
    )
    upstream = out_grad[0].astype(WIDE)
    middle_part, gain2_grad = rms_back(middle, second_factor, norm2_gain, second_grad)
    middle_grad = upstream + middle_part
    branch_low = middle_grad.astype(LOW)

    width = hidden.shape[2]

    router_weight_grad = jnp.dot(second_low.astype(WIDE).T, logits_grad, precision=PRECISE)
    router_bias_grad = jnp.sum(logits_grad, axis=0)
    out_bias_grad = jnp.sum(branch_low.astype(WIDE), axis=0)
    early = [out_bias_grad, gain2_grad, router_weight_grad.T.reshape(-1), router_bias_grad]
    early = jnp.concatenate(early)
    branch_full, _ = ring_gather(branch_low, ids, freight)
    heads_grad = mul(out_group, branch_full, NT).astype(LOW)
    query_grad, pair_grad, sink_grad = attend_back(
        places_at, sink_part, turned, pair_rows, attended, heads_grad, log_totals, cosine, sine
    )
    projected_grad = jnp.concatenate([query_grad, pair_grad])
    bias_term = jnp.sum(projected_grad.astype(WIDE), axis=1)
    if planned:
        projected_grad = jnp.take(
            projected_grad.reshape(fsdp * rounds, unit, -1),
            jnp.asarray(back)[device],
            axis=0,
            mode="clip",
        ).reshape(projected_grad.shape)

    bias_full = jnp.zeros((query_width + 2 * pair_width,), WIDE)
    bias_full = lax.dynamic_update_slice(
        bias_full, bias_term[:group_query], (bias_at[0] * group_query,)
    )
    bias_full = lax.dynamic_update_slice(
        bias_full, bias_term[group_query : group_query + HD], (query_width + bias_at[1] * HD,)
    )
    bias_full = lax.dynamic_update_slice(
        bias_full,
        bias_term[group_query + HD :],
        (query_width + pair_width + bias_at[2] * HD,),
    )
    sink_full = lax.dynamic_update_slice_in_dim(
        jnp.zeros((head_count,), WIDE), sink_grad[:, 0, 0], group * group_heads, 0
    )

    def out_first(grad):
        terms = straight(mul(attended, grad).astype(LOW)).reshape(fsdp, out_weight.shape[0], -1)
        if not by_block:
            terms = straight(straighten(terms, "fsdp"))

        def use(total):
            back = [(b, a) for a, b in out_moves]
            freight.need(send(total.astype(LOW), BOTH, back), keep("out_shard"))

        freight.blocks(terms, use)

    def qkv_first(grad):
        terms = mul(grad, first_full)
        low = straight(terms.astype(LOW))
        sums = jnp.sum(low.astype(WIDE) * qkv_group.astype(WIDE), axis=0) / norm1_gain
        values = jnp.concatenate([sums, bias_full, sink_full, early])
        for step in sum_steps(BOTH):
            values = step(values)
        held["late"] = values
        if not planned:
            held["qkv_term"] = terms
            return

        def use(total):
            total = total.astype(LOW)
            returned = [
                send(total[i], BOTH, [(b, a) for a, b in pairs[i]]) for i in range(rounds)
            ]
            freight.need(straight(jnp.stack(returned)), keep("returned"))

        freight.blocks(low.reshape(fsdp, rounds, unit, -1), use)

    freight.need(projected_grad, qkv_first)
    freight.need(branch_full, out_first)
    first_grad = ring_reduce(
        lambda index: mul(columns_of(projected_grad, index, tokens), qkv_group, TN), ids, freight
    )
    freight.finish()
    down_shard, bias_sums = add_pieces(held["down_keep"], landed["down"])
    down_bias_shard = rows_of(bias_sums, part, down_bias.shape[1])
    joined_shard, bias_sums = add_pieces(held["joined_keep"], landed["joined"])
    joined_bias_shard = rows_of(bias_sums, part, gate_up_bias.shape[1])
    out_shard = held["out_shard"].astype(WIDE)
    if planned:
        qkv_shard = jnp.take(held["returned"], jnp.asarray(home)[:, device], axis=0, mode="clip")
        qkv_shard = qkv_shard.reshape(rounds * unit, -1).T.astype(WIDE)
    else:
        qkv_term = held["qkv_term"]
        scattered = jnp.zeros((query_width + 2 * pair_width, width), WIDE)
        for start, stop, row in (
            (0, group_query, group * group_query),
            (group_query, group_query + HD, query_width + pair_index * HD),
            (group_query + HD, group_query + 2 * HD, query_width + pair_width + pair_index * HD),
        ):
            scattered = lax.dynamic_update_slice(scattered, qkv_term[start:stop], (row, 0))
        qkv_shard = lax.psum_scatter(scattered, BOTH, scatter_dimension=0, tiled=True).T
    input_part, _ = rms_back(inputs, first_factor, norm1_gain, first_grad)
    input_grad = middle_grad + input_part

    late = held["late"]
    early = late[width + qkv_bias.shape[0] + head_count :]
    router_sums = early[2 * width : 2 * width + width * groups].reshape(groups, width).T
    return (
        outputs.astype(LOW)[None],
        input_grad.astype(LOW)[None],
        late[:width],
        qkv_shard,
        late[width : width + qkv_bias.shape[0]],
        late[width + qkv_bias.shape[0] : width + qkv_bias.shape[0] + head_count],
        out_shard,
        early[:width],
        early[width : 2 * width],
        router_sums,
        early[2 * width + width * groups : 2 * width + (width + 1) * groups],
        joined_shard[None],
        joined_bias_shard[None],
        down_shard[None],
        down_bias_shard[None],
    )


def solution(mesh):
    tokens = P("fsdp", "seq", None)
    by_expert = P("seq", "fsdp", None)
    return jax.shard_map(
        body,
        mesh=mesh,
        in_specs=(
            tokens, tokens, tokens, P(), P(None, BOTH), P(), P(), P(BOTH, None), P(), P(), P(), P(),
            by_expert, P("seq", "fsdp"), by_expert, P("seq", "fsdp"),
        ),
        out_specs=(
            tokens, tokens, P(), P(None, BOTH), P(), P(), P(BOTH, None), P(), P(), P(), P(),
            by_expert, P("seq", "fsdp"), by_expert, P("seq", "fsdp"),
        ),
        check_vma=False,
    )
```

time: 2970 us -> 1060 us (0.36)
  waiting for transfers between devices: 1590 us -> 363 us
  blocking collectives: 836 us -> 0 us
  Pallas kernels: 0 us -> 124 us
  matrix products: 338 us -> 215 us
  starting transfers between devices: 57 us -> 125 us
  local copies, waits for them, and re-layouts: 66 us -> 124 us
    reduce_scatter x2 -> x0, waiting for transfers between devices: 899 us -> none  [the longest x1 899 us: body(): lax.psum_scatter(qkv_term, ('fsdp', 'seq'), scatter_dimension=1, tiled=True)]
    reduce_scatter x1 -> x0, blocking collectives: 745 us -> none  [body(): lax.psum_scatter(joined_term[None], 'fsdp', scatter_dimension=1, tiled=True)]
    all_gather x4 -> x2, waiting for transfers between devices: 389 us -> 3.33 us  [use(): held[name] = lax.all_gather(shard, 'fsdp', axis=0, tiled=True)]
    ppermute x0 -> x102, waiting for transfers between devices: none -> 359 us  [the longest x86 337 us: send(): return straight(lax.ppermute(blocks, axis, pairs)).reshape(values.shape)]
    all_to_all x9 -> x1, waiting for transfers between devices: 294 us -> 0.01 us  [body(): lax.all_to_all(mixing_grad.reshape(groups, tokens), 'seq', split_axis=0,...]
    pallas_call x0 -> x14, Pallas kernels: none -> 124 us  [the longest x8 77.7 us: weight_term(): pl.pallas_call(functools.partial(term_kernel, others=len(others)), grid_s...]
    dot_general x30 -> x46, matrix products: 338 us -> 215 us  [the longest x44 210 us: mul(): return lax.dot_general(left, right, dims, preferred_element_type=WIDE)]
    ppermute x0 -> x102, starting transfers between devices: none -> 119 us  [the longest x86 108 us: send(): return straight(lax.ppermute(blocks, axis, pairs)).reshape(values.shape)]
  transfers between devices with their start and end apart: 19 -> 105, of which waited for: 12 -> 48; matrix products, arithmetic and copies ran while one was open for 14% -> 33% of each run, Pallas kernels for 0% -> 9%
where the time goes in v1:
time: 1060 us; the launch traced here: 1050 us
  waiting for transfers between devices  363 us (34%)
  matrix products  215 us (20%)
  starting transfers between devices  125 us (12%)
  local copies, waits for them, and re-layouts  124 us (12%)
  Pallas kernels  124 us (12%)
  other arithmetic  64.3 us (6%)
  between operations  33.3 us (3%)
    ppermute x86, waiting for transfers between devices, send(): return straight(lax.ppermute(blocks, axis, pairs)).reshape(values.shape)  337 us
    dot_general x44, matrix products, mul(): return lax.dot_general(left, right, dims, preferred_element_type=WIDE)  210 us
    ppermute x86, starting transfers between devices, send(): return straight(lax.ppermute(blocks, axis, pairs)).reshape(values.shape)  108 us
    pallas_call x8, Pallas kernels, weight_term(): pl.pallas_call(functools.partial(term_kernel, others=len(others)), grid_s...  77.7 us
    unnamed x253, local copies, waits for them, and re-layouts  36 us
    dynamic_update_slice x34, local copies, waits for them, and re-layouts, put(): lax.dynamic_update_slice(full, part, (index * tokens + offset, 0))  31.9 us
    pallas_call x1, Pallas kernels, attend(): pl.pallas_call(functools.partial(forward_kernel, block=block, scale=HD **...  24.7 us
    pallas_call x1, Pallas kernels, attend_back(): pl.pallas_call(functools.partial(backward_kernel, block=block, scale=HD *...  21.9 us
  transfers between devices with their start and end apart: 105, of which 48 were waited for; matrix products, arithmetic and copies ran while one was open for 33% of the time, Pallas kernels for 9%

profile of v1, /device:TPU:24, one launch (start us, length us, event | category | flops | bytes accessed | tf_op | source)
XLA Modules:
  0.0 1048.1 jit_solution(8530688334723759424)
XLA Ops:
  51.0 23.1 %collective-permute-done.5 = bf16[8,16,2880]{2,1,0:T(8,128)(2,1)} collective-permute-done((bf16[8,16,2880]{2,1,0:T(8,128)(2,1)S(1)}, bf16[8,16,2880]{2,1,0:T(8,128)(2,1)}, u32[]{:S(2)}, u32[]{:S(2)}) %collective-permute-start.5) | collective-permute-done | bytes 737312 | tf_op jit(solution)/shard_map/ppermute | solution.py:68
  84.2 17.4 %collective-permute-done.9 = bf16[8,16,2880]{2,1,0:T(8,128)(2,1)S(1)} collective-permute-done((bf16[8,16,2880]{2,1,0:T(8,128)(2,1)}, bf16[8,16,2880]{2,1,0:T(8,128)(2,1)S(1)}, u32[]{:S(2)}, u32[]{:S(2)}) %collective-permute-start.9) | collective-permute-done | bytes 737312 | tf_op jit(solution)/shard_map/ppermute | solution.py:68
  104.9 15.1 %collective-permute-done.12 = bf16[8,16,2880]{2,1,0:T(8,128)(2,1)S(1)} collective-permute-done((bf16[8,16,2880]{2,1,0:T(8,128)(2,1)S(1)}, bf16[8,16,2880]{2,1,0:T(8,128)(2,1)S(1)}, u32[]{:S(2)}, u32[]{:S(2)}) %collective-permute-start.12) | collective-permute-done | bytes 737312 | tf_op jit(solution)/shard_map/ppermute | solution.py:68
  171.8 12.5 %collective-permute-done.18 = bf16[8,16,2880]{2,1,0:T(8,128)(2,1)S(1)} collective-permute-done((bf16[8,16,2880]{2,1,0:T(8,128)(2,1)}, bf16[8,16,2880]{2,1,0:T(8,128)(2,1)S(1)}, u32[]{:S(2)}, u32[]{:S(2)}) %collective-permute-start.18) | collective-permute-done | bytes 737312 | tf_op jit(solution)/shard_map/ppermute | solution.py:68
  187.1 24.7 %attend.1 = (bf16[512,1024]{1,0:T(8,128)(2,1)S(1)}, bf16[128,1024]{1,0:T(8,128)(2,1)S(1)}, bf16[512,1024]{1,0:T(8,128)(2,1)S(1)}, f32[8,1,1024]{2,1,0:T(1,128)S(1)}) custom-call(s32[28]{0:T(128)S(1)} %pad_add_fusion.2.at_ref, f32[8]{0:T(128)S(1)} %dynamic_slice.138.sink_ref, ...), custom_call_target="tpu_custom_call" | custom-call | tf_op jit(solution)/shard_map/attend/pallas_call | solution.py:440
  236.6 12.7 %collective-permute-done.26 = bf16[8,16,2880]{2,1,0:T(8,128)(2,1)} collective-permute-done((bf16[8,16,2880]{2,1,0:T(8,128)(2,1)S(1)}, bf16[8,16,2880]{2,1,0:T(8,128)(2,1)}, u32[]{:S(2)}, u32[]{:S(2)}) %collective-permute-start.26) | collective-permute-done | bytes 737312 | tf_op jit(solution)/shard_map/ppermute | solution.py:68
  259.1 11.6 %collective-permute-done.31 = bf16[8,16,2880]{2,1,0:T(8,128)(2,1)S(1)} collective-permute-done((bf16[8,16,2880]{2,1,0:T(8,128)(2,1)S(1)}, bf16[8,16,2880]{2,1,0:T(8,128)(2,1)S(1)}, u32[]{:S(2)}, u32[]{:S(2)}) %collective-permute-start.31) | collective-permute-done | bytes 737312 | tf_op jit(solution)/shard_map/ppermute | solution.py:68
  286.1 11.0 %collective-permute-done.32 = bf16[8,16,2880]{2,1,0:T(8,128)(2,1)S(1)} collective-permute-done((bf16[8,16,2880]{2,1,0:T(8,128)(2,1)}, bf16[8,16,2880]{2,1,0:T(8,128)(2,1)S(1)}, u32[]{:S(2)}, u32[]{:S(2)}) %collective-permute-start.32) | collective-permute-done | bytes 737312 | tf_op jit(solution)/shard_map/ppermute | solution.py:68
  309.5 14.3 %collective-permute-done.34 = bf16[8,16,2880]{2,1,0:T(8,128)(2,1)} collective-permute-done((bf16[8,16,2880]{2,1,0:T(8,128)(2,1)S(1)}, bf16[8,16,2880]{2,1,0:T(8,128)(2,1)}, u32[]{:S(2)}, u32[]{:S(2)}) %collective-permute-start.34) | collective-permute-done | bytes 737312 | tf_op jit(solution)/shard_map/ppermute | solution.py:68
  328.1 12.9 %collective-permute-done.36 = bf16[8,16,2880]{2,1,0:T(8,128)(2,1)S(1)} collective-permute-done((bf16[8,16,2880]{2,1,0:T(8,128)(2,1)}, bf16[8,16,2880]{2,1,0:T(8,128)(2,1)S(1)}, u32[]{:S(2)}, u32[]{:S(2)}) %collective-permute-start.36) | collective-permute-done | bytes 737312 | tf_op jit(solution)/shard_map/ppermute | solution.py:68
  394.2 27.7 %convolution_add_fusion = f32[576,5760]{1,0:T(8,128)S(1)} fusion(bf16[576,2880]{0,1:T(8,128)(2,1)} %convolution_convert_fusion.1, bf16[2880,5760]{1,0:T(8,128)(2,1)} %all-gather.3.cloned.1.call-done, f32[5760]{0:T(1024)S(1)} %reshape.898), kind=kOutput, calls=%fused_computation.2 | convolution fusion | flops 19113615360 | bytes 49789440 | tf_op jit(solution)/shard_map/dot_general | solution.py:31
  434.1 15.2 %add_convert_fusion = bf16[576,2880]{1,0:T(8,128)(2,1)S(1)} fusion(bf16[576,2880]{1,0:T(8,128)(2,1)S(1)} %multiply_convert_fusion.1, bf16[2880,2880]{1,0:T(8,128)(2,1)} %all-gather.5.cloned.1.call-done, f32[2880]{0:T(1024)S(1)} %reshape.899), kind=kOutput, calls=%fused_computation.13 | convolution fusion | flops 9558466560 | bytes 23235840 | tf_op jit(solution)/shard_map/dot_general | solution.py:31
  483.9 22.6 %select_convert_fusion.1 = (bf16[576,2880]{1,0:T(8,128)(2,1)}, bf16[576,2880]{1,0:T(8,128)(2,1)}) fusion(f32[576,5760]{1,0:T(8,128)} %copy-done.57, bf16[576,2880]{1,0:T(8,128)(2,1)S(1)} %get-tuple-element.189.right_ref, bf16[2880,2880]{1,0:T(8,128)(2,1)} %all-gather.5.cloned.1.call-done), kind=kOutput, calls=%fused_computation.11 | convolution fusion | flops 9591644160 | bytes 39813120 | tf_op jit(solution)/shard_map/dot_general | solution.py:31
  518.7 11.0 %weight_term.11 = bf16[736,5760]{1,0:T(8,128)(2,1)} custom-call(s32[1]{0:T(128)} %bitcast.119.at_ref, bf16[2880,576]{1,0:T(8,128)(2,1)S(1)} %bitcast.439, bf16[576,5760]{1,0:T(8,128)(2,1)S(1)} %pad_maximum_fusion.right_ref), custom_call_target="tpu_custom_call" | custom-call | flops 4777574400 | bytes 24053760 | tf_op jit(solution)/shard_map/weight_term/pallas_call | solution.py:625
  563.2 11.8 %weight_term.12 = bf16[736,5760]{1,0:T(8,128)(2,1)S(1)} custom-call(s32[1]{0:T(128)} %bitcast.107.at_ref, bf16[2880,576]{1,0:T(8,128)(2,1)S(1)} %bitcast.441, bf16[576,5760]{1,0:T(8,128)(2,1)S(1)} %bitcast.436, bf16[736,5760]{1,0:T(8,128)(2,1)} %bitcast.133.refs_0_), custom_call_target="tpu_custom_call" | custom-call | flops 4777574400 | bytes 32348160 | tf_op jit(solution)/shard_map/weight_term/pallas_call | solution.py:625
  582.9 26.3 %convolution_convert_fusion.2 = bf16[576,2880]{1,0:T(8,128)(2,1)} fusion(bf16[576,5760]{1,0:T(8,128)(2,1)S(1)} %bitcast.436, bf16[2880,5760]{1,0:T(8,128)(2,1)} %all-gather.3.cloned.1.call-done), kind=kOutput, calls=%fused_computation.26 | convolution fusion | flops 19111956480 | bytes 43130880 | tf_op jit(solution)/shard_map/dot_general | solution.py:31
  621.1 36.8 %collective-permute-done.59 = bf16[46,16,2880]{2,1,0:T(8,128)(2,1)} collective-permute-done((bf16[46,16,2880]{2,1,0:T(8,128)(2,1)}, bf16[46,16,2880]{2,1,0:T(8,128)(2,1)}, u32[]{:S(2)}, u32[]{:S(2)}) %collective-permute-start.59) | collective-permute-done | bytes 4239392 | tf_op jit(solution)/shard_map/ppermute | solution.py:68
  760.7 15.2 %weight_term.15 = (f32[720,5760]{1,0:T(8,128)}, f32[16,5760]{1,0:T(8,128)S(1)}) custom-call(s32[1]{0:T(128)} %bitcast.157.at_ref, bf16[2880,576]{1,0:T(8,128)(2,1)S(1)} %bitcast.442, bf16[576,5760]{1,0:T(8,128)(2,1)S(1)} %bitcast.438, bf16[736,5760]{1,0:T(8,128)(2,1)} %bitcast.146.refs_0_), custom_call_target="tpu_custom_call" | custom-call | flops 4777574400 | bytes 32348160 | tf_op jit(solution)/shard_map/weight_term/pallas_call | solution.py:625
  791.3 19.0 %collective-permute-done.73 = bf16[16,16,5760]{2,1,0:T(8,128)(2,1)S(1)} collective-permute-done((bf16[16,16,5760]{2,1,0:T(8,128)(2,1)}, bf16[16,16,5760]{2,1,0:T(8,128)(2,1)S(1)}, u32[]{:S(2)}, u32[]{:S(2)}) %collective-permute-start.73) | collective-permute-done | bytes 2949152 | tf_op jit(solution)/shard_map/ppermute | solution.py:68
  813.5 13.7 %collective-permute-done.74 = bf16[8,16,2880]{2,1,0:T(8,128)(2,1)S(1)} collective-permute-done((bf16[8,16,2880]{2,1,0:T(8,128)(2,1)S(1)}, bf16[8,16,2880]{2,1,0:T(8,128)(2,1)S(1)}, u32[]{:S(2)}, u32[]{:S(2)}) %collective-permute-start.74) | collective-permute-done | bytes 737312 | tf_op jit(solution)/shard_map/ppermute | solution.py:68
  839.3 21.9 %attend_back.1 = (bf16[512,1024]{1,0:T(8,128)(2,1)S(1)}, bf16[128,1024]{1,0:T(8,128)(2,1)S(1)}, f32[8,1,128]{2,1,0:T(1,128)S(1)}) custom-call(s32[28]{0:T(128)S(1)} %copy-done.31, f32[8]{0:T(128)S(1)} %copy-done.29, bf16[512,1024]{1,0:T(8,128)(2,1)S(1)} %copy-done.25, bf16[128,1024]{1,0:T(8,128)(2,1)S(1)} %copy-done.27, bf16[512,1024]{1,0:T(8,128)(2,1)S(1)} %copy-done.19, ...), custom_call_target="tpu_custom_call" | custom-call | tf_op jit(solution)/shard_map/attend_back/pallas_call | solution.py:557
  934.8 11.0 %collective-permute-done.83 = bf16[8,16,2880]{2,1,0:T(8,128)(2,1)S(1)} collective-permute-done((bf16[8,16,2880]{2,1,0:T(8,128)(2,1)}, bf16[8,16,2880]{2,1,0:T(8,128)(2,1)S(1)}, u32[]{:S(2)}, u32[]{:S(2)}) %collective-permute-start.83) | collective-permute-done | bytes 737312 | tf_op jit(solution)/shard_map/ppermute | solution.py:68
  981.7 20.4 %collective-permute-done.96 = bf16[2,16,2880]{2,1,0:T(8,128)(2,1)S(1)} collective-permute-done((bf16[2,16,2880]{2,1,0:T(8,128)(2,1)S(1)}, bf16[2,16,2880]{2,1,0:T(8,128)(2,1)S(1)}, u32[]{:S(2)}, u32[]{:S(2)}) %collective-permute-start.96) | collective-permute-done | bytes 184352 | tf_op jit(solution)/shard_map/ppermute | solution.py:68
  1007.7 16.8 %collective-permute-done.100 = bf16[2,16,2880]{2,1,0:T(8,128)(2,1)S(1)} collective-permute-done((bf16[2,16,2880]{2,1,0:T(8,128)(2,1)S(1)}, bf16[2,16,2880]{2,1,0:T(8,128)(2,1)S(1)}, u32[]{:S(2)}, u32[]{:S(2)}) %collective-permute-start.100) | collective-permute-done | bytes 184352 | tf_op jit(solution)/shard_map/ppermute | solution.py:68
  (697 shorter events, 590.1 us)
Async XLA Ops:
  7.2 387.0 %all-gather.3.cloned.1.call-start = ((), (), s32[]{:S(2)}) async-start(), calls=%async_computation.1 | async-start | bytes 41472000 | tf_op jit(solution)/shard_map/all_gather | solution.py:802
  43.6 38.2 %collective-permute-start.8 = (bf16[5,32,2880]{2,1,0:T(8,128)(2,1)S(1)}, bf16[5,32,2880]{2,1,0:T(8,128)(2,1)S(1)}, u32[]{:S(2)}, u32[]{:S(2)}) collective-permute-start(bf16[5,32,2880]{2,1,0:T(8,128)(2,1)S(1)} %bitcast_dynamic-update-slice_fusion.5), channel_id=1, source_target_pairs={{0,16},{8,24},{16,0},{24,8},{1,17},{9,25},{17,1},{25,9},{2,18},{10... | collective-permute-start | bytes 2764808 | tf_op jit(solution)/shard_map/ppermute | solution.py:69
  44.2 29.9 %collective-permute-start.5 = (bf16[8,16,2880]{2,1,0:T(8,128)(2,1)S(1)}, bf16[8,16,2880]{2,1,0:T(8,128)(2,1)}, u32[]{:S(2)}, u32[]{:S(2)}) collective-permute-start(bf16[8,16,2880]{2,1,0:T(8,128)(2,1)S(1)} %bitcast.515), channel_id=1, source_target_pairs={{0,2},{2,4},{4,6},{6,7},{7,5},{5,3},{3,1},{1,0},{8,10},{10,12},{12... | collective-permute-start | bytes 2211848 | tf_op jit(solution)/shard_map/ppermute | solution.py:68
  50.5 31.3 %collective-permute-start.7 = (bf16[8,16,2880]{2,1,0:T(8,128)(2,1)}, bf16[8,16,2880]{2,1,0:T(8,128)(2,1)S(1)}, u32[]{:S(2)}, u32[]{:S(2)}) collective-permute-start(bf16[8,16,2880]{2,1,0:T(8,128)(2,1)} %bitcast.525), channel_id=1, source_target_pairs={{0,1},{1,25},{2,9},{3,17},{4,20},{5,28},{6,4},{7,12},{8,14},{9,22}... | collective-permute-start | bytes 2211848 | tf_op jit(solution)/shard_map/ppermute | solution.py:68
  122.6 311.5 %all-gather.5.cloned.1.call-start = ((), (), s32[]{:S(2)}) async-start(), calls=%async_computation.2 | async-start | bytes 21196800 | tf_op jit(solution)/shard_map/all_gather | solution.py:802
  184.9 29.6 %collective-permute-start.20 = (bf16[8,16,2880]{2,1,0:T(8,128)(2,1)S(1)}, bf16[8,16,2880]{2,1,0:T(8,128)(2,1)}, u32[]{:S(2)}, u32[]{:S(2)}) collective-permute-start(bf16[8,16,2880]{2,1,0:T(8,128)(2,1)S(1)} %collective-permute-done.18), channel_id=1, source_target_pairs={{0,2},{2,4},{4,6},{6,7},{7,5},{5,3},{3,1},{1,0},{8,10},{10,12},{12... | collective-permute-start | bytes 2211848 | tf_op jit(solution)/shard_map/ppermute | solution.py:68
  483.4 33.1 %collective-permute-start.49 = (bf16[4,16,2880]{2,1,0:T(8,128)(2,1)}, bf16[4,16,2880]{2,1,0:T(8,128)(2,1)}, u32[]{:S(2)}, u32[]{:S(2)}) collective-permute-start(bf16[4,16,2880]{2,1,0:T(8,128)(2,1)} %bitcast.124), channel_id=1, source_target_pairs={{2,0},{4,2},{6,4},{7,6},{5,7},{3,5},{1,3},{0,1},{10,8},{12,10},{14... | collective-permute-start | bytes 1105928 | tf_op jit(solution)/shard_map/ppermute | solution.py:68
  554.7 103.2 %collective-permute-start.58 = (bf16[46,16,5760]{2,1,0:T(8,128)(2,1)}, bf16[46,16,5760]{2,1,0:T(8,128)(2,1)}, u32[]{:S(2)}, u32[]{:S(2)}) collective-permute-start(bf16[46,16,5760]{2,1,0:T(8,128)(2,1)} %bitcast.443), channel_id=1, source_target_pairs={{0,8},{8,0},{16,24},{24,16},{1,9},{9,1},{17,25},{25,17},{2,10},{10... | collective-permute-start | bytes 25436168 | tf_op jit(solution)/shard_map/ppermute | solution.py:68
  561.6 59.5 %collective-permute-start.57 = (bf16[46,16,2880]{2,1,0:T(8,128)(2,1)}, bf16[46,16,2880]{2,1,0:T(8,128)(2,1)}, u32[]{:S(2)}, u32[]{:S(2)}) collective-permute-start(bf16[46,16,2880]{2,1,0:T(8,128)(2,1)} %bitcast.143), channel_id=1, source_target_pairs={{0,8},{8,0},{16,24},{24,16},{1,9},{9,1},{17,25},{25,17},{2,10},{10... | collective-permute-start | bytes 12718088 | tf_op jit(solution)/shard_map/ppermute | solution.py:68
  562.1 95.9 %collective-permute-start.59 = (bf16[46,16,2880]{2,1,0:T(8,128)(2,1)}, bf16[46,16,2880]{2,1,0:T(8,128)(2,1)}, u32[]{:S(2)}, u32[]{:S(2)}) collective-permute-start(bf16[46,16,2880]{2,1,0:T(8,128)(2,1)} %bitcast.444), channel_id=1, source_target_pairs={{0,16},{8,24},{16,0},{24,8},{1,17},{9,25},{17,1},{25,9},{2,18},{10... | collective-permute-start | bytes 12718088 | tf_op jit(solution)/shard_map/ppermute | solution.py:68
  675.7 60.8 %collective-permute-start.66 = (bf16[15,16,5760]{2,1,0:T(8,128)(2,1)}, bf16[15,16,5760]{2,1,0:T(8,128)(2,1)}, u32[]{:S(2)}, u32[]{:S(2)}) collective-permute-start(bf16[15,16,5760]{2,1,0:T(8,128)(2,1)} %bitcast.500), channel_id=1, source_target_pairs={{0,16},{8,24},{16,0},{24,8},{1,17},{9,25},{17,1},{25,9},{2,18},{10... | collective-permute-start | bytes 8294408 | tf_op jit(solution)/shard_map/ppermute | solution.py:68
  680.5 32.1 %collective-permute-start.56 = (bf16[8,16,2880]{2,1,0:T(8,128)(2,1)}, bf16[8,16,2880]{2,1,0:T(8,128)(2,1)S(1)}, u32[]{:S(2)}, u32[]{:S(2)}) collective-permute-start(bf16[8,16,2880]{2,1,0:T(8,128)(2,1)} %bitcast.511), channel_id=1, source_target_pairs={{2,0},{4,2},{6,4},{7,6},{5,7},{3,5},{1,3},{0,1},{10,8},{12,10},{14... | collective-permute-start | bytes 2211848 | tf_op jit(solution)/shard_map/ppermute | solution.py:68
  681.1 31.6 %collective-permute-start.55 = (bf16[8,16,2880]{2,1,0:T(8,128)(2,1)}, bf16[8,16,2880]{2,1,0:T(8,128)(2,1)S(1)}, u32[]{:S(2)}, u32[]{:S(2)}) collective-permute-start(bf16[8,16,2880]{2,1,0:T(8,128)(2,1)} %bitcast.510), channel_id=1, source_target_pairs={{0,2},{2,4},{4,6},{6,7},{7,5},{5,3},{3,1},{1,0},{8,10},{10,12},{12... | collective-permute-start | bytes 2211848 | tf_op jit(solution)/shard_map/ppermute | solution.py:68
  747.3 63.1 %collective-permute-start.73 = (bf16[16,16,5760]{2,1,0:T(8,128)(2,1)}, bf16[16,16,5760]{2,1,0:T(8,128)(2,1)S(1)}, u32[]{:S(2)}, u32[]{:S(2)}) collective-permute-start(bf16[16,16,5760]{2,1,0:T(8,128)(2,1)} %bitcast.499), channel_id=1, source_target_pairs={{0,16},{8,24},{16,0},{24,8},{1,17},{9,25},{17,1},{25,9},{2,18},{10... | collective-permute-start | bytes 8847368 | tf_op jit(solution)/shard_map/ppermute | solution.py:68
  812.8 114.7 %collective-permute-start.82 = (bf16[15,16,5760]{2,1,0:T(8,128)(2,1)}, bf16[15,16,5760]{2,1,0:T(8,128)(2,1)}, u32[]{:S(2)}, u32[]{:S(2)}) collective-permute-start(bf16[15,16,5760]{2,1,0:T(8,128)(2,1)} %bitcast.204), channel_id=1, source_target_pairs={{0,16},{8,24},{16,0},{24,8},{1,17},{9,25},{17,1},{25,9},{2,18},{10... | collective-permute-start | bytes 8294408 | tf_op jit(solution)/shard_map/ppermute | solution.py:68
  867.2 39.1 %collective-permute-start.78 = (bf16[4,16,2880]{2,1,0:T(8,128)(2,1)}, bf16[4,16,2880]{2,1,0:T(8,128)(2,1)}, u32[]{:S(2)}, u32[]{:S(2)}) collective-permute-start(bf16[4,16,2880]{2,1,0:T(8,128)(2,1)} %bitcast.196), channel_id=1, source_target_pairs={{0,2},{2,4},{4,6},{6,7},{7,5},{5,3},{3,1},{1,0},{8,10},{10,12},{12... | collective-permute-start | bytes 1105928 | tf_op jit(solution)/shard_map/ppermute | solution.py:68
  867.8 46.1 %collective-permute-start.79 = (bf16[4,16,2880]{2,1,0:T(8,128)(2,1)S(1)}, bf16[4,16,2880]{2,1,0:T(8,128)(2,1)}, u32[]{:S(2)}, u32[]{:S(2)}) collective-permute-start(bf16[4,16,2880]{2,1,0:T(8,128)(2,1)S(1)} %bitcast.541), channel_id=1, source_target_pairs={{2,0},{4,2},{6,4},{7,6},{5,7},{3,5},{1,3},{0,1},{10,8},{12,10},{14... | collective-permute-start | bytes 1105928 | tf_op jit(solution)/shard_map/ppermute | solution.py:68
  879.4 48.2 %collective-permute-start.80 = (bf16[2,5,32,2880]{3,2,1,0:T(8,128)(2,1)}, bf16[2,5,32,2880]{3,2,1,0:T(8,128)(2,1)}, u32[]{:S(2)}, u32[]{:S(2)}) collective-permute-start(bf16[2,5,32,2880]{3,2,1,0:T(8,128)(2,1)} %pad_maximum_fusion.4), channel_id=1, source_target_pairs={{0,8},{8,0},{16,24},{24,16},{1,9},{9,1},{17,25},{25,17},{2,10},{10... | collective-permute-start | bytes 5529608 | tf_op jit(solution)/shard_map/ppermute | solution.py:69
  931.4 37.6 %collective-permute-start.87 = (bf16[5,32,2880]{2,1,0:T(8,128)(2,1)S(1)}, bf16[5,32,2880]{2,1,0:T(8,128)(2,1)S(1)}, u32[]{:S(2)}, u32[]{:S(2)}) collective-permute-start(bf16[5,32,2880]{2,1,0:T(8,128)(2,1)S(1)} %fusion.7), channel_id=1, source_target_pairs={{0,16},{8,24},{16,0},{24,8},{1,17},{9,25},{17,1},{25,9},{2,18},{10... | collective-permute-start | bytes 2764808 | tf_op jit(solution)/shard_map/ppermute | solution.py:69
  933.3 35.7 %collective-permute-start.88 = (bf16[8,16,2880]{2,1,0:T(8,128)(2,1)S(1)}, bf16[8,16,2880]{2,1,0:T(8,128)(2,1)S(1)}, u32[]{:S(2)}, u32[]{:S(2)}) collective-permute-start(bf16[8,16,2880]{2,1,0:T(8,128)(2,1)S(1)} %bitcast.520), channel_id=1, source_target_pairs={{0,16},{8,24},{16,0},{24,8},{1,17},{9,25},{17,1},{25,9},{2,18},{10... | collective-permute-start | bytes 2211848 | tf_op jit(solution)/shard_map/ppermute | solution.py:68
  969.0 61.6 %collective-permute-start.90 = (bf16[8,16,2880]{2,1,0:T(8,128)(2,1)}, bf16[8,16,2880]{2,1,0:T(8,128)(2,1)}, u32[]{:S(2)}, u32[]{:S(2)}) collective-permute-start(bf16[8,16,2880]{2,1,0:T(8,128)(2,1)} %bitcast.221), channel_id=1, source_target_pairs={{2,0},{4,2},{6,4},{7,6},{5,7},{3,5},{1,3},{0,1},{10,8},{12,10},{14... | collective-permute-start | bytes 2211848 | tf_op jit(solution)/shard_map/ppermute | solution.py:68
  969.3 61.4 %collective-permute-start.89 = (bf16[8,16,2880]{2,1,0:T(8,128)(2,1)}, bf16[8,16,2880]{2,1,0:T(8,128)(2,1)}, u32[]{:S(2)}, u32[]{:S(2)}) collective-permute-start(bf16[8,16,2880]{2,1,0:T(8,128)(2,1)} %bitcast.219), channel_id=1, source_target_pairs={{0,2},{2,4},{4,6},{6,7},{7,5},{5,3},{3,1},{1,0},{8,10},{10,12},{12... | collective-permute-start | bytes 2211848 | tf_op jit(solution)/shard_map/ppermute | solution.py:68
  976.2 29.8 %collective-permute-start.98 = (bf16[2,16,2880]{2,1,0:T(8,128)(2,1)S(1)}, bf16[2,16,2880]{2,1,0:T(8,128)(2,1)S(1)}, u32[]{:S(2)}, u32[]{:S(2)}) collective-permute-start(bf16[2,16,2880]{2,1,0:T(8,128)(2,1)S(1)} %bitcast.560), channel_id=1, source_target_pairs={{17,0},{9,1},{1,2},{28,3},{4,4},{12,5},{22,6},{6,7},{14,8},{27,9},... | collective-permute-start | bytes 552968 | tf_op jit(solution)/shard_map/ppermute | solution.py:68
  1006.1 32.1 %collective-permute-start.101 = (bf16[8,16,2880]{2,1,0:T(8,128)(2,1)}, bf16[8,16,2880]{2,1,0:T(8,128)(2,1)}, u32[]{:S(2)}, u32[]{:S(2)}) collective-permute-start(bf16[8,16,2880]{2,1,0:T(8,128)(2,1)} %bitcast.240), channel_id=1, source_target_pairs={{1,0},{25,1},{9,2},{17,3},{20,4},{28,5},{4,6},{12,7},{14,8},{22,9}... | collective-permute-start | bytes 2211848 | tf_op jit(solution)/shard_map/ppermute | solution.py:68
  (201 other events, 3161.9 us)
Sparse Core Ops, SparseCore 0:
  122.8 200.3 all-gather.2
  324.7 109.4 all-gather.4

commit v2 on v1

--- a/solution.py
+++ b/solution.py
@@ -44,6 +44,68 @@
     )()
 
 
+def free():
+    return pl.CostEstimate(flops=0, bytes_accessed=0, transcendentals=0)
+
+
+def pick_kernel(*refs, count):
+    out = refs[-1]
+    for i in range(count):
+
+        @pl.when(pl.program_id(0) == i)
+        def _(i=i):
+            out[...] = refs[i][...].reshape(out.shape)
+
+
+def lay(*parts):
+    arrays, specs = [], []
+    for part in parts:
+        array, index = part if isinstance(part, tuple) else (part[None], 0)
+        arrays.append(array)
+        zeros = (0,) * (array.ndim - 1)
+        specs.append(
+            pl.BlockSpec((1, *array.shape[1:]), lambda n, at=(index, *zeros): at)
+        )
+    block = arrays[0].shape[1:]
+    zeros = (0,) * len(block)
+    return pl.pallas_call(
+        functools.partial(pick_kernel, count=len(parts)),
+        grid=(len(parts),),
+        in_specs=specs,
+        out_specs=pl.BlockSpec((1, *block), lambda n: (n, *zeros)),
+        out_shape=jax.ShapeDtypeStruct((len(parts), *block), arrays[0].dtype),
+        compiler_params=pltpu.CompilerParams(
+            dimension_semantics=("arbitrary",), vmem_limit_bytes=32 * 2**20
+        ),
+        cost_estimate=free(),
+        name="lay",
+    )(*arrays)
+
+
+def picked_kernel(at_ref, source_ref, out_ref):
+    out_ref[...] = source_ref[...]
+
+
+def picked(array, at):
+    block = (1, *array.shape[1:])
+    zeros = (0,) * (array.ndim - 1)
+    return pl.pallas_call(
+        picked_kernel,
+        grid_spec=pltpu.PrefetchScalarGridSpec(
+            num_scalar_prefetch=1,
+            grid=(at.shape[0],),
+            in_specs=[pl.BlockSpec(block, lambda n, at: (at[n], *zeros))],
+            out_specs=pl.BlockSpec(block, lambda n, at: (n, *zeros)),
+        ),
+        out_shape=jax.ShapeDtypeStruct((at.shape[0], *array.shape[1:]), array.dtype),
+        compiler_params=pltpu.CompilerParams(
+            dimension_semantics=("arbitrary",), vmem_limit_bytes=32 * 2**20
+        ),
+        cost_estimate=free(),
+        name="picked",
+    )(at, array)
+
+
 def ring_order(count):
     return list(range(0, count, 2)) + list(range(1, count, 2))[::-1]
 
@@ -75,68 +137,50 @@
 
 class Freight:
     def __init__(self):
-        self.hurried, self.flying, self.pending = [], [], []
-        self.now = 0
-
-    def load(self, values, sizes, land, when, lags, start=0):
-        for size, delay, lag in zip(sizes, when, lags):
-            piece = values[start : start + size]
-            start += size
-            self.after(delay, piece, functools.partial(self.hurry, land=land, lag=lag))
-
-    def hurry(self, values, land, lag=1):
-        self.hurried.append((values, land, lag))
+        self.pending, self.now = [], 0
+
+    def at(self, event, values, use):
+        self.pending.append((max(event, self.now + 1), values, use))
+
+    def after(self, events, values, use):
+        self.at(self.now + events, values, use)
 
     def need(self, values, use):
-        self.pending.append((values, use))
-
-    def __call__(self, *values):
-        self.now += 1
-        due = self.pending + [(array, use) for array, use, when in self.flying if when <= self.now]
-        self.flying = [flight for flight in self.flying if flight[2] > self.now]
-        self.pending = []
-        if due:
-            out = lax.optimization_barrier((*values, *(array for array, _ in due)))
-            values = out[: len(values)]
-            for array, (_, use) in zip(out[len(values) :], due):
-                use(array)
-        going, self.hurried = self.hurried, []
-        for fresh, use, lag in going:
-            self.flying.append((swap(fresh, "fsdp", 2), use, self.now + lag))
-        return values
-
-    def after(self, events, values, use):
-        if events == 0:
-            return use(values)
-        self.need(values, lambda held: self.after(events - 1, held, use))
+        self.after(1, values, use)
+
+    def carry(self, values, land, lag=1):
+        self.after(lag, swap(values, "fsdp", 2), land)
+
+    def blocks(self, terms, near_at, far_at, use):
+        part = lax.axis_index("fsdp")
+        terms = picked(terms, part ^ jnp.array([3, 1, 2, 0], jnp.int32))
+
+        def near_there(near):
+            away = straight((terms[2].astype(WIDE) + near[0].astype(WIDE)).astype(LOW))
+            own = terms[3].astype(WIDE) + near[1].astype(WIDE)
+            self.at(far_at, swap(away, "fsdp", 2), lambda far: use(own + far.astype(WIDE)))
+
+        self.at(near_at, swap(straight(terms[:2]), "fsdp", 1), near_there)
 
     def chain(self, values, steps, use):
         if not steps:
             return use(values)
         self.need(values, lambda held: self.chain(steps[0](held), steps[1:], use))
 
-    def blocks(self, terms, use):
-        def near_there(near):
-            away = straight((terms[2].astype(WIDE) + near[0].astype(WIDE)).astype(LOW))
-            own = terms[0].astype(WIDE) + near[1].astype(WIDE)
-            self.hurry(away, lambda far: use(own + far.astype(WIDE)), 2)
-
-        self.need(swap(straight(jnp.stack([terms[3], terms[1]])), "fsdp", 1), near_there)
-
-    def settle(self):
+    def __call__(self, *values):
+        self.now += 1
+        due = [(array, use) for event, array, use in self.pending if event <= self.now]
+        self.pending = [item for item in self.pending if item[0] > self.now]
+        out = lax.optimization_barrier((*values, *(array for array, _ in due)))
+        for array, (_, use) in zip(out[len(values) :], due):
+            use(array)
+        return out[: len(values)]
+
+    def finish(self):
         while self.pending:
             due, self.pending = self.pending, []
-            for array, use in due:
+            for _, array, use in due:
                 use(array)
-
-    def finish(self):
-        self.settle()
-        while self.flying or self.hurried:
-            self.flying += [(swap(fresh, "fsdp", 2), use, 0) for fresh, use, _ in self.hurried]
-            due, self.flying, self.hurried = self.flying, [], []
-            for array, use, _ in due:
-                use(array)
-            self.settle()
 
 
 def alone(*values):
@@ -233,23 +277,6 @@
         for axis in axes
         for i in range((lax.axis_size(axis) - 1).bit_length())
     ]
-
-
-def spread(total, parts):
-    ends = [round(total * sum(parts[: i + 1]) / sum(parts) / 16) * 16 for i in range(len(parts))]
-    ends[-1] = total
-    return [end - start for start, end in zip([0] + ends, ends)]
-
-
-def add_pieces(kept, pieces):
-    total, sums = kept
-    start = 0
-    for piece in pieces:
-        size = min(piece.shape[0], total.shape[0] - start)
-        rows = total[start : start + size] + piece[:size].astype(WIDE)
-        total = straight(lax.dynamic_update_slice(total, rows, (start, 0)))
-        start += size
-    return total, sums[0] + pieces[-1][-1].astype(WIDE)
 
 
 UNIT_PARTS = [
@@ -331,12 +358,12 @@
     order = np.zeros((total, count), np.int32)
     back = np.zeros((total, count), np.int32)
     for device in range(total):
-        part, group = divmod(device, groups)
-        for j in range(fsdp):
+        group = device % groups
+        for part in range(fsdp):
             for i in range(rounds):
-                place = place_at[i, (part ^ j) * groups + group]
-                order[device, place] = j * rounds + i
-                back[device, j * rounds + i] = place
+                place = place_at[i, part * groups + group]
+                order[device, place] = part * rounds + i
+                back[device, part * rounds + i] = place
     home = np.argsort(send, axis=0).astype(np.int32)
     return unit, rounds, pairs, send, order, back, home
 
@@ -348,9 +375,7 @@
     moves = [(b, parts[b] * groups + spots[b // fsdp]) for b in range(total)]
     found = np.zeros((total, fsdp), np.int32)
     for b, target in moves:
-        part, spot = divmod(target, groups)
-        for turn in range(fsdp):
-            found[(part ^ turn) * groups + spot, b % fsdp] = turn
+        found[target % groups :: groups, b % fsdp] = target // groups
     return moves, found
 
 
@@ -597,54 +622,40 @@
 EXTRA = 16
 
 
-def term_kernel(at_ref, left_ref, right_ref, *refs, others):
+def term_kernel(left_ref, right_ref, extra_ref, out_ref):
     size = left_ref.shape[0]
-    total = mul(left_ref[...], right_ref[...])
-    sums = jnp.sum(right_ref[...].astype(WIDE), axis=0, keepdims=True)
-    sums = jnp.broadcast_to(sums, (EXTRA, sums.shape[1]))
-    for other in refs[:others]:
-        total = total + other[:size, :].astype(WIDE)
-        sums = sums + other[size:, :].astype(WIDE)
-    if len(refs) > others + 1:
-        refs[-2][...], refs[-1][...] = total, sums
-    else:
-        refs[-1][:size, :] = total.astype(LOW)
-        refs[-1][size:, :] = sums.astype(LOW)
-
-
-def weight_term(left, right, index, size, *others, final=False):
+    out_ref[:size, :] = mul(left_ref[...], right_ref[...]).astype(LOW)
+    out_ref[size:, :] = extra_ref[...].astype(LOW)
+
+
+def column_parts(width, count):
+    block = min(640, width)
+    tiles = pl.cdiv(width, block)
+    ends = [round(tiles * i / count) for i in range(count + 1)]
+    return block, [(a, b - a) for a, b in zip(ends, ends[1:]) if b > a]
+
+
+def weight_term(left, right, extra, size, block, tiles):
     depth, width = right.shape
-    block = min(640, width)
-    at = jnp.full((1,), index, jnp.int32)
-
-    def tile(rows):
-        return pl.BlockSpec((rows, block), lambda n, at: (0, n))
-
-    low = jax.ShapeDtypeStruct((size + EXTRA, width), LOW)
-    split = [jax.ShapeDtypeStruct((rows, width), WIDE) for rows in (size, EXTRA)]
+    first, count = tiles
+    shards = left.shape[0] // size
+    columns = min(width, (first + count) * block) - first * block
     return pl.pallas_call(
-        functools.partial(term_kernel, others=len(others)),
-        grid_spec=pltpu.PrefetchScalarGridSpec(
-            num_scalar_prefetch=1,
-            grid=(pl.cdiv(width, block),),
-            in_specs=[
-                pl.BlockSpec((size, depth), lambda n, at: (at[0], 0)),
-                pl.BlockSpec((depth, block), lambda n, at: (0, n)),
-                *[tile(size + EXTRA)] * len(others),
-            ],
-            out_specs=[tile(size), tile(EXTRA)] if final else tile(size + EXTRA),
-        ),
-        out_shape=split if final else low,
+        term_kernel,
+        grid=(shards, count),
+        in_specs=[
+            pl.BlockSpec((size, depth), lambda m, n: (m, 0)),
+            pl.BlockSpec((depth, block), lambda m, n: (0, n + first)),
+            pl.BlockSpec((EXTRA, block), lambda m, n: (0, n + first)),
+        ],
+        out_specs=pl.BlockSpec((size + EXTRA, block), lambda m, n: (m, n)),
+        out_shape=jax.ShapeDtypeStruct((shards * (size + EXTRA), columns), LOW),
         compiler_params=pltpu.CompilerParams(
-            dimension_semantics=("arbitrary",), vmem_limit_bytes=32 * 2**20
-        ),
-        cost_estimate=pl.CostEstimate(
-            flops=2 * size * depth * width,
-            bytes_accessed=2 * (depth * (size + width) + (2 + len(others)) * size * width),
-            transcendentals=0,
-        ),
+            dimension_semantics=("arbitrary", "arbitrary"), vmem_limit_bytes=56 * 2**20
+        ),
+        cost_estimate=free(),
         name="weight_term",
-    )(at, left, right, *others)
+    )(left, right, extra)
 
 
 def rms_scale(values, norm_gain):
@@ -744,23 +755,8 @@
     def keep(name):
         return lambda values: held.__setitem__(name, values)
 
-    def gather_parts(name):
-        def land(far):
-            mine = held[name]
-
-            def near(other):
-                held[name] = jnp.stack([mine, other[0], far, other[1]])
-
-            freight.need(swap(jnp.stack([mine, far]), "fsdp", 1), near)
-
-        return land
-
-    def arrived(name, lag=1):
-        def use(block):
-            held[name] = block
-            freight.hurry(block, gather_parts(name), lag)
-
-        return use
+    def gathered(name):
+        return lambda block: held.__setitem__(name, lax.all_gather(block, "fsdp", axis=0))
 
     if planned:
         unit, rounds, pairs, send_slots, order, back, home = unit_plan(
@@ -769,12 +765,16 @@
         slots = jnp.asarray(send_slots)[:, device]
         bias_at = (group, group, group)
         head_units = jnp.asarray(order)[device]
-        units = qkv_rows.reshape(rounds, unit, -1)
-        blocks = [
-            send(lax.dynamic_index_in_dim(units, slots[i], 0, keepdims=False), BOTH, pairs[i])
-            for i in range(rounds)
-        ]
-        freight.after(1, straight(jnp.stack(blocks)), arrived("qkv"))
+
+        def open_units(weight):
+            units = weight.reshape(rounds, unit, -1)
+            blocks = [
+                send(lax.dynamic_index_in_dim(units, slots[i], 0, keepdims=False), BOTH, pairs[i])
+                for i in range(rounds)
+            ]
+            freight.need(lay(*blocks).reshape(rounds * unit, -1), gathered("qkv"))
+
+        freight.need(qkv_rows, open_units)
     else:
         pair_index = group * KV_HEADS // groups
         bias_at = (group, pair_index, pair_index)
@@ -795,17 +795,19 @@
     places_at = jnp.concatenate([head_units, head_ids])
 
     def open_out(weight):
-        freight.need(send(weight, BOTH, out_moves), arrived("out", 2))
-
-    def open_expert(name):
-        def use(shard):
-            held[name] = lax.all_gather(shard, "fsdp", axis=0, tiled=True)
-
-        return use
-
-    freight.need(out_weight, open_out)
-    freight.after(4, gate_up_weight[0], open_expert("gate_up"))
-    freight.after(4, down_weight[0], open_expert("down"))
+        mine = send(weight, BOTH, out_moves)
+        held["out"] = lax.all_gather(mine, "fsdp", axis=0)
+        gate_up, down, _ = lax.optimization_barrier((gate_up_weight[0], down_weight[0], mine))
+        held["gate_up"] = lax.all_gather(gate_up, "fsdp", axis=0, tiled=True)
+        held["down"] = lax.all_gather(down, "fsdp", axis=0, tiled=True)
+
+    freight.after(4, out_weight, open_out)
+
+    def open_routes(own):
+        own = jnp.broadcast_to(own.reshape(1, -1), (groups, tokens * TOPK))
+        held["routes"] = lax.all_to_all(own, "seq", split_axis=0, concat_axis=0, tiled=True)
+
+    freight.after(4, routes, open_routes)
 
     inputs = hidden[0].astype(WIDE)
     first_normed, first_factor = rms_scale(inputs, norm1_gain)
@@ -815,9 +817,9 @@
     cosine, sine = jnp.cos(angles), jnp.sin(angles)
     sink_part = rows_of(sink_logits, group, group_heads)
     gather = ring_gather_steps(out_grad[0], ids, freight, first_last)
-    next(gather)
+    hop = next(gather)
     if planned:
-        qkv_group = straight(held["qkv"]).reshape(fsdp * rounds * unit, -1)
+        qkv_group = straight(held["qkv"].reshape(fsdp * rounds * unit, -1))
     else:
         qkv_full = lax.all_gather(qkv_rows, BOTH, axis=0, tiled=True)
         qkv_group = jnp.concatenate(
@@ -827,19 +829,15 @@
                 rows_of(qkv_full[query_width + pair_width :], pair_index, HD),
             ]
         )
-    freight.need(mul(qkv_group, first_full, NT), keep("projected"))
-    hop = next(gather)
-    out_group = straight(held["out"])
-    if not by_block:
-        out_group = straight(straighten(out_group, "fsdp"))
-    out_group = out_group.reshape(fsdp * out_weight.shape[0], -1)
-    held["projected"], out_group = lax.optimization_barrier((held["projected"], out_group))
+    projected, held["routes"] = lax.optimization_barrier(
+        (mul(qkv_group, first_full, NT), held["routes"])
+    )
+    out_group = straight(held["out"].reshape(fsdp * out_weight.shape[0], -1))
     turned, pair_rows, attended, log_totals = attend(
-        places_at, held["projected"], bias_group[:, None], sink_part, cosine, sine, group_heads
+        places_at, projected, bias_group[:, None], sink_part, cosine, sine, group_heads
     )
 
     freight.need(hop, gather.send)
-    freight.chain(routes, xor_steps("seq"), keep("routes"))
     biases = jnp.concatenate([gate_up_bias, down_bias], axis=1)
     freight.chain(biases, xor_steps("fsdp"), keep("biases"))
     branch = ring_reduce(
@@ -852,9 +850,9 @@
     second_full, last = ring_gather(second_low, ids, freight)
     freight.need(last[0], lambda values: None)
     next(gather)
-    freight.settle()
+    freight.finish()
     joined_weight, down_full = held["gate_up"], held["down"]
-    all_routes = straighten(held["routes"], "seq").reshape(length, TOPK)
+    all_routes = held["routes"].reshape(length, TOPK)
     biases = straighten(held["biases"], "fsdp")
     joined_bias = biases[:, : gate_up_bias.shape[1]].reshape(-1).astype(WIDE)
     down_shift = biases[:, gate_up_bias.shape[1] :].reshape(-1).astype(WIDE)
@@ -870,82 +868,90 @@
     expert_ids = jnp.arange(groups, dtype=jnp.int32)
     mixing_mine = jnp.sum(jnp.where(expert_ids == position, mixing_all, 0.0), axis=1)
     mixing_rows = jnp.sum(jnp.where(into, mixing_mine[None, :], 0.0), axis=1)[:, None]
+    next(gather)
     expert_rows = mul(into_low, second_full).astype(LOW)
-    joined = mul(expert_rows, joined_weight) + joined_bias
+    freight.need(straight(mul(expert_rows, joined_weight) + joined_bias), keep("joined"))
+    next(gather)
+    joined = held["joined"]
     activated = lax.optimization_barrier(clamped_glu(joined, expert_width).astype(LOW))
     expert_columns = expert_rows.T
-    activated_rows = activated.T
     upstream_full = None
     for upstream_full in gather:
         pass
     upstream_full = upstream_full[0]
     freight.finish()
     freight = Freight()
-    landed = {"down": [], "joined": []}
-    down_rows = expert_width // fsdp
-    joined_rows = hidden.shape[2] // fsdp
-
-    def down_term(j, *others, final=False):
-        return weight_term(activated_rows, rows_grad, part ^ j, down_rows, *others, final=final)
-
-    def joined_term(j, *others, final=False):
-        grad = held["joined_grad"]
-        return weight_term(expert_columns, grad, part ^ j, joined_rows, *others, final=final)
-
     upstream_rows = mul(into_low, upstream_full)
     rows_grad = (upstream_rows * mixing_rows).astype(LOW)
-    near = swap(down_term(3), "fsdp", 1)
-    down_away = down_term(2, near)
-    down_close = swap(down_term(1), "fsdp", 1)
-    freight.load(down_away, [down_away.shape[0]], landed["down"].append, [1], [4])
+    down_term = straight(mul(activated, rows_grad, TN).astype(LOW))
+    down_total = lax.psum_scatter(down_term, "fsdp", scatter_dimension=0, tiled=True)
+    freight.at(9, down_total, lambda total: freight.need(total.astype(WIDE), keep("down_shard")))
+    activated, _ = lax.optimization_barrier((activated, down_term))
     expert_out = (mul(activated, down_full) + down_shift).astype(LOW).astype(WIDE)
     weighted = (expert_out * mixing_rows).astype(LOW)
     mixing_grad_rows = jnp.sum(upstream_rows * expert_out, axis=1)
+    down_sums = jnp.sum(rows_grad.astype(WIDE), axis=0, keepdims=True)
+
 
     def back_first(upstream):
         activated_grad = mul(upstream, down_full, NT)
-        joined_grad = glu_back(joined, expert_width, activated_grad).astype(LOW)
-        freight.need(joined_grad, back_second)
-
-    def back_second(joined_grad):
-        held["joined_grad"] = joined_grad
-        near = swap(joined_term(3), "fsdp", 1)
-        freight.need(joined_term(1), keep("joined_one"))
-        freight.need(near, back_third)
-
-    def back_third(near):
-        held["joined_close"] = swap(held["joined_one"], "fsdp", 1)
-        freight.need(held["joined_grad"], keep("joined_grad"))
-        freight.need(joined_term(2, near), back_fourth)
-
-    def back_fourth(away):
-        sizes = spread(away.shape[0], [1, 1, 1])
-        freight.load(away, sizes, landed["joined"].append, [1, 4, 7], [3, 3, 3])
-        rows = mul(held["joined_grad"], joined_weight, NT).astype(LOW)
-        held["input_rows_grad"] = rows
-
+        grad = straight(glu_back(joined, expert_width, activated_grad).astype(LOW))
+        freight.need(grad, back_second)
+
+    def back_second(grad):
+        held["input_rows_grad"] = straight(mul(grad, joined_weight, NT).astype(LOW))
+        back_third(grad)
+
+    def back_third(grad):
+        sums = jnp.sum(grad.astype(WIDE), axis=0, keepdims=True)
+        extra = jnp.concatenate([sums, jnp.pad(down_sums, ((0, 0), (0, expert_width)))])
+        extra = jnp.pad(extra, ((0, EXTRA - 2), (0, 0)))
+        block, split = column_parts(grad.shape[1], 3)
+        held["joined_parts"] = [None] * len(split)
+        held["joined_shard"] = blank((hidden.shape[2] // fsdp, grad.shape[1]), WIDE)
+
+        def part_there(i, term):
+            total = lax.psum_scatter(term, "fsdp", scatter_dimension=0, tiled=True)
+            freight.at([11, 13, 16][i], total, functools.partial(part_kept, i))
+
+        def part_kept(i, total):
+            own_rows = hidden.shape[2] // fsdp
+            rows = total[:own_rows].astype(WIDE)
+            start = split[i][0] * block
+            held["joined_shard"] = lax.dynamic_update_slice(held["joined_shard"], rows, (0, start))
+            held["joined_parts"][i] = total[own_rows : own_rows + 2].astype(WIDE)
+            if i + 1 < len(split):
+                freight.need(held["joined_shard"], keep("joined_shard"))
+
+        def begin(i, held_here):
+            grad, extra = held_here
+            size = hidden.shape[2] // fsdp
+            term = weight_term(expert_columns, grad, extra, size, block, split[i])
+            freight.need(term, functools.partial(part_there, i))
+
+        begin(0, (grad, extra))
+        for i in range(1, len(split)):
+            freight.at([2, 5, 7][i], (grad, extra), functools.partial(begin, i))
+
+    def mixing_back(rows):
+        tokens_grad = jnp.sum(jnp.where(back_to, rows[None, :], 0.0), axis=1)
+        by_device = lax.all_to_all(
+            tokens_grad.reshape(groups, tokens), "seq", split_axis=0, concat_axis=0, tiled=True
+        )
+        freight.need(by_device, keep("mixing_grad"))
+
+    freight.need(mixing_grad_rows, mixing_back)
     freight.need(rows_grad, back_first)
     combined = ring_reduce(lambda index: mul(rows_of(back_low, index, tokens), weighted), ids, freight)
-    outputs = middle + combined
-    mixing_grad = jnp.sum(jnp.where(back_to, mixing_grad_rows[None, :], 0.0), axis=1)
-    mixing_grad = lax.all_to_all(
-        mixing_grad.reshape(groups, tokens), "seq", split_axis=0, concat_axis=0, tiled=True
-    ).T
+    freight.need((middle + combined).astype(LOW), keep("outputs"))
     if "input_rows_grad" not in held:
-        freight.settle()
-    joined_grad, input_rows_grad = held["joined_grad"], held["input_rows_grad"]
-    def down_last(close):
-        freight.need(down_term(0, close, final=True), keep("down_keep"))
-
-    def joined_last(close):
-        freight.need(joined_term(0, close, final=True), keep("joined_keep"))
-
-    freight.after(2, down_close, down_last)
-    freight.after(5, held["joined_close"], joined_last)
+        freight.finish()
+    input_rows_grad = held["input_rows_grad"]
     second_grad = ring_reduce(
         lambda index: mul(rows_of(back_low, index, tokens), input_rows_grad), ids, freight
     )
     mixing = mixing_of(second_low, routes[0], router_weight, router_bias)
+    mixing_grad = held["mixing_grad"].T
     logits_grad = mixing * (
         mixing_grad - jnp.sum(mixing * mixing_grad, axis=-1, keepdims=True)
     )
@@ -963,7 +969,6 @@
     router_bias_grad = jnp.sum(logits_grad, axis=0)
     out_bias_grad = jnp.sum(branch_low.astype(WIDE), axis=0)
     early = [out_bias_grad, gain2_grad, router_weight_grad.T.reshape(-1), router_bias_grad]
-    early = jnp.concatenate(early)
     branch_full, _ = ring_gather(branch_low, ids, freight)
     heads_grad = mul(out_group, branch_full, NT).astype(LOW)
     query_grad, pair_grad, sink_grad = attend_back(
@@ -996,47 +1001,42 @@
     )
 
     def out_first(grad):
-        terms = straight(mul(attended, grad).astype(LOW)).reshape(fsdp, out_weight.shape[0], -1)
-        if not by_block:
-            terms = straight(straighten(terms, "fsdp"))
+        terms = straight(mul(attended, grad).astype(LOW))
 
         def use(total):
-            back = [(b, a) for a, b in out_moves]
-            freight.need(send(total.astype(LOW), BOTH, back), keep("out_shard"))
-
-        freight.blocks(terms, use)
+            held["out_shard"] = send(total.astype(LOW), BOTH, [(b, a) for a, b in out_moves])
+
+        freight.blocks(terms.reshape(fsdp, out_weight.shape[0], -1), 15, 16, use)
 
     def qkv_first(grad):
         terms = mul(grad, first_full)
         low = straight(terms.astype(LOW))
         sums = jnp.sum(low.astype(WIDE) * qkv_group.astype(WIDE), axis=0) / norm1_gain
-        values = jnp.concatenate([sums, bias_full, sink_full, early])
-        for step in sum_steps(BOTH):
-            values = step(values)
-        held["late"] = values
+        held["late"] = jnp.concatenate([sums, bias_full, sink_full, *early])
         if not planned:
             held["qkv_term"] = terms
             return
 
-        def use(total):
-            total = total.astype(LOW)
+        def come_back(total):
+            total = straight(total.astype(LOW))
             returned = [
                 send(total[i], BOTH, [(b, a) for a, b in pairs[i]]) for i in range(rounds)
             ]
-            freight.need(straight(jnp.stack(returned)), keep("returned"))
-
-        freight.blocks(low.reshape(fsdp, rounds, unit, -1), use)
+            held["returned"] = lay(*returned)
+
+        freight.blocks(low.reshape(fsdp, rounds, unit, -1), 14, 15, come_back)
 
     freight.need(projected_grad, qkv_first)
-    freight.need(branch_full, out_first)
+    freight.at(14, branch_full, out_first)
     first_grad = ring_reduce(
         lambda index: mul(columns_of(projected_grad, index, tokens), qkv_group, TN), ids, freight
     )
     freight.finish()
-    down_shard, bias_sums = add_pieces(held["down_keep"], landed["down"])
-    down_bias_shard = rows_of(bias_sums, part, down_bias.shape[1])
-    joined_shard, bias_sums = add_pieces(held["joined_keep"], landed["joined"])
-    joined_bias_shard = rows_of(bias_sums, part, gate_up_bias.shape[1])
+    joined_sums = jnp.concatenate(held["joined_parts"], axis=1)
+    joined_shard = held["joined_shard"]
+    joined_bias_shard = rows_of(joined_sums[0], part, gate_up_bias.shape[1])
+    down_bias_shard = rows_of(joined_sums[1, :width], part, down_bias.shape[1])
+    down_shard = held["down_shard"]
     out_shard = held["out_shard"].astype(WIDE)
     if planned:
         qkv_shard = jnp.take(held["returned"], jnp.asarray(home)[:, device], axis=0, mode="clip")
@@ -1051,14 +1051,16 @@
         ):
             scattered = lax.dynamic_update_slice(scattered, qkv_term[start:stop], (row, 0))
         qkv_shard = lax.psum_scatter(scattered, BOTH, scatter_dimension=0, tiled=True).T
+    late, first_grad = lax.optimization_barrier((held["late"], first_grad))
+    for step in sum_steps(BOTH):
+        late = step(late)
     input_part, _ = rms_back(inputs, first_factor, norm1_gain, first_grad)
     input_grad = middle_grad + input_part
 
-    late = held["late"]
     early = late[width + qkv_bias.shape[0] + head_count :]
     router_sums = early[2 * width : 2 * width + width * groups].reshape(groups, width).T
     return (
-        outputs.astype(LOW)[None],
+        held["outputs"][None],
         input_grad.astype(LOW)[None],
         late[:width],
         qkv_shard,

time: 1060 us -> 1010 us (0.953)
  waiting for transfers between devices: 363 us -> 311 us
  local copies, waits for them, and re-layouts: 124 us -> 94.2 us
  matrix products: 215 us -> 243 us
  starting transfers between devices: 125 us -> 149 us
  Pallas kernels: 124 us -> 104 us
    ppermute x86 -> x77, waiting for transfers between devices: 337 us -> 269 us  [send(): return straight(lax.ppermute(blocks, axis, pairs)).reshape(values.shape)]
    dot_general x44 -> x45, matrix products: 210 us -> 241 us  [mul(): return lax.dot_general(left, right, dims, preferred_element_type=WIDE)]
    unnamed x253 -> x173, local copies, waits for them, and re-layouts: 36 us -> 14.4 us
    pallas_call x8 -> x7, Pallas kernels: 77.7 us -> 57.8 us  [the longest x3 53.8 us: weight_term(): pl.pallas_call(term_kernel, grid=(shards, count), in_specs=[pl.BlockSpec(...]
    slice x13 -> x5, local copies, waits for them, and re-layouts: 15.7 us -> 2.04 us  [the longest x2 1.37 us: blocks(): self.at(near_at, swap(straight(terms[:2]), 'fsdp', 1), near_there)]
    ppermute x86 -> x77, starting transfers between devices: 108 us -> 121 us  [send(): return straight(lax.ppermute(blocks, axis, pairs)).reshape(values.shape)]
    ppermute x16 -> x10, waiting for transfers between devices: 21.8 us -> 33.3 us  [send(): return straight(lax.ppermute(straight(values), axis, pairs))]
    dynamic_update_slice x34 -> x33, local copies, waits for them, and re-layouts: 31.9 us -> 42 us  [put(): lax.dynamic_update_slice(full, part, (index * tokens + offset, 0))]
  transfers between devices with their start and end apart: 105 -> 97, of which waited for: 48 -> 49; matrix products, arithmetic and copies ran while one was open for 33% -> 38% of each run, Pallas kernels for 9% -> 10%
where the time goes in v2:
time: 1010 us; the launch traced here: 996 us
  waiting for transfers between devices  311 us (31%)
  matrix products  243 us (24%)
  starting transfers between devices  149 us (15%)
  Pallas kernels  104 us (10%)
  local copies, waits for them, and re-layouts  94.2 us (9%)
  other arithmetic  62.1 us (6%)
  between operations  32.5 us (3%)
    ppermute x77, waiting for transfers between devices, send(): return straight(lax.ppermute(blocks, axis, pairs)).reshape(values.shape)  269 us
    dot_general x45, matrix products, mul(): return lax.dot_general(left, right, dims, preferred_element_type=WIDE)  241 us
    ppermute x77, starting transfers between devices, send(): return straight(lax.ppermute(blocks, axis, pairs)).reshape(values.shape)  121 us
    pallas_call x3, Pallas kernels, weight_term(): pl.pallas_call(term_kernel, grid=(shards, count), in_specs=[pl.BlockSpec(...  53.8 us
    dynamic_update_slice x33, local copies, waits for them, and re-layouts, put(): lax.dynamic_update_slice(full, part, (index * tokens + offset, 0))  42 us
    ppermute x10, waiting for transfers between devices, send(): return straight(lax.ppermute(straight(values), axis, pairs))  33.3 us
    pallas_call x1, Pallas kernels, attend(): pl.pallas_call(functools.partial(forward_kernel, block=block, scale=HD **...  24.7 us
    pallas_call x1, Pallas kernels, attend_back(): pl.pallas_call(functools.partial(backward_kernel, block=block, scale=HD *...  21.9 us
  transfers between devices with their start and end apart: 97, of which 49 were waited for; matrix products, arithmetic and copies ran while one was open for 38% of the time, Pallas kernels for 10%

profile of v2, /device:TPU:24, one launch (start us, length us, event | category | flops | bytes accessed | tf_op | source)
XLA Modules:
  0.0 996.5 jit_solution(17216985425761744956)
XLA Ops:
  51.8 17.4 %collective-permute-done.7 = bf16[8,16,2880]{2,1,0:T(8,128)(2,1)S(1)} collective-permute-done((bf16[8,16,2880]{2,1,0:T(8,128)(2,1)S(1)}, bf16[8,16,2880]{2,1,0:T(8,128)(2,1)S(1)}, u32[]{:S(2)}, u32[]{:S(2)}) %collective-permute-start.7) | collective-permute-done | bytes 737312 | tf_op jit(solution)/shard_map/ppermute | solution.py:130
  71.6 17.3 %collective-permute-done.9 = bf16[8,16,2880]{2,1,0:T(8,128)(2,1)S(1)} collective-permute-done((bf16[8,16,2880]{2,1,0:T(8,128)(2,1)S(1)}, bf16[8,16,2880]{2,1,0:T(8,128)(2,1)S(1)}, u32[]{:S(2)}, u32[]{:S(2)}) %collective-permute-start.9) | collective-permute-done | bytes 737312 | tf_op jit(solution)/shard_map/ppermute | solution.py:130
  93.8 19.2 %collective-permute-done.13 = bf16[8,16,2880]{2,1,0:T(8,128)(2,1)S(1)} collective-permute-done((bf16[8,16,2880]{2,1,0:T(8,128)(2,1)S(1)}, bf16[8,16,2880]{2,1,0:T(8,128)(2,1)S(1)}, u32[]{:S(2)}, u32[]{:S(2)}) %collective-permute-start.13) | collective-permute-done | bytes 737312 | tf_op jit(solution)/shard_map/ppermute | solution.py:130
  163.6 24.7 %attend.1 = (bf16[512,1024]{1,0:T(8,128)(2,1)S(1)}, bf16[128,1024]{1,0:T(8,128)(2,1)S(1)}, bf16[512,1024]{1,0:T(8,128)(2,1)S(1)}, f32[8,1,1024]{2,1,0:T(1,128)S(1)}) custom-call(s32[28]{0:T(128)S(1)} %pad_add_fusion.at_ref, f32[8]{0:T(128)S(1)} %dynamic_slice.147.sink_ref, ...), custom_call_target="tpu_custom_call" | custom-call | tf_op jit(solution)/shard_map/attend/pallas_call | solution.py:465
  217.1 14.6 %collective-permute-done.20 = bf16[8,16,2880]{2,1,0:T(8,128)(2,1)} collective-permute-done((bf16[8,16,2880]{2,1,0:T(8,128)(2,1)}, bf16[8,16,2880]{2,1,0:T(8,128)(2,1)}, u32[]{:S(2)}, u32[]{:S(2)}) %collective-permute-start.20) | collective-permute-done | bytes 737312 | tf_op jit(solution)/shard_map/ppermute | solution.py:130
  237.1 15.5 %collective-permute-done.22 = bf16[8,16,2880]{2,1,0:T(8,128)(2,1)S(1)} collective-permute-done((bf16[8,16,2880]{2,1,0:T(8,128)(2,1)S(1)}, bf16[8,16,2880]{2,1,0:T(8,128)(2,1)S(1)}, u32[]{:S(2)}, u32[]{:S(2)}) %collective-permute-start.22) | collective-permute-done | bytes 737312 | tf_op jit(solution)/shard_map/ppermute | solution.py:130
  256.3 14.5 %collective-permute-done.23 = bf16[8,16,2880]{2,1,0:T(8,128)(2,1)S(1)} collective-permute-done((bf16[8,16,2880]{2,1,0:T(8,128)(2,1)S(1)}, bf16[8,16,2880]{2,1,0:T(8,128)(2,1)S(1)}, u32[]{:S(2)}, u32[]{:S(2)}) %collective-permute-start.23) | collective-permute-done | bytes 737312 | tf_op jit(solution)/shard_map/ppermute | solution.py:130
  278.8 14.8 %collective-permute-done.25 = bf16[8,16,2880]{2,1,0:T(8,128)(2,1)} collective-permute-done((bf16[8,16,2880]{2,1,0:T(8,128)(2,1)}, bf16[8,16,2880]{2,1,0:T(8,128)(2,1)}, u32[]{:S(2)}, u32[]{:S(2)}) %collective-permute-start.25) | collective-permute-done | bytes 737312 | tf_op jit(solution)/shard_map/ppermute | solution.py:130
  317.0 10.8 %collective-permute-done.29 = bf16[8,16,2880]{2,1,0:T(8,128)(2,1)S(1)} collective-permute-done((bf16[8,16,2880]{2,1,0:T(8,128)(2,1)S(1)}, bf16[8,16,2880]{2,1,0:T(8,128)(2,1)S(1)}, u32[]{:S(2)}, u32[]{:S(2)}) %collective-permute-start.29) | collective-permute-done | bytes 737312 | tf_op jit(solution)/shard_map/ppermute | solution.py:130
  356.7 13.5 %collective-permute-start.35 = (bf16[8,16,2880]{2,1,0:T(8,128)(2,1)S(1)}, bf16[8,16,2880]{2,1,0:T(8,128)(2,1)S(1)}, u32[]{:S(2)}, u32[]{:S(2)}) collective-permute-start(bf16[8,16,2880]{2,1,0:T(8,128)(2,1)S(1)} %collective-permute-done.33), channel_id=1, source_target_pairs={{2,0},{4,2},{6,4},{7,6},{5,7},{3,5},{1,3},{0,1},{10,8},{12,10},{14... | collective-permute-start | bytes 2211848 | tf_op jit(solution)/shard_map/ppermute | solution.py:130
  381.9 27.7 %convolution_add_fusion = f32[576,5760]{1,0:T(8,128)S(1)} fusion(bf16[576,2880]{0,1:T(8,128)(2,1)} %convolution_convert_fusion.2, bf16[2880,5760]{1,0:T(8,128)(2,1)} %all-gather.8.cloned.1.call-done, f32[5760]{0:T(1024)S(1)} %reshape.814), kind=kOutput, calls=%fused_computation.4 | convolution fusion | flops 19113615360 | bytes 49789440 | tf_op jit(solution)/shard_map/dot_general | solution.py:31
  429.7 16.8 %convolution_convert_fusion = bf16[2880,2880]{1,0:T(8,128)(2,1)} fusion(bf16[576,2880]{1,0:T(8,128)(2,1)S(1)} %multiply_convert_fusion.1, bf16[576,2880]{1,0:T(8,128)(2,1)S(1)} %get-tuple-element.179), kind=kOutput, calls=%fused_computation.2 | convolution fusion | flops 9563443200 | bytes 23224320 | tf_op jit(solution)/shard_map/dot_general | solution.py:31
  454.1 17.5 %fusion.1 = (f32[576]{0:T(1024)S(1)}, bf16[576,2880]{1,0:T(8,128)(2,1)S(1)}) fusion(f32[576,2880]{1,0:T(8,128)} %get-tuple-element.365, f32[576]{0:T(1024)S(1)} %select_reduce_fusion.1, f32[2880]{0:T(1024)S(1)} %reshape.815, bf16[576,2880]{1,0:T(8,128)(2,1)} %copy-done.34, bf16[2880,2880]{1,0:T(8,128)(2,1)} %all-gather.10.cloned.1.call-done), kind=kOutput, calls=%fused_computation.9 | convolution fusion | flops 9566759936 | bytes 29875968 | tf_op jit(solution)/shard_map/dot_general | solution.py:31
  485.0 22.2 %select_convert_fusion.1 = (bf16[576,2880]{1,0:T(8,128)(2,1)}, bf16[576,2880]{1,0:T(8,128)(2,1)}) fusion(f32[576,5760]{1,0:T(8,128)} %copy-done.26, bf16[576,2880]{1,0:T(8,128)(2,1)} %copy-done.80, bf16[2880,2880]{1,0:T(8,128)(2,1)} %all-gather.10.cloned.1.call-done), kind=kOutput, calls=%fused_computation.13 | convolution fusion | flops 9591644160 | bytes 39813120 | tf_op jit(solution)/shard_map/dot_general | solution.py:31
  527.2 18.1 %weight_term.3 = bf16[2944,1920]{1,0:T(8,128)(2,1)} custom-call(bf16[2880,576]{1,0:T(8,128)(2,1)} %bitcast.390, bf16[576,5760]{1,0:T(8,128)(2,1)} %pad_maximum_fusion.right_ref, f32[16,5760]{1,0:T(8,128)} %pad.67.extra_ref), custom_call_target="tpu_custom_call" | custom-call | tf_op jit(solution)/shard_map/weight_term/pallas_call | solution.py:643
  554.4 27.6 %convolution_convert_fusion.3 = bf16[576,2880]{1,0:T(8,128)(2,1)S(1)} fusion(bf16[576,5760]{1,0:T(8,128)(2,1)} %pad_maximum_fusion.right_ref, bf16[2880,5760]{1,0:T(8,128)(2,1)} %all-gather.8.cloned.1.call-done), kind=kOutput, calls=%fused_computation.25 | convolution fusion | flops 19111956480 | bytes 43130880 | tf_op jit(solution)/shard_map/dot_general | solution.py:31
  590.7 13.3 %collective-permute-done.46 = bf16[8,16,2880]{2,1,0:T(8,128)(2,1)S(1)} collective-permute-done((bf16[8,16,2880]{2,1,0:T(8,128)(2,1)S(1)}, bf16[8,16,2880]{2,1,0:T(8,128)(2,1)S(1)}, u32[]{:S(2)}, u32[]{:S(2)}) %collective-permute-start.46) | collective-permute-done | bytes 737312 | tf_op jit(solution)/shard_map/ppermute | solution.py:130
  609.2 17.9 %weight_term.4 = bf16[2944,1920]{1,0:T(8,128)(2,1)} custom-call(bf16[2880,576]{1,0:T(8,128)(2,1)} %bitcast.391, bf16[576,5760]{1,0:T(8,128)(2,1)} %pad_maximum_fusion.right_ref, f32[16,5760]{1,0:T(8,128)} %pad.67.extra_ref), custom_call_target="tpu_custom_call" | custom-call | tf_op jit(solution)/shard_map/weight_term/pallas_call | solution.py:643
  636.2 13.3 %collective-permute-done.51 = bf16[8,16,2880]{2,1,0:T(8,128)(2,1)S(1)} collective-permute-done((bf16[8,16,2880]{2,1,0:T(8,128)(2,1)}, bf16[8,16,2880]{2,1,0:T(8,128)(2,1)S(1)}, u32[]{:S(2)}, u32[]{:S(2)}) %collective-permute-start.51) | collective-permute-done | bytes 737312 | tf_op jit(solution)/shard_map/ppermute | solution.py:130
  657.9 17.8 %weight_term.5 = bf16[2944,1920]{1,0:T(8,128)(2,1)} custom-call(bf16[2880,576]{1,0:T(8,128)(2,1)} %bitcast.392, bf16[576,5760]{1,0:T(8,128)(2,1)} %pad_maximum_fusion.right_ref, f32[16,5760]{1,0:T(8,128)} %pad.67.extra_ref), custom_call_target="tpu_custom_call" | custom-call | tf_op jit(solution)/shard_map/weight_term/pallas_call | solution.py:643
  769.8 21.9 %attend_back.1 = (bf16[512,1024]{1,0:T(8,128)(2,1)S(1)}, bf16[128,1024]{1,0:T(8,128)(2,1)S(1)}, f32[8,1,128]{2,1,0:T(1,128)S(1)}) custom-call(s32[28]{0:T(128)S(1)} %pad_add_fusion.at_ref, f32[8]{0:T(128)S(1)} %dynamic_slice.147.sink_ref, bf16[512,1024]{1,0:T(8,128)(2,1)S(1)} %get-tuple-element.201.turned_ref, ...), custom_call_target="tpu_custom_call" | custom-call | tf_op jit(solution)/shard_map/attend_back/pallas_call | solution.py:582
  838.5 12.6 %collective-permute-done.68 = bf16[8,16,2880]{2,1,0:T(8,128)(2,1)} collective-permute-done((bf16[8,16,2880]{2,1,0:T(8,128)(2,1)}, bf16[8,16,2880]{2,1,0:T(8,128)(2,1)}, u32[]{:S(2)}, u32[]{:S(2)}) %collective-permute-start.68) | collective-permute-done | bytes 737312 | tf_op jit(solution)/shard_map/ppermute | solution.py:130
  860.7 19.4 %collective-permute-done.70 = bf16[5,32,2880]{2,1,0:T(8,128)(2,1)} collective-permute-done((bf16[5,32,2880]{2,1,0:T(8,128)(2,1)}, bf16[5,32,2880]{2,1,0:T(8,128)(2,1)}, u32[]{:S(2)}, u32[]{:S(2)}) %collective-permute-start.70) | collective-permute-done | bytes 921632 | tf_op jit(solution)/shard_map/ppermute | solution.py:131
  935.7 13.2 %collective-permute-done.74 = bf16[8,16,2880]{2,1,0:T(8,128)(2,1)S(1)} collective-permute-done((bf16[8,16,2880]{2,1,0:T(8,128)(2,1)}, bf16[8,16,2880]{2,1,0:T(8,128)(2,1)S(1)}, u32[]{:S(2)}, u32[]{:S(2)}) %collective-permute-start.74) | collective-permute-done | bytes 737312 | tf_op jit(solution)/shard_map/ppermute | solution.py:130
  (583 shorter events, 542.2 us)
Async XLA Ops:
  7.2 147.3 %all-gather.12.cloned.1.call-start = ((), (), s32[]{:S(2)}) async-start(), calls=%async_computation.12 | async-start | bytes 4710400 | tf_op jit(solution)/shard_map/all_gather | solution.py:759
  11.2 38.5 %collective-permute-start = (bf16[8,16,2880]{2,1,0:T(8,128)(2,1)S(1)}, bf16[8,16,2880]{2,1,0:T(8,128)(2,1)S(1)}, u32[]{:S(2)}, u32[]{:S(2)}) collective-permute-start(bf16[8,16,2880]{2,1,0:T(8,128)(2,1)S(1)} %bitcast.421), channel_id=1, source_target_pairs={{0,2},{2,4},{4,6},{6,7},{7,5},{5,3},{3,1},{1,0},{8,10},{10,12},{12... | collective-permute-start | bytes 2211848 | tf_op jit(solution)/shard_map/ppermute | solution.py:130
  12.7 37.0 %collective-permute-start.1 = (bf16[8,16,2880]{2,1,0:T(8,128)(2,1)S(1)}, bf16[8,16,2880]{2,1,0:T(8,128)(2,1)}, u32[]{:S(2)}, u32[]{:S(2)}) collective-permute-start(bf16[8,16,2880]{2,1,0:T(8,128)(2,1)S(1)} %bitcast.422), channel_id=1, source_target_pairs={{2,0},{4,2},{6,4},{7,6},{5,7},{3,5},{1,3},{0,1},{10,8},{12,10},{14... | collective-permute-start | bytes 2211848 | tf_op jit(solution)/shard_map/ppermute | solution.py:130
  49.7 138.6 %all-gather.6.cloned.1.call-start = ((), (), s32[]{:S(2)}) async-start(), calls=%async_computation.6 | async-start | bytes 3686400 | tf_op jit(solution)/shard_map/all_gather | solution.py:799
  114.1 267.8 %all-gather.8.cloned.1.call-start = ((), (), s32[]{:S(2)}) async-start(), calls=%async_computation.7 | async-start | bytes 41472000 | tf_op jit(solution)/shard_map/all_gather | solution.py:801
  115.0 339.1 %all-gather.10.cloned.1.call-start = ((), (), s32[]{:S(2)}) async-start(), calls=%async_computation.8 | async-start | bytes 21196800 | tf_op jit(solution)/shard_map/all_gather | solution.py:802
  145.4 561.8 %reduce-scatter.13.cloned.1.call-start = ((), (), s32[]{:S(2)}) async-start(), calls=%async_computation.13 | async-start | bytes 21196800
  148.7 47.5 %collective-permute-start.14 = (bf16[8,16,2880]{2,1,0:T(8,128)(2,1)}, bf16[8,16,2880]{2,1,0:T(8,128)(2,1)}, u32[]{:S(2)}, u32[]{:S(2)}) collective-permute-start(bf16[8,16,2880]{2,1,0:T(8,128)(2,1)} %bitcast.57), channel_id=1, source_target_pairs={{0,2},{2,4},{4,6},{6,7},{7,5},{5,3},{3,1},{1,0},{8,10},{10,12},{12... | collective-permute-start | bytes 2211848 | tf_op jit(solution)/shard_map/ppermute | solution.py:130
  149.4 46.9 %collective-permute-start.15 = (bf16[8,16,2880]{2,1,0:T(8,128)(2,1)}, bf16[8,16,2880]{2,1,0:T(8,128)(2,1)}, u32[]{:S(2)}, u32[]{:S(2)}) collective-permute-start(bf16[8,16,2880]{2,1,0:T(8,128)(2,1)} %bitcast.59), channel_id=1, source_target_pairs={{2,0},{4,2},{6,4},{7,6},{5,7},{3,5},{1,3},{0,1},{10,8},{12,10},{14... | collective-permute-start | bytes 2211848 | tf_op jit(solution)/shard_map/ppermute | solution.py:130
  356.7 23.3 %collective-permute-start.35 = (bf16[8,16,2880]{2,1,0:T(8,128)(2,1)S(1)}, bf16[8,16,2880]{2,1,0:T(8,128)(2,1)S(1)}, u32[]{:S(2)}, u32[]{:S(2)}) collective-permute-start(bf16[8,16,2880]{2,1,0:T(8,128)(2,1)S(1)} %collective-permute-done.33), channel_id=1, source_target_pairs={{2,0},{4,2},{6,4},{7,6},{5,7},{3,5},{1,3},{0,1},{10,8},{12,10},{14... | collective-permute-start | bytes 2211848 | tf_op jit(solution)/shard_map/ppermute | solution.py:130
  476.9 43.0 %all-to-all-start.1 = ((f32[8,1,128]{2,1,0:T(1,128)}), f32[8,1,128]{2,1,0:T(1,128)S(1)}, u32[]{:S(2)}, u32[]{:S(2)}) async-start(f32[8,1,128]{2,1,0:T(1,128)} %bitcast.115), calls=%async_computation.1 | async-start | bytes 8192 | tf_op jit(solution)/shard_map/all_to_all | solution.py:938
  482.9 247.8 %reduce-scatter.7.cloned.1.call-start = ((), (), s32[]{:S(2)}) async-start(), calls=%async_computation.9 | async-start | bytes 14131200 | tf_op jit(solution)/shard_map/reduce_scatter | solution.py:914
  482.9 31.8 %collective-permute-start.41 = (bf16[4,16,2880]{2,1,0:T(8,128)(2,1)}, bf16[4,16,2880]{2,1,0:T(8,128)(2,1)S(1)}, u32[]{:S(2)}, u32[]{:S(2)}) collective-permute-start(bf16[4,16,2880]{2,1,0:T(8,128)(2,1)} %bitcast.455), channel_id=1, source_target_pairs={{2,0},{4,2},{6,4},{7,6},{5,7},{3,5},{1,3},{0,1},{10,8},{12,10},{14... | collective-permute-start | bytes 1105928 | tf_op jit(solution)/shard_map/ppermute | solution.py:130
  483.5 33.8 %collective-permute-start.40 = (bf16[4,16,2880]{2,1,0:T(8,128)(2,1)S(1)}, bf16[4,16,2880]{2,1,0:T(8,128)(2,1)S(1)}, u32[]{:S(2)}, u32[]{:S(2)}) collective-permute-start(bf16[4,16,2880]{2,1,0:T(8,128)(2,1)S(1)} %bitcast.454), channel_id=1, source_target_pairs={{0,2},{2,4},{4,6},{6,7},{7,5},{5,3},{3,1},{1,0},{8,10},{10,12},{12... | collective-permute-start | bytes 1105928 | tf_op jit(solution)/shard_map/ppermute | solution.py:130
  519.9 25.4 %collective-permute-start.43 = (bf16[8,16,2880]{2,1,0:T(8,128)(2,1)}, bf16[8,16,2880]{2,1,0:T(8,128)(2,1)}, u32[]{:S(2)}, u32[]{:S(2)}) collective-permute-start(bf16[8,16,2880]{2,1,0:T(8,128)(2,1)} %bitcast.428), channel_id=1, source_target_pairs={{2,0},{4,2},{6,4},{7,6},{5,7},{3,5},{1,3},{0,1},{10,8},{12,10},{14... | collective-permute-start | bytes 2211848 | tf_op jit(solution)/shard_map/ppermute | solution.py:130
  524.9 24.4 %collective-permute-start.42 = (bf16[8,16,2880]{2,1,0:T(8,128)(2,1)}, bf16[8,16,2880]{2,1,0:T(8,128)(2,1)}, u32[]{:S(2)}, u32[]{:S(2)}) collective-permute-start(bf16[8,16,2880]{2,1,0:T(8,128)(2,1)} %bitcast.117), channel_id=1, source_target_pairs={{0,2},{2,4},{4,6},{6,7},{7,5},{5,3},{3,1},{1,0},{8,10},{10,12},{12... | collective-permute-start | bytes 2211848 | tf_op jit(solution)/shard_map/ppermute | solution.py:130
  552.2 244.7 %reduce-scatter.9.cloned.1.call-start = ((), (), s32[]{:S(2)}) async-start(), calls=%async_computation.10 | async-start | bytes 14131200 | tf_op jit(solution)/shard_map/reduce_scatter | solution.py:914
  552.3 29.7 %collective-permute-start.45 = (bf16[8,16,2880]{2,1,0:T(8,128)(2,1)}, bf16[8,16,2880]{2,1,0:T(8,128)(2,1)S(1)}, u32[]{:S(2)}, u32[]{:S(2)}) collective-permute-start(bf16[8,16,2880]{2,1,0:T(8,128)(2,1)} %bitcast.429), channel_id=1, source_target_pairs={{2,0},{4,2},{6,4},{7,6},{5,7},{3,5},{1,3},{0,1},{10,8},{12,10},{14... | collective-permute-start | bytes 2211848 | tf_op jit(solution)/shard_map/ppermute | solution.py:130
  552.9 33.1 %collective-permute-start.44 = (bf16[8,16,2880]{2,1,0:T(8,128)(2,1)}, bf16[8,16,2880]{2,1,0:T(8,128)(2,1)S(1)}, u32[]{:S(2)}, u32[]{:S(2)}) collective-permute-start(bf16[8,16,2880]{2,1,0:T(8,128)(2,1)} %bitcast.430), channel_id=1, source_target_pairs={{0,2},{2,4},{4,6},{6,7},{7,5},{5,3},{3,1},{1,0},{8,10},{10,12},{12... | collective-permute-start | bytes 2211848 | tf_op jit(solution)/shard_map/ppermute | solution.py:130
  633.8 293.2 %reduce-scatter.11.cloned.1.call-start = ((), (), s32[]{:S(2)}) async-start(), calls=%async_computation.11 | async-start | bytes 14131200 | tf_op jit(solution)/shard_map/reduce_scatter | solution.py:914
  831.6 26.5 %collective-permute-start.69 = (bf16[2,128,2880]{1,2,0:T(8,128)(2,1)}, bf16[2,128,2880]{1,2,0:T(8,128)(2,1)}, u32[]{:S(2)}, u32[]{:S(2)}) collective-permute-start(bf16[2,128,2880]{1,2,0:T(8,128)(2,1)} %copy.88), channel_id=1, source_target_pairs={{0,8},{8,0},{16,24},{24,16},{1,9},{9,1},{17,25},{25,17},{2,10},{10... | collective-permute-start | bytes 4423688 | tf_op jit(solution)/shard_map/ppermute | solution.py:131
  836.2 43.9 %collective-permute-start.70 = (bf16[5,32,2880]{2,1,0:T(8,128)(2,1)}, bf16[5,32,2880]{2,1,0:T(8,128)(2,1)}, u32[]{:S(2)}, u32[]{:S(2)}) collective-permute-start(bf16[5,32,2880]{2,1,0:T(8,128)(2,1)} %fusion.39), channel_id=1, source_target_pairs={{0,16},{8,24},{16,0},{24,8},{1,17},{9,25},{17,1},{25,9},{2,18},{10... | collective-permute-start | bytes 2764808 | tf_op jit(solution)/shard_map/ppermute | solution.py:131
  900.4 26.6 %collective-permute-start.73 = (bf16[8,16,2880]{2,1,0:T(8,128)(2,1)}, bf16[8,16,2880]{2,1,0:T(8,128)(2,1)}, u32[]{:S(2)}, u32[]{:S(2)}) collective-permute-start(bf16[8,16,2880]{2,1,0:T(8,128)(2,1)} %bitcast.186), channel_id=1, source_target_pairs={{0,16},{8,24},{16,0},{24,8},{1,17},{9,25},{17,1},{25,9},{2,18},{10... | collective-permute-start | bytes 2211848 | tf_op jit(solution)/shard_map/ppermute | solution.py:130
  932.0 47.5 %collective-permute-start.86 = (bf16[8,16,2880]{2,1,0:T(8,128)(2,1)S(1)}, bf16[8,16,2880]{2,1,0:T(8,128)(2,1)S(1)}, u32[]{:S(2)}, u32[]{:S(2)}) collective-permute-start(bf16[8,16,2880]{2,1,0:T(8,128)(2,1)S(1)} %bitcast.423), channel_id=1, source_target_pairs={{1,0},{25,1},{9,2},{17,3},{20,4},{28,5},{4,6},{12,7},{14,8},{22,9}... | collective-permute-start | bytes 2211848 | tf_op jit(solution)/shard_map/ppermute | solution.py:130
  (157 other events, 2447.2 us)
Sparse Core Ops, SparseCore 0:
  49.8 39.0 all-gather.11
  114.3 27.7 all-gather.5
  143.6 199.5 all-gather.7
  344.6 109.4 all-gather.9
  456.6 129.6 reduce-scatter.12
  588.9 90.6 reduce-scatter.6
  682.4 90.6 reduce-scatter.8
  776.0 110.8 reduce-scatter.10

commit v3 on v2

--- a/solution.py
+++ b/solution.py
@@ -57,29 +57,35 @@
             out[...] = refs[i][...].reshape(out.shape)
 
 
-def lay(*parts):
+def lay_kernel(at_ref, *refs, count):
+    pick_kernel(*refs, count=count)
+
+
+def lay(*parts, at=None):
     arrays, specs = [], []
     for part in parts:
         array, index = part if isinstance(part, tuple) else (part[None], 0)
         arrays.append(array)
-        zeros = (0,) * (array.ndim - 1)
-        specs.append(
-            pl.BlockSpec((1, *array.shape[1:]), lambda n, at=(index, *zeros): at)
-        )
+        place = (index,) + (0,) * (array.ndim - 1)
+        specs.append(pl.BlockSpec((1, *array.shape[1:]), lambda n, at, place=place: place))
     block = arrays[0].shape[1:]
     zeros = (0,) * len(block)
+    at = jnp.arange(len(parts), dtype=jnp.int32) if at is None else at
     return pl.pallas_call(
-        functools.partial(pick_kernel, count=len(parts)),
-        grid=(len(parts),),
-        in_specs=specs,
-        out_specs=pl.BlockSpec((1, *block), lambda n: (n, *zeros)),
+        functools.partial(lay_kernel, count=len(parts)),
+        grid_spec=pltpu.PrefetchScalarGridSpec(
+            num_scalar_prefetch=1,
+            grid=(len(parts),),
+            in_specs=specs,
+            out_specs=pl.BlockSpec((1, *block), lambda n, at: (at[n], *zeros)),
+        ),
         out_shape=jax.ShapeDtypeStruct((len(parts), *block), arrays[0].dtype),
         compiler_params=pltpu.CompilerParams(
             dimension_semantics=("arbitrary",), vmem_limit_bytes=32 * 2**20
         ),
         cost_estimate=free(),
         name="lay",
-    )(*arrays)
+    )(at, *arrays)
 
 
 def picked_kernel(at_ref, source_ref, out_ref):
@@ -498,7 +504,7 @@
             dimension_semantics=("arbitrary",), vmem_limit_bytes=40 * 2**20
         ),
         cost_estimate=pl.CostEstimate(
-            flops=0, bytes_accessed=0, transcendentals=0
+            flops=0, bytes_accessed=22 * rows * length * 8, transcendentals=0
         ),
         name="attend",
     )(at, sinks, *[projected] * 6, bias, bias, cosine, sine)
@@ -755,9 +761,6 @@
     def keep(name):
         return lambda values: held.__setitem__(name, values)
 
-    def gathered(name):
-        return lambda block: held.__setitem__(name, lax.all_gather(block, "fsdp", axis=0))
-
     if planned:
         unit, rounds, pairs, send_slots, order, back, home = unit_plan(
             fsdp, groups, query_width, pair_width
@@ -772,7 +775,10 @@
                 send(lax.dynamic_index_in_dim(units, slots[i], 0, keepdims=False), BOTH, pairs[i])
                 for i in range(rounds)
             ]
-            freight.need(lay(*blocks).reshape(rounds * unit, -1), gathered("qkv"))
+            freight.need(lay(*blocks).reshape(rounds * unit, -1), units_there)
+
+        def units_there(mine):
+            held["qkv"] = lax.all_gather(mine, "fsdp", axis=0, tiled=True)
 
         freight.need(qkv_rows, open_units)
     else:
@@ -795,13 +801,17 @@
     places_at = jnp.concatenate([head_units, head_ids])
 
     def open_out(weight):
-        mine = send(weight, BOTH, out_moves)
-        held["out"] = lax.all_gather(mine, "fsdp", axis=0)
-        gate_up, down, _ = lax.optimization_barrier((gate_up_weight[0], down_weight[0], mine))
-        held["gate_up"] = lax.all_gather(gate_up, "fsdp", axis=0, tiled=True)
-        held["down"] = lax.all_gather(down, "fsdp", axis=0, tiled=True)
-
-    freight.after(4, out_weight, open_out)
+        freight.after(2, send(weight, BOTH, out_moves), out_there)
+
+    def out_there(mine):
+        held["out_mine"], held["out_far"] = mine, swap(mine, "fsdp", 2)
+
+    def open_gate_up(shard):
+        held["gate_up"] = lax.all_gather(shard, "fsdp", axis=0, tiled=True)
+
+    held["down"] = lax.all_gather(down_weight[0], "fsdp", axis=0, tiled=True)
+    freight.after(2, out_weight, open_out)
+    freight.after(3, gate_up_weight[0], open_gate_up)
 
     def open_routes(own):
         own = jnp.broadcast_to(own.reshape(1, -1), (groups, tokens * TOPK))
@@ -819,7 +829,7 @@
     gather = ring_gather_steps(out_grad[0], ids, freight, first_last)
     hop = next(gather)
     if planned:
-        qkv_group = straight(held["qkv"].reshape(fsdp * rounds * unit, -1))
+        qkv_group = held["qkv"]
     else:
         qkv_full = lax.all_gather(qkv_rows, BOTH, axis=0, tiled=True)
         qkv_group = jnp.concatenate(
@@ -832,10 +842,13 @@
     projected, held["routes"] = lax.optimization_barrier(
         (mul(qkv_group, first_full, NT), held["routes"])
     )
-    out_group = straight(held["out"].reshape(fsdp * out_weight.shape[0], -1))
     turned, pair_rows, attended, log_totals = attend(
         places_at, projected, bias_group[:, None], sink_part, cosine, sine, group_heads
     )
+    mine, far, attended = lax.optimization_barrier((held["out_mine"], held["out_far"], attended))
+    near = swap(lay(mine, far), "fsdp", 1)
+    parts = part ^ jnp.arange(fsdp, dtype=jnp.int32)
+    out_group = lay(mine, (near, 0), far, (near, 1), at=parts).reshape(fsdp * mine.shape[0], -1)
 
     freight.need(hop, gather.send)
     biases = jnp.concatenate([gate_up_bias, down_bias], axis=1)
@@ -912,7 +925,7 @@
 
         def part_there(i, term):
             total = lax.psum_scatter(term, "fsdp", scatter_dimension=0, tiled=True)
-            freight.at([11, 13, 16][i], total, functools.partial(part_kept, i))
+            freight.at([11, 14, 16][i], total, functools.partial(part_kept, i))
 
         def part_kept(i, total):
             own_rows = hidden.shape[2] // fsdp
@@ -1004,7 +1017,7 @@
         terms = straight(mul(attended, grad).astype(LOW))
 
         def use(total):
-            held["out_shard"] = send(total.astype(LOW), BOTH, [(b, a) for a, b in out_moves])
+            held["out_total"] = total.astype(LOW)
 
         freight.blocks(terms.reshape(fsdp, out_weight.shape[0], -1), 15, 16, use)
 
@@ -1012,19 +1025,16 @@
         terms = mul(grad, first_full)
         low = straight(terms.astype(LOW))
         sums = jnp.sum(low.astype(WIDE) * qkv_group.astype(WIDE), axis=0) / norm1_gain
-        held["late"] = jnp.concatenate([sums, bias_full, sink_full, *early])
+        late = jnp.concatenate([sums, bias_full, sink_full, *early])
+        freight.chain(late, sum_steps(["seq"]), keep("late"))
         if not planned:
             held["qkv_term"] = terms
             return
 
         def come_back(total):
-            total = straight(total.astype(LOW))
-            returned = [
-                send(total[i], BOTH, [(b, a) for a, b in pairs[i]]) for i in range(rounds)
-            ]
-            held["returned"] = lay(*returned)
-
-        freight.blocks(low.reshape(fsdp, rounds, unit, -1), 14, 15, come_back)
+            held["qkv_total"] = straight(total.astype(LOW))
+
+        freight.blocks(low.reshape(fsdp, rounds, unit, -1), 14, 16, come_back)
 
     freight.need(projected_grad, qkv_first)
     freight.at(14, branch_full, out_first)
@@ -1037,9 +1047,19 @@
     joined_bias_shard = rows_of(joined_sums[0], part, gate_up_bias.shape[1])
     down_bias_shard = rows_of(joined_sums[1, :width], part, down_bias.shape[1])
     down_shard = held["down_shard"]
-    out_shard = held["out_shard"].astype(WIDE)
+    qkv_total = held.get("qkv_total", held["out_total"])
+    late, first_grad, out_total, qkv_total = lax.optimization_barrier(
+        (held["late"], first_grad, held["out_total"], qkv_total)
+    )
     if planned:
-        qkv_shard = jnp.take(held["returned"], jnp.asarray(home)[:, device], axis=0, mode="clip")
+        returned = lay(
+            *[
+                send(qkv_total[i], BOTH, [(b, a) for a, b in pairs[i]])
+                for i in range(rounds)
+            ]
+        )
+    if planned:
+        qkv_shard = jnp.take(returned, jnp.asarray(home)[:, device], axis=0, mode="clip")
         qkv_shard = qkv_shard.reshape(rounds * unit, -1).T.astype(WIDE)
     else:
         qkv_term = held["qkv_term"]
@@ -1051,8 +1071,8 @@
         ):
             scattered = lax.dynamic_update_slice(scattered, qkv_term[start:stop], (row, 0))
         qkv_shard = lax.psum_scatter(scattered, BOTH, scatter_dimension=0, tiled=True).T
-    late, first_grad = lax.optimization_barrier((held["late"], first_grad))
-    for step in sum_steps(BOTH):
+    out_shard = send(out_total, BOTH, [(b, a) for a, b in out_moves]).astype(WIDE)
+    for step in sum_steps(["fsdp"]):
         late = step(late)
     input_part, _ = rms_back(inputs, first_factor, norm1_gain, first_grad)
     input_grad = middle_grad + input_part

time: 1010 us -> 987 us (0.977)
  starting transfers between devices: 149 us -> 130 us
  matrix products: 243 us -> 232 us
    ppermute x77 -> x78, waiting for transfers between devices: 269 us -> 297 us  [send(): return straight(lax.ppermute(blocks, axis, pairs)).reshape(values.shape)]
    ppermute x77 -> x78, starting transfers between devices: 121 us -> 107 us  [send(): return straight(lax.ppermute(blocks, axis, pairs)).reshape(values.shape)]
    ppermute x10 -> x11, waiting for transfers between devices: 33.3 us -> 19.3 us  [send(): return straight(lax.ppermute(straight(values), axis, pairs))]
    unnamed x173 -> x187, local copies, waits for them, and re-layouts: 14.4 us -> 23.9 us
    dynamic_update_slice x33 -> x34, local copies, waits for them, and re-layouts: 42 us -> 42.7 us  [put(): lax.dynamic_update_slice(full, part, (index * tokens + offset, 0))]
  transfers between devices with their start and end apart: 97 -> 98, of which waited for: 49 -> 42; matrix products, arithmetic and copies ran while one was open for 38% -> 37% of each run, Pallas kernels for 10% -> 11%
where the time goes in v3:
time: 987 us; the launch traced here: 976 us
  waiting for transfers between devices  317 us (32%)
  matrix products  232 us (24%)
  starting transfers between devices  130 us (13%)
  Pallas kernels  108 us (11%)
  local copies, waits for them, and re-layouts  98.7 us (10%)
  other arithmetic  57.1 us (6%)
  between operations  33.2 us (3%)
    ppermute x78, waiting for transfers between devices, send(): return straight(lax.ppermute(blocks, axis, pairs)).reshape(values.shape)  297 us
    dot_general x45, matrix products, mul(): return lax.dot_general(left, right, dims, preferred_element_type=WIDE)  231 us
    ppermute x78, starting transfers between devices, send(): return straight(lax.ppermute(blocks, axis, pairs)).reshape(values.shape)  107 us
    pallas_call x3, Pallas kernels, weight_term(): pl.pallas_call(term_kernel, grid=(shards, count), in_specs=[pl.BlockSpec(...  54.6 us
    dynamic_update_slice x34, local copies, waits for them, and re-layouts, put(): lax.dynamic_update_slice(full, part, (index * tokens + offset, 0))  42.7 us
    pallas_call x1, Pallas kernels, attend(): pl.pallas_call(functools.partial(forward_kernel, block=block, scale=HD **...  24.7 us
    unnamed x187, local copies, waits for them, and re-layouts  23.9 us
    pallas_call x1, Pallas kernels, attend_back(): pl.pallas_call(functools.partial(backward_kernel, block=block, scale=HD *...  22 us
  transfers between devices with their start and end apart: 98, of which 42 were waited for; matrix products, arithmetic and copies ran while one was open for 37% of the time, Pallas kernels for 11%

profile of v3, /device:TPU:24, one launch (start us, length us, event | category | flops | bytes accessed | tf_op | source)
XLA Modules:
  0.0 976.3 jit_solution(18148509797376475934)
XLA Ops:
  52.4 17.6 %collective-permute-done.7 = bf16[8,16,2880]{2,1,0:T(8,128)(2,1)S(1)} collective-permute-done((bf16[8,16,2880]{2,1,0:T(8,128)(2,1)}, bf16[8,16,2880]{2,1,0:T(8,128)(2,1)S(1)}, u32[]{:S(2)}, u32[]{:S(2)}) %collective-permute-start.7) | collective-permute-done | bytes 737312 | tf_op jit(solution)/shard_map/ppermute | solution.py:136
  94.4 23.8 %collective-permute-done.9 = bf16[8,16,2880]{2,1,0:T(8,128)(2,1)S(1)} collective-permute-done((bf16[8,16,2880]{2,1,0:T(8,128)(2,1)}, bf16[8,16,2880]{2,1,0:T(8,128)(2,1)S(1)}, u32[]{:S(2)}, u32[]{:S(2)}) %collective-permute-start.9) | collective-permute-done | bytes 737312 | tf_op jit(solution)/shard_map/ppermute | solution.py:136
  145.6 24.7 %attend.1 = (bf16[512,1024]{1,0:T(8,128)(2,1)S(1)}, bf16[128,1024]{1,0:T(8,128)(2,1)S(1)}, bf16[512,1024]{1,0:T(8,128)(2,1)S(1)}, f32[8,1,1024]{2,1,0:T(1,128)S(1)}) custom-call(s32[28]{0:T(128)S(1)} %pad_add_fusion.at_ref, f32[8]{0:T(128)S(1)} %dynamic_slice.147.sink_ref, ...), custom_call_target="tpu_custom_call" | custom-call | bytes 92274688 | tf_op jit(solution)/shard_map/attend/pallas_call | solution.py:471
  220.1 13.2 %collective-permute-done.22 = bf16[8,16,2880]{2,1,0:T(8,128)(2,1)} collective-permute-done((bf16[8,16,2880]{2,1,0:T(8,128)(2,1)}, bf16[8,16,2880]{2,1,0:T(8,128)(2,1)}, u32[]{:S(2)}, u32[]{:S(2)}) %collective-permute-start.22) | collective-permute-done | bytes 737312 | tf_op jit(solution)/shard_map/ppermute | solution.py:136
  241.8 11.6 %collective-permute-done.24 = bf16[8,16,2880]{2,1,0:T(8,128)(2,1)S(1)} collective-permute-done((bf16[8,16,2880]{2,1,0:T(8,128)(2,1)S(1)}, bf16[8,16,2880]{2,1,0:T(8,128)(2,1)S(1)}, u32[]{:S(2)}, u32[]{:S(2)}) %collective-permute-start.24) | collective-permute-done | bytes 737312 | tf_op jit(solution)/shard_map/ppermute | solution.py:136
  260.4 14.1 %collective-permute-done.25 = bf16[8,16,2880]{2,1,0:T(8,128)(2,1)S(1)} collective-permute-done((bf16[8,16,2880]{2,1,0:T(8,128)(2,1)S(1)}, bf16[8,16,2880]{2,1,0:T(8,128)(2,1)S(1)}, u32[]{:S(2)}, u32[]{:S(2)}) %collective-permute-start.25) | collective-permute-done | bytes 737312 | tf_op jit(solution)/shard_map/ppermute | solution.py:136
  280.4 13.8 %collective-permute-done.27 = bf16[8,16,2880]{2,1,0:T(8,128)(2,1)S(1)} collective-permute-done((bf16[8,16,2880]{2,1,0:T(8,128)(2,1)S(1)}, bf16[8,16,2880]{2,1,0:T(8,128)(2,1)S(1)}, u32[]{:S(2)}, u32[]{:S(2)}) %collective-permute-start.27) | collective-permute-done | bytes 737312 | tf_op jit(solution)/shard_map/ppermute | solution.py:136
  298.7 12.6 %collective-permute-done.29 = bf16[8,16,2880]{2,1,0:T(8,128)(2,1)S(1)} collective-permute-done((bf16[8,16,2880]{2,1,0:T(8,128)(2,1)S(1)}, bf16[8,16,2880]{2,1,0:T(8,128)(2,1)S(1)}, u32[]{:S(2)}, u32[]{:S(2)}) %collective-permute-start.29) | collective-permute-done | bytes 737312 | tf_op jit(solution)/shard_map/ppermute | solution.py:136
  317.0 11.3 %collective-permute-done.31 = bf16[8,16,2880]{2,1,0:T(8,128)(2,1)S(1)} collective-permute-done((bf16[8,16,2880]{2,1,0:T(8,128)(2,1)S(1)}, bf16[8,16,2880]{2,1,0:T(8,128)(2,1)S(1)}, u32[]{:S(2)}, u32[]{:S(2)}) %collective-permute-start.31) | collective-permute-done | bytes 737312 | tf_op jit(solution)/shard_map/ppermute | solution.py:136
  373.6 27.5 %convolution_add_fusion = f32[576,5760]{1,0:T(8,128)S(1)} fusion(bf16[576,2880]{0,1:T(8,128)(2,1)} %convolution_convert_fusion.2, bf16[2880,5760]{1,0:T(8,128)(2,1)} %all-gather.7.cloned.1.call-done, f32[5760]{0:T(1024)S(1)} %reshape.821), kind=kOutput, calls=%fused_computation.8 | convolution fusion | flops 19113615360 | bytes 49789440 | tf_op jit(solution)/shard_map/dot_general | solution.py:31
  421.7 16.7 %convolution_convert_fusion = bf16[2880,2880]{1,0:T(8,128)(2,1)} fusion(bf16[576,2880]{1,0:T(8,128)(2,1)S(1)} %multiply_convert_fusion.1, bf16[576,2880]{1,0:T(8,128)(2,1)S(1)} %get-tuple-element.190), kind=kOutput, calls=%fused_computation.2 | convolution fusion | flops 9563443200 | bytes 23224320 | tf_op jit(solution)/shard_map/dot_general | solution.py:31
  439.0 17.4 %fusion.5 = (f32[576]{0:T(1024)S(1)}, bf16[576,2880]{1,0:T(8,128)(2,1)S(1)}) fusion(f32[576,2880]{1,0:T(8,128)} %get-tuple-element.381, f32[576]{0:T(1024)S(1)} %select_reduce_fusion.1, f32[2880]{0:T(1024)S(1)} %reshape.822, bf16[576,2880]{1,0:T(8,128)(2,1)} %copy-done.51, bf16[1,2880,2880]{2,1,0:T(8,128)(2,1)} %all-gather.9.cloned.1.call-done), kind=kOutput, calls=%fused_computation.13 | convolution fusion | flops 9566759936 | bytes 29875968 | tf_op jit(solution)/shard_map/dot_general | solution.py:31
  469.4 21.8 %select_convert_fusion.1 = (bf16[576,2880]{1,0:T(8,128)(2,1)S(1)}, bf16[576,2880]{1,0:T(8,128)(2,1)}) fusion(f32[576,5760]{1,0:T(8,128)} %copy-done.42, bf16[576,2880]{1,0:T(8,128)(2,1)} %copy-done.89, bf16[1,2880,2880]{2,1,0:T(8,128)(2,1)} %all-gather.9.cloned.1.call-done), kind=kOutput, calls=%fused_computation.17 | convolution fusion | flops 9591644160 | bytes 39813120 | tf_op jit(solution)/shard_map/dot_general | solution.py:31
  508.8 18.4 %weight_term.3 = bf16[2944,1920]{1,0:T(8,128)(2,1)} custom-call(bf16[2880,576]{1,0:T(8,128)(2,1)} %bitcast.400, bf16[576,5760]{1,0:T(8,128)(2,1)} %pad_maximum_fusion.right_ref, f32[16,5760]{1,0:T(8,128)} %pad.67.extra_ref), custom_call_target="tpu_custom_call" | custom-call | tf_op jit(solution)/shard_map/weight_term/pallas_call | solution.py:649
  535.4 27.6 %convolution_convert_fusion.3 = bf16[576,2880]{1,0:T(8,128)(2,1)S(1)} fusion(bf16[576,5760]{1,0:T(8,128)(2,1)} %pad_maximum_fusion.right_ref, bf16[2880,5760]{1,0:T(8,128)(2,1)} %all-gather.7.cloned.1.call-done), kind=kOutput, calls=%fused_computation.29 | convolution fusion | flops 19111956480 | bytes 43130880 | tf_op jit(solution)/shard_map/dot_general | solution.py:31
  570.1 12.0 %collective-permute-done.48 = bf16[8,16,2880]{2,1,0:T(8,128)(2,1)S(1)} collective-permute-done((bf16[8,16,2880]{2,1,0:T(8,128)(2,1)S(1)}, bf16[8,16,2880]{2,1,0:T(8,128)(2,1)S(1)}, u32[]{:S(2)}, u32[]{:S(2)}) %collective-permute-start.48) | collective-permute-done | bytes 737312 | tf_op jit(solution)/shard_map/ppermute | solution.py:136
  587.5 18.3 %weight_term.4 = bf16[2944,1920]{1,0:T(8,128)(2,1)} custom-call(bf16[2880,576]{1,0:T(8,128)(2,1)} %bitcast.401, bf16[576,5760]{1,0:T(8,128)(2,1)} %pad_maximum_fusion.right_ref, f32[16,5760]{1,0:T(8,128)} %pad.67.extra_ref), custom_call_target="tpu_custom_call" | custom-call | tf_op jit(solution)/shard_map/weight_term/pallas_call | solution.py:649
  613.7 17.1 %collective-permute-done.53 = bf16[8,16,2880]{2,1,0:T(8,128)(2,1)S(1)} collective-permute-done((bf16[8,16,2880]{2,1,0:T(8,128)(2,1)}, bf16[8,16,2880]{2,1,0:T(8,128)(2,1)S(1)}, u32[]{:S(2)}, u32[]{:S(2)}) %collective-permute-start.53) | collective-permute-done | bytes 737312 | tf_op jit(solution)/shard_map/ppermute | solution.py:136
  638.6 17.9 %weight_term.5 = bf16[2944,1920]{1,0:T(8,128)(2,1)} custom-call(bf16[2880,576]{1,0:T(8,128)(2,1)} %bitcast.402, bf16[576,5760]{1,0:T(8,128)(2,1)} %pad_maximum_fusion.right_ref, f32[16,5760]{1,0:T(8,128)} %pad.67.extra_ref), custom_call_target="tpu_custom_call" | custom-call | tf_op jit(solution)/shard_map/weight_term/pallas_call | solution.py:649
  667.4 16.4 %collective-permute-done.56 = bf16[8,16,2880]{2,1,0:T(8,128)(2,1)S(1)} collective-permute-done((bf16[8,16,2880]{2,1,0:T(8,128)(2,1)}, bf16[8,16,2880]{2,1,0:T(8,128)(2,1)S(1)}, u32[]{:S(2)}, u32[]{:S(2)}) %collective-permute-start.56) | collective-permute-done | bytes 737312 | tf_op jit(solution)/shard_map/ppermute | solution.py:136
  754.2 22.0 %attend_back.1 = (bf16[512,1024]{1,0:T(8,128)(2,1)S(1)}, bf16[128,1024]{1,0:T(8,128)(2,1)S(1)}, f32[8,1,128]{2,1,0:T(1,128)S(1)}) custom-call(s32[28]{0:T(128)S(1)} %copy-done.21, f32[8]{0:T(128)S(1)} %copy-done.19, bf16[512,1024]{1,0:T(8,128)(2,1)S(1)} %copy-done.17, bf16[128,1024]{1,0:T(8,128)(2,1)S(1)} %get-tuple-element.213.pairs_ref, ...), custom_call_target="tpu_custom_call" | custom-call | tf_op jit(solution)/shard_map/attend_back/pallas_call | solution.py:588
  858.6 14.5 %collective-permute-done.74 = bf16[8,16,2880]{2,1,0:T(8,128)(2,1)S(1)} collective-permute-done((bf16[8,16,2880]{2,1,0:T(8,128)(2,1)}, bf16[8,16,2880]{2,1,0:T(8,128)(2,1)S(1)}, u32[]{:S(2)}, u32[]{:S(2)}) %collective-permute-start.74) | collective-permute-done | bytes 737312 | tf_op jit(solution)/shard_map/ppermute | solution.py:136
  895.2 18.6 %collective-permute-done.78 = f32[36872]{0:T(1024)S(1)} collective-permute-done((f32[36872]{0:T(1024)S(1)}, f32[36872]{0:T(1024)S(1)}, u32[]{:S(2)}, u32[]{:S(2)}) %collective-permute-start.78) | collective-permute-done | bytes 147520 | tf_op jit(solution)/shard_map/ppermute | solution.py:137
  941.3 18.8 %collective-permute-done.87 = bf16[2,16,2880]{2,1,0:T(8,128)(2,1)S(1)} collective-permute-done((bf16[2,16,2880]{2,1,0:T(8,128)(2,1)}, bf16[2,16,2880]{2,1,0:T(8,128)(2,1)S(1)}, u32[]{:S(2)}, u32[]{:S(2)}) %collective-permute-start.87) | collective-permute-done | bytes 184352 | tf_op jit(solution)/shard_map/ppermute | solution.py:136
  (603 shorter events, 515.5 us)
Async XLA Ops:
  7.2 130.8 %all-gather.5.cloned.1.call-start = ((), (), s32[]{:S(2)}) async-start(), calls=%async_computation.6 | async-start | bytes 4710400 | tf_op jit(solution)/shard_map/all_gather | solution.py:781
  11.2 39.0 %collective-permute-start = (bf16[8,16,2880]{2,1,0:T(8,128)(2,1)S(1)}, bf16[8,16,2880]{2,1,0:T(8,128)(2,1)}, u32[]{:S(2)}, u32[]{:S(2)}) collective-permute-start(bf16[8,16,2880]{2,1,0:T(8,128)(2,1)S(1)} %bitcast.431), channel_id=1, source_target_pairs={{0,2},{2,4},{4,6},{6,7},{7,5},{5,3},{3,1},{1,0},{8,10},{10,12},{12... | collective-permute-start | bytes 2211848 | tf_op jit(solution)/shard_map/ppermute | solution.py:136
  12.8 37.5 %collective-permute-start.1 = (bf16[8,16,2880]{2,1,0:T(8,128)(2,1)S(1)}, bf16[8,16,2880]{2,1,0:T(8,128)(2,1)S(1)}, u32[]{:S(2)}, u32[]{:S(2)}) collective-permute-start(bf16[8,16,2880]{2,1,0:T(8,128)(2,1)S(1)} %bitcast.432), channel_id=1, source_target_pairs={{2,0},{4,2},{6,4},{7,6},{5,7},{3,5},{1,3},{0,1},{10,8},{12,10},{14... | collective-permute-start | bytes 2211848 | tf_op jit(solution)/shard_map/ppermute | solution.py:136
  50.3 323.4 %all-gather.7.cloned.1.call-start = ((), (), s32[]{:S(2)}) async-start(), calls=%async_computation.7 | async-start | bytes 41472000 | tf_op jit(solution)/shard_map/all_gather | solution.py:810
  81.7 37.3 %collective-permute-start.11 = (bf16[8,16,2880]{2,1,0:T(8,128)(2,1)S(1)}, bf16[8,16,2880]{2,1,0:T(8,128)(2,1)S(1)}, u32[]{:S(2)}, u32[]{:S(2)}) collective-permute-start(bf16[8,16,2880]{2,1,0:T(8,128)(2,1)S(1)} %bitcast.435), channel_id=1, source_target_pairs={{0,1},{1,25},{2,9},{3,17},{4,20},{5,28},{6,4},{7,12},{8,14},{9,22}... | collective-permute-start | bytes 2211848 | tf_op jit(solution)/shard_map/ppermute | solution.py:136
  86.2 32.0 %collective-permute-start.9 = (bf16[8,16,2880]{2,1,0:T(8,128)(2,1)}, bf16[8,16,2880]{2,1,0:T(8,128)(2,1)S(1)}, u32[]{:S(2)}, u32[]{:S(2)}) collective-permute-start(bf16[8,16,2880]{2,1,0:T(8,128)(2,1)} %copy-done.62), channel_id=1, source_target_pairs={{0,2},{2,4},{4,6},{6,7},{7,5},{5,3},{3,1},{1,0},{8,10},{10,12},{12... | collective-permute-start | bytes 2211848 | tf_op jit(solution)/shard_map/ppermute | solution.py:136
  87.2 31.7 %collective-permute-start.10 = (bf16[8,16,2880]{2,1,0:T(8,128)(2,1)}, bf16[8,16,2880]{2,1,0:T(8,128)(2,1)S(1)}, u32[]{:S(2)}, u32[]{:S(2)}) collective-permute-start(bf16[8,16,2880]{2,1,0:T(8,128)(2,1)} %copy-done.61), channel_id=1, source_target_pairs={{2,0},{4,2},{6,4},{7,6},{5,7},{3,5},{1,3},{0,1},{10,8},{12,10},{14... | collective-permute-start | bytes 2211848 | tf_op jit(solution)/shard_map/ppermute | solution.py:136
  127.8 311.2 %all-gather.9.cloned.1.call-start = ((), (), s32[]{:S(2)}) async-start(), calls=%async_computation.11 | async-start | bytes 21196800 | tf_op jit(solution)/shard_map/all_gather | solution.py:812
  127.8 44.6 %collective-permute-start.14 = (bf16[8,16,2880]{2,1,0:T(8,128)(2,1)S(1)}, bf16[8,16,2880]{2,1,0:T(8,128)(2,1)S(1)}, u32[]{:S(2)}, u32[]{:S(2)}) collective-permute-start(bf16[8,16,2880]{2,1,0:T(8,128)(2,1)S(1)} %collective-permute-done.11), channel_id=1, source_target_pairs={{0,16},{8,24},{16,0},{24,8},{1,17},{9,25},{17,1},{25,9},{2,18},{10... | collective-permute-start | bytes 2211848 | tf_op jit(solution)/shard_map/ppermute | solution.py:136
  174.6 516.4 %reduce-scatter.13.cloned.1.call-start = ((), (), s32[]{:S(2)}) async-start(), calls=%async_computation.12 | async-start | bytes 21196800
  460.8 40.6 %all-to-all-start.1 = ((f32[8,1,128]{2,1,0:T(1,128)}), f32[8,1,128]{2,1,0:T(1,128)S(1)}, u32[]{:S(2)}, u32[]{:S(2)}) async-start(f32[8,1,128]{2,1,0:T(1,128)} %bitcast.119), calls=%async_computation.1 | async-start | bytes 8192 | tf_op jit(solution)/shard_map/all_to_all | solution.py:951
  467.4 247.7 %reduce-scatter.7.cloned.1.call-start = ((), (), s32[]{:S(2)}) async-start(), calls=%async_computation.8 | async-start | bytes 14131200 | tf_op jit(solution)/shard_map/reduce_scatter | solution.py:927
  467.4 30.4 %collective-permute-start.43 = (bf16[4,16,2880]{2,1,0:T(8,128)(2,1)}, bf16[4,16,2880]{2,1,0:T(8,128)(2,1)}, u32[]{:S(2)}, u32[]{:S(2)}) collective-permute-start(bf16[4,16,2880]{2,1,0:T(8,128)(2,1)} %bitcast.117), channel_id=1, source_target_pairs={{2,0},{4,2},{6,4},{7,6},{5,7},{3,5},{1,3},{0,1},{10,8},{12,10},{14... | collective-permute-start | bytes 1105928 | tf_op jit(solution)/shard_map/ppermute | solution.py:136
  467.9 31.7 %collective-permute-start.42 = (bf16[4,16,2880]{2,1,0:T(8,128)(2,1)S(1)}, bf16[4,16,2880]{2,1,0:T(8,128)(2,1)}, u32[]{:S(2)}, u32[]{:S(2)}) collective-permute-start(bf16[4,16,2880]{2,1,0:T(8,128)(2,1)S(1)} %bitcast.471), channel_id=1, source_target_pairs={{0,2},{2,4},{4,6},{6,7},{7,5},{5,3},{3,1},{1,0},{8,10},{10,12},{12... | collective-permute-start | bytes 1105928 | tf_op jit(solution)/shard_map/ppermute | solution.py:136
  501.4 25.8 %collective-permute-start.45 = (bf16[8,16,2880]{2,1,0:T(8,128)(2,1)S(1)}, bf16[8,16,2880]{2,1,0:T(8,128)(2,1)}, u32[]{:S(2)}, u32[]{:S(2)}) collective-permute-start(bf16[8,16,2880]{2,1,0:T(8,128)(2,1)S(1)} %bitcast.438), channel_id=1, source_target_pairs={{2,0},{4,2},{6,4},{7,6},{5,7},{3,5},{1,3},{0,1},{10,8},{12,10},{14... | collective-permute-start | bytes 2211848 | tf_op jit(solution)/shard_map/ppermute | solution.py:136
  533.3 278.8 %reduce-scatter.9.cloned.1.call-start = ((), (), s32[]{:S(2)}) async-start(), calls=%async_computation.9 | async-start | bytes 14131200 | tf_op jit(solution)/shard_map/reduce_scatter | solution.py:927
  533.3 29.7 %collective-permute-start.47 = (bf16[8,16,2880]{2,1,0:T(8,128)(2,1)}, bf16[8,16,2880]{2,1,0:T(8,128)(2,1)}, u32[]{:S(2)}, u32[]{:S(2)}) collective-permute-start(bf16[8,16,2880]{2,1,0:T(8,128)(2,1)} %bitcast.128), channel_id=1, source_target_pairs={{2,0},{4,2},{6,4},{7,6},{5,7},{3,5},{1,3},{0,1},{10,8},{12,10},{14... | collective-permute-start | bytes 2211848 | tf_op jit(solution)/shard_map/ppermute | solution.py:136
  533.9 31.6 %collective-permute-start.46 = (bf16[8,16,2880]{2,1,0:T(8,128)(2,1)S(1)}, bf16[8,16,2880]{2,1,0:T(8,128)(2,1)S(1)}, u32[]{:S(2)}, u32[]{:S(2)}) collective-permute-start(bf16[8,16,2880]{2,1,0:T(8,128)(2,1)S(1)} %bitcast.443), channel_id=1, source_target_pairs={{0,2},{2,4},{4,6},{6,7},{7,5},{5,3},{3,1},{1,0},{8,10},{10,12},{12... | collective-permute-start | bytes 2211848 | tf_op jit(solution)/shard_map/ppermute | solution.py:136
  611.4 268.2 %reduce-scatter.11.cloned.1.call-start = ((), (), s32[]{:S(2)}) async-start(), calls=%async_computation.10 | async-start | bytes 14131200 | tf_op jit(solution)/shard_map/reduce_scatter | solution.py:927
  832.3 47.3 %collective-permute-start.75 = (bf16[5,32,2880]{2,1,0:T(8,128)(2,1)}, bf16[5,32,2880]{2,1,0:T(8,128)(2,1)}, u32[]{:S(2)}, u32[]{:S(2)}) collective-permute-start(bf16[5,32,2880]{2,1,0:T(8,128)(2,1)} %fusion.49), channel_id=1, source_target_pairs={{0,16},{8,24},{16,0},{24,8},{1,17},{9,25},{17,1},{25,9},{2,18},{10... | collective-permute-start | bytes 2764808 | tf_op jit(solution)/shard_map/ppermute | solution.py:137
  857.9 26.3 %collective-permute-start.76 = (bf16[8,16,2880]{2,1,0:T(8,128)(2,1)}, bf16[8,16,2880]{2,1,0:T(8,128)(2,1)}, u32[]{:S(2)}, u32[]{:S(2)}) collective-permute-start(bf16[8,16,2880]{2,1,0:T(8,128)(2,1)} %bitcast.190), channel_id=1, source_target_pairs={{0,16},{8,24},{16,0},{24,8},{1,17},{9,25},{17,1},{25,9},{2,18},{10... | collective-permute-start | bytes 2211848 | tf_op jit(solution)/shard_map/ppermute | solution.py:136
  888.8 25.0 %collective-permute-start.79 = (bf16[8,16,2880]{2,1,0:T(8,128)(2,1)S(1)}, bf16[8,16,2880]{2,1,0:T(8,128)(2,1)S(1)}, u32[]{:S(2)}, u32[]{:S(2)}) collective-permute-start(bf16[8,16,2880]{2,1,0:T(8,128)(2,1)S(1)} %bitcast.468), channel_id=1, source_target_pairs={{0,2},{2,4},{4,6},{6,7},{7,5},{5,3},{3,1},{1,0},{8,10},{10,12},{12... | collective-permute-start | bytes 2211848 | tf_op jit(solution)/shard_map/ppermute | solution.py:136
  930.0 30.1 %collective-permute-start.87 = (bf16[2,16,2880]{2,1,0:T(8,128)(2,1)}, bf16[2,16,2880]{2,1,0:T(8,128)(2,1)S(1)}, u32[]{:S(2)}, u32[]{:S(2)}) collective-permute-start(bf16[2,16,2880]{2,1,0:T(8,128)(2,1)} %bitcast.207), channel_id=1, source_target_pairs={{9,0},{25,1},{1,2},{20,3},{12,4},{4,5},{28,6},{14,7},{6,8},{30,9},... | collective-permute-start | bytes 552968 | tf_op jit(solution)/shard_map/ppermute | solution.py:136
  938.6 28.6 %collective-permute-start.88 = (bf16[8,16,2880]{2,1,0:T(8,128)(2,1)S(1)}, bf16[8,16,2880]{2,1,0:T(8,128)(2,1)S(1)}, u32[]{:S(2)}, u32[]{:S(2)}) collective-permute-start(bf16[8,16,2880]{2,1,0:T(8,128)(2,1)S(1)} %bitcast.430), channel_id=1, source_target_pairs={{1,0},{25,1},{9,2},{17,3},{20,4},{28,5},{4,6},{12,7},{14,8},{22,9}... | collective-permute-start | bytes 2211848 | tf_op jit(solution)/shard_map/ppermute | solution.py:136
  (165 other events, 2910.5 us)
Sparse Core Ops, SparseCore 0:
  50.4 39.8 all-gather.4
  91.9 216.8 all-gather.6
  310.4 109.4 all-gather.8
  438.6 130.5 reduce-scatter.12
  571.8 90.6 reduce-scatter.6
  665.1 90.7 reduce-scatter.8
  758.7 103.0 reduce-scatter.10

commit v4 on v3

--- a/solution.py
+++ b/solution.py
@@ -462,7 +462,7 @@
     length = projected.shape[1]
     rows = heads * HD
     half = HD // 2
-    block = min(256, length)
+    block = min(512, length)
     last = rows // (2 * HD)
 
     def piece(place):
@@ -580,7 +580,7 @@
 def attend_back(at, sinks, turned, pairs, attended, upstream, totals, cosine, sine):
     heads, _, length = totals.shape
     rows = heads * HD
-    block = min(256, length)
+    block = min(512, length)
     by_head = pl.BlockSpec((HD, length), lambda h, at: (h, 0))
     moved = pl.BlockSpec((HD, length), lambda h, at: (at[2 * heads + 4 + h], 0))
     table = pl.BlockSpec((HD // 2, length), lambda h, at: (0, 0))

time: 987 us -> 978 us (level)
  Pallas kernels: 108 us -> 93.8 us
    pallas_call x1, Pallas kernels: 24.7 us -> 13.8 us  [attend(): pl.pallas_call(functools.partial(forward_kernel, block=block, scale=HD **...]
  transfers between devices with their start and end apart: 98 -> 98, of which waited for: 42 -> 46; matrix products, arithmetic and copies ran while one was open for 37% -> 37% of each run, Pallas kernels for 11% -> 10%
where the time goes in v4:
time: 978 us; the launch traced here: 966 us
  waiting for transfers between devices  320 us (33%)
  matrix products  234 us (24%)
  starting transfers between devices  129 us (13%)
  local copies, waits for them, and re-layouts  98.7 us (10%)
  Pallas kernels  93.8 us (10%)
  other arithmetic  57.2 us (6%)
  between operations  33.2 us (3%)
    ppermute x78, waiting for transfers between devices, send(): return straight(lax.ppermute(blocks, axis, pairs)).reshape(values.shape)  300 us
    dot_general x45, matrix products, mul(): return lax.dot_general(left, right, dims, preferred_element_type=WIDE)  232 us
    ppermute x78, starting transfers between devices, send(): return straight(lax.ppermute(blocks, axis, pairs)).reshape(values.shape)  107 us
    pallas_call x3, Pallas kernels, weight_term(): pl.pallas_call(term_kernel, grid=(shards, count), in_specs=[pl.BlockSpec(...  54.6 us
    dynamic_update_slice x34, local copies, waits for them, and re-layouts, put(): lax.dynamic_update_slice(full, part, (index * tokens + offset, 0))  42.7 us
    unnamed x187, local copies, waits for them, and re-layouts  23.8 us
  transfers between devices with their start and end apart: 98, of which 46 were waited for; matrix products, arithmetic and copies ran while one was open for 37% of the time, Pallas kernels for 10%

profile of v4, /device:TPU:24, one launch (start us, length us, event | category | flops | bytes accessed | tf_op | source)
XLA Modules:
  0.0 966.0 jit_solution(7909777535240717224)
XLA Ops:
  52.4 17.6 %collective-permute-done.7 = bf16[8,16,2880]{2,1,0:T(8,128)(2,1)S(1)} collective-permute-done((bf16[8,16,2880]{2,1,0:T(8,128)(2,1)}, bf16[8,16,2880]{2,1,0:T(8,128)(2,1)S(1)}, u32[]{:S(2)}, u32[]{:S(2)}) %collective-permute-start.7) | collective-permute-done | bytes 737312 | tf_op jit(solution)/shard_map/ppermute | solution.py:136
  94.4 23.8 %collective-permute-done.9 = bf16[8,16,2880]{2,1,0:T(8,128)(2,1)S(1)} collective-permute-done((bf16[8,16,2880]{2,1,0:T(8,128)(2,1)}, bf16[8,16,2880]{2,1,0:T(8,128)(2,1)S(1)}, u32[]{:S(2)}, u32[]{:S(2)}) %collective-permute-start.9) | collective-permute-done | bytes 737312 | tf_op jit(solution)/shard_map/ppermute | solution.py:136
  145.6 13.8 %attend.1 = (bf16[512,1024]{1,0:T(8,128)(2,1)S(1)}, bf16[128,1024]{1,0:T(8,128)(2,1)S(1)}, bf16[512,1024]{1,0:T(8,128)(2,1)S(1)}, f32[8,1,1024]{2,1,0:T(1,128)S(1)}) custom-call(s32[28]{0:T(128)S(1)} %pad_add_fusion.at_ref, f32[8]{0:T(128)S(1)} %dynamic_slice.147.sink_ref, ...), custom_call_target="tpu_custom_call" | custom-call | bytes 92274688 | tf_op jit(solution)/shard_map/attend/pallas_call | solution.py:471
  212.1 13.2 %collective-permute-done.22 = bf16[8,16,2880]{2,1,0:T(8,128)(2,1)} collective-permute-done((bf16[8,16,2880]{2,1,0:T(8,128)(2,1)}, bf16[8,16,2880]{2,1,0:T(8,128)(2,1)}, u32[]{:S(2)}, u32[]{:S(2)}) %collective-permute-start.22) | collective-permute-done | bytes 737312 | tf_op jit(solution)/shard_map/ppermute | solution.py:136
  233.9 11.6 %collective-permute-done.24 = bf16[8,16,2880]{2,1,0:T(8,128)(2,1)S(1)} collective-permute-done((bf16[8,16,2880]{2,1,0:T(8,128)(2,1)S(1)}, bf16[8,16,2880]{2,1,0:T(8,128)(2,1)S(1)}, u32[]{:S(2)}, u32[]{:S(2)}) %collective-permute-start.24) | collective-permute-done | bytes 737312 | tf_op jit(solution)/shard_map/ppermute | solution.py:136
  252.3 14.1 %collective-permute-done.25 = bf16[8,16,2880]{2,1,0:T(8,128)(2,1)S(1)} collective-permute-done((bf16[8,16,2880]{2,1,0:T(8,128)(2,1)S(1)}, bf16[8,16,2880]{2,1,0:T(8,128)(2,1)S(1)}, u32[]{:S(2)}, u32[]{:S(2)}) %collective-permute-start.25) | collective-permute-done | bytes 737312 | tf_op jit(solution)/shard_map/ppermute | solution.py:136
  272.8 13.9 %collective-permute-done.27 = bf16[8,16,2880]{2,1,0:T(8,128)(2,1)S(1)} collective-permute-done((bf16[8,16,2880]{2,1,0:T(8,128)(2,1)S(1)}, bf16[8,16,2880]{2,1,0:T(8,128)(2,1)S(1)}, u32[]{:S(2)}, u32[]{:S(2)}) %collective-permute-start.27) | collective-permute-done | bytes 737312 | tf_op jit(solution)/shard_map/ppermute | solution.py:136
  291.4 12.7 %collective-permute-done.29 = bf16[8,16,2880]{2,1,0:T(8,128)(2,1)S(1)} collective-permute-done((bf16[8,16,2880]{2,1,0:T(8,128)(2,1)S(1)}, bf16[8,16,2880]{2,1,0:T(8,128)(2,1)S(1)}, u32[]{:S(2)}, u32[]{:S(2)}) %collective-permute-start.29) | collective-permute-done | bytes 737312 | tf_op jit(solution)/shard_map/ppermute | solution.py:136
  310.4 10.8 %collective-permute-done.31 = bf16[8,16,2880]{2,1,0:T(8,128)(2,1)S(1)} collective-permute-done((bf16[8,16,2880]{2,1,0:T(8,128)(2,1)S(1)}, bf16[8,16,2880]{2,1,0:T(8,128)(2,1)S(1)}, u32[]{:S(2)}, u32[]{:S(2)}) %collective-permute-start.31) | collective-permute-done | bytes 737312 | tf_op jit(solution)/shard_map/ppermute | solution.py:136
  364.9 27.5 %convolution_add_fusion = f32[576,5760]{1,0:T(8,128)S(1)} fusion(bf16[576,2880]{0,1:T(8,128)(2,1)} %convolution_convert_fusion.2, bf16[2880,5760]{1,0:T(8,128)(2,1)} %all-gather.7.cloned.1.call-done, f32[5760]{0:T(1024)S(1)} %reshape.821), kind=kOutput, calls=%fused_computation.8 | convolution fusion | flops 19113615360 | bytes 49789440 | tf_op jit(solution)/shard_map/dot_general | solution.py:31
  412.3 16.7 %convolution_convert_fusion = bf16[2880,2880]{1,0:T(8,128)(2,1)} fusion(bf16[576,2880]{1,0:T(8,128)(2,1)S(1)} %multiply_convert_fusion.1, bf16[576,2880]{1,0:T(8,128)(2,1)S(1)} %get-tuple-element.190), kind=kOutput, calls=%fused_computation.2 | convolution fusion | flops 9563443200 | bytes 23224320 | tf_op jit(solution)/shard_map/dot_general | solution.py:31
  429.6 17.7 %fusion.5 = (f32[576]{0:T(1024)S(1)}, bf16[576,2880]{1,0:T(8,128)(2,1)S(1)}) fusion(f32[576,2880]{1,0:T(8,128)} %get-tuple-element.381, f32[576]{0:T(1024)S(1)} %select_reduce_fusion.1, f32[2880]{0:T(1024)S(1)} %reshape.822, bf16[576,2880]{1,0:T(8,128)(2,1)} %copy-done.51, bf16[1,2880,2880]{2,1,0:T(8,128)(2,1)} %all-gather.9.cloned.1.call-done), kind=kOutput, calls=%fused_computation.13 | convolution fusion | flops 9566759936 | bytes 29875968 | tf_op jit(solution)/shard_map/dot_general | solution.py:31
  461.7 22.5 %select_convert_fusion.1 = (bf16[576,2880]{1,0:T(8,128)(2,1)S(1)}, bf16[576,2880]{1,0:T(8,128)(2,1)}) fusion(f32[576,5760]{1,0:T(8,128)} %copy-done.42, bf16[576,2880]{1,0:T(8,128)(2,1)} %copy-done.89, bf16[1,2880,2880]{2,1,0:T(8,128)(2,1)} %all-gather.9.cloned.1.call-done), kind=kOutput, calls=%fused_computation.17 | convolution fusion | flops 9591644160 | bytes 39813120 | tf_op jit(solution)/shard_map/dot_general | solution.py:31
  501.9 18.4 %weight_term.3 = bf16[2944,1920]{1,0:T(8,128)(2,1)} custom-call(bf16[2880,576]{1,0:T(8,128)(2,1)} %bitcast.400, bf16[576,5760]{1,0:T(8,128)(2,1)} %pad_maximum_fusion.right_ref, f32[16,5760]{1,0:T(8,128)} %pad.67.extra_ref), custom_call_target="tpu_custom_call" | custom-call | tf_op jit(solution)/shard_map/weight_term/pallas_call | solution.py:649
  528.6 27.3 %convolution_convert_fusion.3 = bf16[576,2880]{1,0:T(8,128)(2,1)S(1)} fusion(bf16[576,5760]{1,0:T(8,128)(2,1)} %pad_maximum_fusion.right_ref, bf16[2880,5760]{1,0:T(8,128)(2,1)} %all-gather.7.cloned.1.call-done), kind=kOutput, calls=%fused_computation.29 | convolution fusion | flops 19111956480 | bytes 43130880 | tf_op jit(solution)/shard_map/dot_general | solution.py:31
  563.1 12.0 %collective-permute-done.48 = bf16[8,16,2880]{2,1,0:T(8,128)(2,1)S(1)} collective-permute-done((bf16[8,16,2880]{2,1,0:T(8,128)(2,1)S(1)}, bf16[8,16,2880]{2,1,0:T(8,128)(2,1)S(1)}, u32[]{:S(2)}, u32[]{:S(2)}) %collective-permute-start.48) | collective-permute-done | bytes 737312 | tf_op jit(solution)/shard_map/ppermute | solution.py:136
  579.9 18.3 %weight_term.4 = bf16[2944,1920]{1,0:T(8,128)(2,1)} custom-call(bf16[2880,576]{1,0:T(8,128)(2,1)} %bitcast.401, bf16[576,5760]{1,0:T(8,128)(2,1)} %pad_maximum_fusion.right_ref, f32[16,5760]{1,0:T(8,128)} %pad.67.extra_ref), custom_call_target="tpu_custom_call" | custom-call | tf_op jit(solution)/shard_map/weight_term/pallas_call | solution.py:649
  606.4 16.4 %collective-permute-done.53 = bf16[8,16,2880]{2,1,0:T(8,128)(2,1)S(1)} collective-permute-done((bf16[8,16,2880]{2,1,0:T(8,128)(2,1)}, bf16[8,16,2880]{2,1,0:T(8,128)(2,1)S(1)}, u32[]{:S(2)}, u32[]{:S(2)}) %collective-permute-start.53) | collective-permute-done | bytes 737312 | tf_op jit(solution)/shard_map/ppermute | solution.py:136
  630.3 17.9 %weight_term.5 = bf16[2944,1920]{1,0:T(8,128)(2,1)} custom-call(bf16[2880,576]{1,0:T(8,128)(2,1)} %bitcast.402, bf16[576,5760]{1,0:T(8,128)(2,1)} %pad_maximum_fusion.right_ref, f32[16,5760]{1,0:T(8,128)} %pad.67.extra_ref), custom_call_target="tpu_custom_call" | custom-call | tf_op jit(solution)/shard_map/weight_term/pallas_call | solution.py:649
  659.2 16.0 %collective-permute-done.56 = bf16[8,16,2880]{2,1,0:T(8,128)(2,1)S(1)} collective-permute-done((bf16[8,16,2880]{2,1,0:T(8,128)(2,1)}, bf16[8,16,2880]{2,1,0:T(8,128)(2,1)S(1)}, u32[]{:S(2)}, u32[]{:S(2)}) %collective-permute-start.56) | collective-permute-done | bytes 737312 | tf_op jit(solution)/shard_map/ppermute | solution.py:136
  745.8 18.7 %attend_back.1 = (bf16[512,1024]{1,0:T(8,128)(2,1)S(1)}, bf16[128,1024]{1,0:T(8,128)(2,1)S(1)}, f32[8,1,128]{2,1,0:T(1,128)S(1)}) custom-call(s32[28]{0:T(128)S(1)} %copy-done.21, f32[8]{0:T(128)S(1)} %copy-done.19, bf16[512,1024]{1,0:T(8,128)(2,1)S(1)} %copy-done.17, bf16[128,1024]{1,0:T(8,128)(2,1)S(1)} %get-tuple-element.213.pairs_ref, ...), custom_call_target="tpu_custom_call" | custom-call | tf_op jit(solution)/shard_map/attend_back/pallas_call | solution.py:588
  846.4 14.4 %collective-permute-done.74 = bf16[8,16,2880]{2,1,0:T(8,128)(2,1)S(1)} collective-permute-done((bf16[8,16,2880]{2,1,0:T(8,128)(2,1)}, bf16[8,16,2880]{2,1,0:T(8,128)(2,1)S(1)}, u32[]{:S(2)}, u32[]{:S(2)}) %collective-permute-start.74) | collective-permute-done | bytes 737312 | tf_op jit(solution)/shard_map/ppermute | solution.py:136
  884.9 18.6 %collective-permute-done.78 = f32[36872]{0:T(1024)S(1)} collective-permute-done((f32[36872]{0:T(1024)S(1)}, f32[36872]{0:T(1024)S(1)}, u32[]{:S(2)}, u32[]{:S(2)}) %collective-permute-start.78) | collective-permute-done | bytes 147520 | tf_op jit(solution)/shard_map/ppermute | solution.py:137
  931.0 18.7 %collective-permute-done.87 = bf16[2,16,2880]{2,1,0:T(8,128)(2,1)S(1)} collective-permute-done((bf16[2,16,2880]{2,1,0:T(8,128)(2,1)}, bf16[2,16,2880]{2,1,0:T(8,128)(2,1)S(1)}, u32[]{:S(2)}, u32[]{:S(2)}) %collective-permute-start.87) | collective-permute-done | bytes 184352 | tf_op jit(solution)/shard_map/ppermute | solution.py:136
  (603 shorter events, 520.1 us)
Async XLA Ops:
  7.2 130.8 %all-gather.5.cloned.1.call-start = ((), (), s32[]{:S(2)}) async-start(), calls=%async_computation.6 | async-start | bytes 4710400 | tf_op jit(solution)/shard_map/all_gather | solution.py:781
  11.2 39.0 %collective-permute-start = (bf16[8,16,2880]{2,1,0:T(8,128)(2,1)S(1)}, bf16[8,16,2880]{2,1,0:T(8,128)(2,1)}, u32[]{:S(2)}, u32[]{:S(2)}) collective-permute-start(bf16[8,16,2880]{2,1,0:T(8,128)(2,1)S(1)} %bitcast.431), channel_id=1, source_target_pairs={{0,2},{2,4},{4,6},{6,7},{7,5},{5,3},{3,1},{1,0},{8,10},{10,12},{12... | collective-permute-start | bytes 2211848 | tf_op jit(solution)/shard_map/ppermute | solution.py:136
  12.8 37.5 %collective-permute-start.1 = (bf16[8,16,2880]{2,1,0:T(8,128)(2,1)S(1)}, bf16[8,16,2880]{2,1,0:T(8,128)(2,1)S(1)}, u32[]{:S(2)}, u32[]{:S(2)}) collective-permute-start(bf16[8,16,2880]{2,1,0:T(8,128)(2,1)S(1)} %bitcast.432), channel_id=1, source_target_pairs={{2,0},{4,2},{6,4},{7,6},{5,7},{3,5},{1,3},{0,1},{10,8},{12,10},{14... | collective-permute-start | bytes 2211848 | tf_op jit(solution)/shard_map/ppermute | solution.py:136
  50.3 314.6 %all-gather.7.cloned.1.call-start = ((), (), s32[]{:S(2)}) async-start(), calls=%async_computation.7 | async-start | bytes 41472000 | tf_op jit(solution)/shard_map/all_gather | solution.py:810
  81.7 37.3 %collective-permute-start.11 = (bf16[8,16,2880]{2,1,0:T(8,128)(2,1)S(1)}, bf16[8,16,2880]{2,1,0:T(8,128)(2,1)S(1)}, u32[]{:S(2)}, u32[]{:S(2)}) collective-permute-start(bf16[8,16,2880]{2,1,0:T(8,128)(2,1)S(1)} %bitcast.435), channel_id=1, source_target_pairs={{0,1},{1,25},{2,9},{3,17},{4,20},{5,28},{6,4},{7,12},{8,14},{9,22}... | collective-permute-start | bytes 2211848 | tf_op jit(solution)/shard_map/ppermute | solution.py:136
  86.2 32.0 %collective-permute-start.9 = (bf16[8,16,2880]{2,1,0:T(8,128)(2,1)}, bf16[8,16,2880]{2,1,0:T(8,128)(2,1)S(1)}, u32[]{:S(2)}, u32[]{:S(2)}) collective-permute-start(bf16[8,16,2880]{2,1,0:T(8,128)(2,1)} %copy-done.62), channel_id=1, source_target_pairs={{0,2},{2,4},{4,6},{6,7},{7,5},{5,3},{3,1},{1,0},{8,10},{10,12},{12... | collective-permute-start | bytes 2211848 | tf_op jit(solution)/shard_map/ppermute | solution.py:136
  87.2 31.7 %collective-permute-start.10 = (bf16[8,16,2880]{2,1,0:T(8,128)(2,1)}, bf16[8,16,2880]{2,1,0:T(8,128)(2,1)S(1)}, u32[]{:S(2)}, u32[]{:S(2)}) collective-permute-start(bf16[8,16,2880]{2,1,0:T(8,128)(2,1)} %copy-done.61), channel_id=1, source_target_pairs={{2,0},{4,2},{6,4},{7,6},{5,7},{3,5},{1,3},{0,1},{10,8},{12,10},{14... | collective-permute-start | bytes 2211848 | tf_op jit(solution)/shard_map/ppermute | solution.py:136
  127.8 301.8 %all-gather.9.cloned.1.call-start = ((), (), s32[]{:S(2)}) async-start(), calls=%async_computation.11 | async-start | bytes 21196800 | tf_op jit(solution)/shard_map/all_gather | solution.py:812
  127.8 36.8 %collective-permute-start.14 = (bf16[8,16,2880]{2,1,0:T(8,128)(2,1)S(1)}, bf16[8,16,2880]{2,1,0:T(8,128)(2,1)S(1)}, u32[]{:S(2)}, u32[]{:S(2)}) collective-permute-start(bf16[8,16,2880]{2,1,0:T(8,128)(2,1)S(1)} %collective-permute-done.11), channel_id=1, source_target_pairs={{0,16},{8,24},{16,0},{24,8},{1,17},{9,25},{17,1},{25,9},{2,18},{10... | collective-permute-start | bytes 2211848 | tf_op jit(solution)/shard_map/ppermute | solution.py:136
  166.9 516.8 %reduce-scatter.13.cloned.1.call-start = ((), (), s32[]{:S(2)}) async-start(), calls=%async_computation.12 | async-start | bytes 21196800
  451.9 42.6 %all-to-all-start.1 = ((f32[8,1,128]{2,1,0:T(1,128)}), f32[8,1,128]{2,1,0:T(1,128)S(1)}, u32[]{:S(2)}, u32[]{:S(2)}) async-start(f32[8,1,128]{2,1,0:T(1,128)} %bitcast.119), calls=%async_computation.1 | async-start | bytes 8192 | tf_op jit(solution)/shard_map/all_to_all | solution.py:951
  459.7 247.6 %reduce-scatter.7.cloned.1.call-start = ((), (), s32[]{:S(2)}) async-start(), calls=%async_computation.8 | async-start | bytes 14131200 | tf_op jit(solution)/shard_map/reduce_scatter | solution.py:927
  459.7 31.1 %collective-permute-start.43 = (bf16[4,16,2880]{2,1,0:T(8,128)(2,1)}, bf16[4,16,2880]{2,1,0:T(8,128)(2,1)}, u32[]{:S(2)}, u32[]{:S(2)}) collective-permute-start(bf16[4,16,2880]{2,1,0:T(8,128)(2,1)} %bitcast.117), channel_id=1, source_target_pairs={{2,0},{4,2},{6,4},{7,6},{5,7},{3,5},{1,3},{0,1},{10,8},{12,10},{14... | collective-permute-start | bytes 1105928 | tf_op jit(solution)/shard_map/ppermute | solution.py:136
  460.3 32.4 %collective-permute-start.42 = (bf16[4,16,2880]{2,1,0:T(8,128)(2,1)S(1)}, bf16[4,16,2880]{2,1,0:T(8,128)(2,1)}, u32[]{:S(2)}, u32[]{:S(2)}) collective-permute-start(bf16[4,16,2880]{2,1,0:T(8,128)(2,1)S(1)} %bitcast.471), channel_id=1, source_target_pairs={{0,2},{2,4},{4,6},{6,7},{7,5},{5,3},{3,1},{1,0},{8,10},{10,12},{12... | collective-permute-start | bytes 1105928 | tf_op jit(solution)/shard_map/ppermute | solution.py:136
  494.5 25.7 %collective-permute-start.45 = (bf16[8,16,2880]{2,1,0:T(8,128)(2,1)S(1)}, bf16[8,16,2880]{2,1,0:T(8,128)(2,1)}, u32[]{:S(2)}, u32[]{:S(2)}) collective-permute-start(bf16[8,16,2880]{2,1,0:T(8,128)(2,1)S(1)} %bitcast.438), channel_id=1, source_target_pairs={{2,0},{4,2},{6,4},{7,6},{5,7},{3,5},{1,3},{0,1},{10,8},{12,10},{14... | collective-permute-start | bytes 2211848 | tf_op jit(solution)/shard_map/ppermute | solution.py:136
  526.5 274.2 %reduce-scatter.9.cloned.1.call-start = ((), (), s32[]{:S(2)}) async-start(), calls=%async_computation.9 | async-start | bytes 14131200 | tf_op jit(solution)/shard_map/reduce_scatter | solution.py:927
  526.5 29.4 %collective-permute-start.47 = (bf16[8,16,2880]{2,1,0:T(8,128)(2,1)}, bf16[8,16,2880]{2,1,0:T(8,128)(2,1)}, u32[]{:S(2)}, u32[]{:S(2)}) collective-permute-start(bf16[8,16,2880]{2,1,0:T(8,128)(2,1)} %bitcast.128), channel_id=1, source_target_pairs={{2,0},{4,2},{6,4},{7,6},{5,7},{3,5},{1,3},{0,1},{10,8},{12,10},{14... | collective-permute-start | bytes 2211848 | tf_op jit(solution)/shard_map/ppermute | solution.py:136
  527.1 31.4 %collective-permute-start.46 = (bf16[8,16,2880]{2,1,0:T(8,128)(2,1)S(1)}, bf16[8,16,2880]{2,1,0:T(8,128)(2,1)S(1)}, u32[]{:S(2)}, u32[]{:S(2)}) collective-permute-start(bf16[8,16,2880]{2,1,0:T(8,128)(2,1)S(1)} %bitcast.443), channel_id=1, source_target_pairs={{0,2},{2,4},{4,6},{6,7},{7,5},{5,3},{3,1},{1,0},{8,10},{10,12},{12... | collective-permute-start | bytes 2211848 | tf_op jit(solution)/shard_map/ppermute | solution.py:136
  604.1 263.2 %reduce-scatter.11.cloned.1.call-start = ((), (), s32[]{:S(2)}) async-start(), calls=%async_computation.10 | async-start | bytes 14131200 | tf_op jit(solution)/shard_map/reduce_scatter | solution.py:927
  820.8 46.5 %collective-permute-start.75 = (bf16[5,32,2880]{2,1,0:T(8,128)(2,1)}, bf16[5,32,2880]{2,1,0:T(8,128)(2,1)}, u32[]{:S(2)}, u32[]{:S(2)}) collective-permute-start(bf16[5,32,2880]{2,1,0:T(8,128)(2,1)} %fusion.49), channel_id=1, source_target_pairs={{0,16},{8,24},{16,0},{24,8},{1,17},{9,25},{17,1},{25,9},{2,18},{10... | collective-permute-start | bytes 2764808 | tf_op jit(solution)/shard_map/ppermute | solution.py:137
  845.6 28.4 %collective-permute-start.76 = (bf16[8,16,2880]{2,1,0:T(8,128)(2,1)}, bf16[8,16,2880]{2,1,0:T(8,128)(2,1)}, u32[]{:S(2)}, u32[]{:S(2)}) collective-permute-start(bf16[8,16,2880]{2,1,0:T(8,128)(2,1)} %bitcast.190), channel_id=1, source_target_pairs={{0,16},{8,24},{16,0},{24,8},{1,17},{9,25},{17,1},{25,9},{2,18},{10... | collective-permute-start | bytes 2211848 | tf_op jit(solution)/shard_map/ppermute | solution.py:136
  878.5 25.0 %collective-permute-start.79 = (bf16[8,16,2880]{2,1,0:T(8,128)(2,1)S(1)}, bf16[8,16,2880]{2,1,0:T(8,128)(2,1)S(1)}, u32[]{:S(2)}, u32[]{:S(2)}) collective-permute-start(bf16[8,16,2880]{2,1,0:T(8,128)(2,1)S(1)} %bitcast.468), channel_id=1, source_target_pairs={{0,2},{2,4},{4,6},{6,7},{7,5},{5,3},{3,1},{1,0},{8,10},{10,12},{12... | collective-permute-start | bytes 2211848 | tf_op jit(solution)/shard_map/ppermute | solution.py:136
  919.7 30.1 %collective-permute-start.87 = (bf16[2,16,2880]{2,1,0:T(8,128)(2,1)}, bf16[2,16,2880]{2,1,0:T(8,128)(2,1)S(1)}, u32[]{:S(2)}, u32[]{:S(2)}) collective-permute-start(bf16[2,16,2880]{2,1,0:T(8,128)(2,1)} %bitcast.207), channel_id=1, source_target_pairs={{9,0},{25,1},{1,2},{20,3},{12,4},{4,5},{28,6},{14,7},{6,8},{30,9},... | collective-permute-start | bytes 552968 | tf_op jit(solution)/shard_map/ppermute | solution.py:136
  928.2 28.7 %collective-permute-start.88 = (bf16[8,16,2880]{2,1,0:T(8,128)(2,1)S(1)}, bf16[8,16,2880]{2,1,0:T(8,128)(2,1)S(1)}, u32[]{:S(2)}, u32[]{:S(2)}) collective-permute-start(bf16[8,16,2880]{2,1,0:T(8,128)(2,1)S(1)} %bitcast.430), channel_id=1, source_target_pairs={{1,0},{25,1},{9,2},{17,3},{20,4},{28,5},{4,6},{12,7},{14,8},{22,9}... | collective-permute-start | bytes 2211848 | tf_op jit(solution)/shard_map/ppermute | solution.py:136
  (165 other events, 2891.3 us)
Sparse Core Ops, SparseCore 0:
  50.4 39.8 all-gather.4
  91.9 216.8 all-gather.6
  310.4 109.4 all-gather.8
  429.1 129.6 reduce-scatter.12
  561.5 90.6 reduce-scatter.6
  654.9 90.6 reduce-scatter.8
  748.4 104.4 reduce-scatter.10
